TPU v7x, 128 devices: a whole 4x4x4 slice. The times are simulated.
128 devices in a mesh: section: 4 (over z_hi, core), dp: 32 (over z_lo, y, x).
Axes of the slice: x: 4, y: 4, z: 4 (z_hi: 2, z_lo: 2; z = z_hi * 2 + z_lo), core: 2. Of those that a mesh axis runs over, the one named last changes fastest.
Arguments:
- node_states: bfloat16 [4096, 128], P('dp'), may hold values from -6 to 6
- edge_features: bfloat16 [16, 32768], P(None, 'dp'), may hold values from -6 to 6
- edge_source: int32 [32768], P('dp'), may hold values from 0 to 31, as said below
- edge_target: int32 [32768], P('dp'), may hold values from 0 to 31, as said below
- edge_live: int32 [32768], P('dp'), may hold values 0 or 1
- w_edge_in: bfloat16 [16, 128], replicated, may hold values from -1.5 to 1.5
- b_edge_in: float32 [128], replicated, may hold values from -3 to 3
- w_edge_out: bfloat16 [128, 16384], replicated, may hold values from -0.0625 to 0.0625
- b_edge_out: float32 [16384], replicated, may hold values from -0.3 to 0.3
- w_input: bfloat16 [128, 384], replicated, may hold values from -0.5 to 0.5
- w_hidden: bfloat16 [128, 384], replicated, may hold values from -0.5 to 0.5
- b_input: float32 [384], replicated, may hold values from -3 to 3
- b_hidden: float32 [384], replicated, may hold values from -3 to 3
- cotangent: float32 [4096, 128], P('dp'), may hold values from -6 to 6
Outputs:
- final_states: float32 [4096, 128], P(('dp', 'section'))
- grad_states: float32 [4096, 128], P(('dp', 'section'))
- grad_w_edge_in: float32 [16, 128], replicated
- grad_b_edge_in: float32 [128], replicated
- grad_w_edge_out: float32 [128, 16384], replicated
- grad_b_edge_out: float32 [16384], replicated
- grad_w_input: float32 [128, 384], replicated
- grad_w_hidden: float32 [128, 384], replicated
- grad_b_input: float32 [384], replicated
- grad_b_hidden: float32 [384], replicated
Inputs may be any that keep to these rules, and one draw needn't show every extreme that they name: `edge_source`: an edge's source and target are two different atom slots of the same molecule, counted from the start of the edge's node block; the edge slots of a molecule are 256 consecutive slots, molecule m of a block owning atom slots m * 32 to m * 32 + 31. `edge_target`: as for edge_source.
All inputs are finite; a program needn't handle non-finite values. No bound on the sum of `edge_live` on one device may be relied on, other than what follows from the above.
Results may differ from a plain program's by a relative error of at most 0.028.
The roundings to bfloat16 on the way count: a program that leaves them out, or rounds other values in their place, can miss the bound.
Values may be sent and summed in bfloat16 or wider, within the bound.
No kernel may reach another device: no remote copies, remote signals or barrier semaphores. Data moves between devices by JAX's collectives and lax.ppermute only.
A program may use at most 128 MiB of HBM per device.

v0:
```python
import functools

import jax
import jax.numpy as jnp
from jax import lax
from jax.experimental import pallas as pl
from jax.experimental.pallas import tpu as pltpu
from jax.sharding import Mesh
from jax.sharding import PartitionSpec as P

H = 128
ATOMS = 32
EPM = 256
MB = 4
NODES = MB * ATOMS
PAIRS = ATOMS * ATOMS
OWN = H // MB
GAP = 129
ROWS = 144
SMALL = 8
GROUP = 32
BF = jnp.bfloat16
F32 = jnp.float32


def nn(left, right):
    return jnp.dot(left, right, preferred_element_type=F32)


def nt(left, right):
    return lax.dot_general(left, right, (((1,), (1,)), ((), ())), preferred_element_type=F32)


def tn(left, right):
    return lax.dot_general(left, right, (((0,), (0,)), ((), ())), preferred_element_type=F32)


def halves(value):
    high = value.astype(BF)
    return high, (value - high.astype(F32)).astype(BF)


def fine(dot, left, right):
    lh, ll = halves(left)
    rh, rl = halves(right)
    return dot(lh, rh) + (dot(lh, rl) + dot(ll, rh))


def fine_left(dot, left, right):
    lh, ll = halves(left)
    return dot(lh, right) + dot(ll, right)


def fine_right(dot, left, right):
    rh, rl = halves(right)
    return dot(left, rh) + dot(left, rl)


def sigmoid(value):
    return 0.5 * jnp.tanh(0.5 * value) + 0.5


def gate_forward(message, states, w_input, w_hidden, b_input, b_hidden):
    from_msg = nn(message, w_input) + b_input
    from_state = nn(states, w_hidden) + b_hidden
    reset = sigmoid(from_msg[:, :H] + from_state[:, :H])
    update = sigmoid(from_msg[:, H : 2 * H] + from_state[:, H : 2 * H])
    state_cand = from_state[:, 2 * H :]
    candidate = jnp.tanh(from_msg[:, 2 * H :] + reset * state_cand)
    renewed = (1.0 - update) * candidate + update * states.astype(F32)
    return reset, update, candidate, state_cand, renewed


def gate_backward(grad, states, parts, w_input, w_hidden):
    reset, update, candidate, state_cand = parts
    act = grad * (1.0 - update) * (1.0 - candidate * candidate)
    d_reset = act * state_cand * reset * (1.0 - reset)
    d_update = grad * (states.astype(F32) - candidate) * update * (1.0 - update)
    d_in = jnp.concatenate([d_reset, d_update, act], axis=1).astype(BF)
    d_hid = jnp.concatenate([d_reset, d_update, act * reset], axis=1).astype(BF)
    g_msg = nt(d_in, w_input).astype(BF)
    grad_states = grad * update + nt(d_hid, w_hidden)
    return d_in, d_hid, g_msg, grad_states


def edge_front(features, w_edge_in, b_edge_in):
    return tn(features, w_edge_in) + b_edge_in


def local_kernel(
    sect_ref,
    states_ref,
    feat_ref,
    ends_ref,
    w_ein_ref,
    b_ein_ref,
    w_hbm,
    b_mat_ref,
    w_in_ref,
    w_hid_ref,
    b_in_ref,
    b_hid_ref,
    cot_ref,
    send_ref,
    final_ref,
    base_ref,
    grad_t_ref,
    pairs_out_ref,
    w_ref,
    u_one,
    u_two,
    d_all,
    d_own,
    pair_h,
    rows_scr,
    small_scr,
    q_scr,
    sems,
):
    sect = sect_ref[0]
    chunk = 2048

    def w_copy(at):
        cols = pl.ds(at * chunk, chunk)
        return pltpu.make_async_copy(w_hbm.at[:, cols], w_ref.at[:, cols], sems.at[at])

    for at in range(8):
        w_copy(at).start()

    states0 = states_ref[...]
    w_ein = w_ein_ref[...]
    b_ein = b_ein_ref[...]
    b_mat = b_mat_ref[...]
    source = ends_ref[0]
    target = ends_ref[1]
    live = ends_ref[2]
    pair = jnp.where(live > 0, source * ATOMS + target, -1)

    slot = lax.broadcasted_iota(jnp.int32, (PAIRS, H), 0)
    for mol in range(MB):
        pre = edge_front(feat_ref[:, mol * EPM : (mol + 1) * EPM], w_ein, b_ein)
        hidden = (pre * sigmoid(pre)).astype(BF)
        hot = jnp.concatenate(
            [
                jnp.where(slot == pair[2 * mol + part : 2 * mol + part + 1, :], 1.0, 0.0).astype(BF)
                for part in range(2)
            ],
            axis=1,
        )
        pair_h[mol * PAIRS : (mol + 1) * PAIRS, :] = nn(hot, hidden).astype(BF)

    node = lax.broadcasted_iota(jnp.int32, (NODES, H), 0)
    hot_t, hot_s = [], []
    for row in range(8):
        shift = (row // 2) * ATOMS
        keep = live[row : row + 1, :] > 0
        t_at = jnp.where(keep, target[row : row + 1, :] + shift, -1)
        s_at = source[row : row + 1, :] + shift
        hot_t.append(jnp.where(node == t_at, 1.0, 0.0).astype(BF))
        hot_s.append(jnp.where(node == s_at, 1.0, 0.0).astype(BF))
    hot_t = jnp.concatenate(hot_t, axis=1)
    hot_s = jnp.concatenate(hot_s, axis=1)
    adj = nt(hot_t, hot_s).astype(BF)
    adj_t = nt(hot_s, hot_t).astype(BF)

    def spread(states, u_ref, wait):
        def step(at):
            base = pl.multiple_of(at * 4 * H, 4 * H)
            four = [w_ref[:, pl.ds(base + q * H, H)] for q in range(4)]
            out = nt(states, jnp.concatenate(four, axis=0))
            for q in range(4):
                u_ref[pl.ds(at * 4 + q, NODES, stride=GAP), :] = out[:, q * H : (q + 1) * H]

        if wait:
            for at in range(8):
                w_copy(at).wait()
                for inner in range(4):
                    step(at * 4 + inner)
        else:

            def body(at, carry):
                step(at)
                return carry

            lax.fori_loop(0, 32, body, 0, unroll=8)

    def u_rows(u_ref, at):
        return u_ref[pl.ds(at * GAP, H), :].astype(BF)

    def gather(states, u_ref):
        side = fine_right(nt, states, b_mat)
        extra = fine_right(nn, adj, side)
        parts = []
        for mol in range(MB):

            def body(at, total, mol=mol):
                first = mol * ATOMS + at * 4
                left = jnp.concatenate(
                    [
                        pair_h[pl.ds(pl.multiple_of((first + q) * ATOMS, ATOMS), ATOMS), :]
                        for q in range(4)
                    ],
                    axis=1,
                )
                right = jnp.concatenate([u_rows(u_ref, first + q) for q in range(4)], axis=1)
                return total + nt(left, right)

            parts.append(lax.fori_loop(0, 8, body, jnp.zeros((ATOMS, H), F32), unroll=True))
        return (jnp.concatenate(parts, axis=0) + extra).astype(BF)

    w_in = w_in_ref[...]
    w_hid = w_hid_ref[...]
    b_in = b_in_ref[...]
    b_hid = b_hid_ref[...]

    spread(states0, u_one, True)
    msg_one = gather(states0, u_one)
    *parts_one, renewed = gate_forward(msg_one, states0, w_in, w_hid, b_in, b_hid)
    states1 = renewed.astype(BF)
    spread(states1, u_two, False)
    msg_two = gather(states1, u_two)
    *parts_two, final = gate_forward(msg_two, states1, w_in, w_hid, b_in, b_hid)
    own_rows = pl.ds(pl.multiple_of(sect * ATOMS, ATOMS), ATOMS)
    rows_scr[...] = final
    final_ref[...] = rows_scr[own_rows, :]

    d_in2, d_hid2, g_two, back_one = gate_backward(cot_ref[...], states1, parts_two, w_in, w_hid)
    g_two_t = g_two.astype(F32).T.astype(BF)

    for mol in range(MB):
        left = g_two_t[:, mol * ATOMS : (mol + 1) * ATOMS]

        def body(at, carry, mol=mol, left=left):
            first = mol * ATOMS + at * 4
            right = jnp.concatenate(
                [
                    pair_h[pl.ds(pl.multiple_of((first + q) * ATOMS, ATOMS), ATOMS), :]
                    for q in range(4)
                ],
                axis=1,
            )
            out = nn(left, right)
            for q in range(4):
                d_all[pl.ds(first + q, H, stride=GAP), :] = out[:, q * H : (q + 1) * H]
            return carry

        lax.fori_loop(0, 8, body, 0, unroll=True)

    def back_body(at, total):
        base = pl.multiple_of(at * 4 * H, 4 * H)
        left = jnp.concatenate(
            [d_all[pl.ds((at * 4 + q) * GAP, NODES), :].astype(BF) for q in range(4)], axis=1
        )
        right = jnp.concatenate([w_ref[:, pl.ds(base + q * H, H)] for q in range(4)], axis=0)
        return total + nn(left, right)

    back_msg = lax.fori_loop(0, 32, back_body, jnp.zeros((NODES, H), F32), unroll=8)
    share = nn(adj_t, g_two)
    grad_one = back_one + back_msg + fine(nn, share, b_mat)

    d_in1, d_hid1, g_one, back_zero = gate_backward(grad_one, states0, parts_one, w_in, w_hid)
    rows_scr[...] = g_one.astype(F32).T
    g_one_t = rows_scr[...].astype(BF)
    g_one_own = rows_scr[own_rows, :].astype(BF)

    for mol in range(MB):
        left = g_one_own[:, mol * ATOMS : (mol + 1) * ATOMS]

        def body(at, carry, mol=mol, left=left):
            first = mol * ATOMS + at * 4
            right = jnp.concatenate(
                [
                    pair_h[pl.ds(pl.multiple_of((first + q) * ATOMS, ATOMS), ATOMS), :]
                    for q in range(4)
                ],
                axis=1,
            )
            out = nn(left, right)
            for q in range(4):
                d_own[pl.ds(first + q, OWN, stride=GAP), :] = out[:, q * H : (q + 1) * H]
            return carry

        lax.fori_loop(0, 8, body, 0, unroll=True)

    both_t = jnp.concatenate([states0.astype(F32).T, states1.astype(F32).T], axis=1).astype(BF)

    def own_body(at, carry):
        right = jnp.concatenate(
            [
                d_own[pl.ds(at * GAP, NODES), :].astype(BF),
                d_all[pl.ds((sect * OWN + at) * GAP, NODES), :].astype(BF),
            ],
            axis=0,
        )
        send_ref[at, 0:H, :] = nn(both_t, right).astype(BF)
        return carry

    lax.fori_loop(0, OWN, own_body, 0, unroll=8)

    rows_scr[...] = g_one.astype(F32)
    g1 = rows_scr[own_rows, :].astype(BF)
    rows_scr[...] = g_two.astype(F32)
    g2 = rows_scr[own_rows, :].astype(BF)
    g_both = jnp.concatenate([g1, g2], axis=1)

    def q_body(at, carry):
        first = sect * ATOMS + at * 2
        right = jnp.concatenate(
            [
                jnp.concatenate([u_rows(u_one, first + q), u_rows(u_two, first + q)], axis=0)
                for q in range(2)
            ],
            axis=1,
        )
        out = nn(g_both, right).astype(BF)
        for q in range(2):
            q_scr[pl.ds(pl.multiple_of((at * 2 + q) * ATOMS, ATOMS), ATOMS), :] = out[
                :, q * H : (q + 1) * H
            ]
        return carry

    lax.fori_loop(0, 16, q_body, 0, unroll=8)
    own_cols = pl.ds(pl.multiple_of(sect * EPM, EPM), EPM)
    feat_own = feat_ref[:, own_cols]
    pre_own = edge_front(feat_own, w_ein, b_ein)
    sig = sigmoid(pre_own)
    slope = sig * (1.0 + pre_own * (1.0 - sig))
    rows_scr[0:8, :] = pair.astype(F32)
    pair_own = rows_scr[pl.ds(sect * 2, 2), :].astype(jnp.int32)
    hot = jnp.concatenate(
        [jnp.where(slot == pair_own[part : part + 1, :], 1.0, 0.0).astype(BF) for part in range(2)],
        axis=1,
    )
    g_pre = tn(hot, q_scr[...]) * slope

    adj_f = adj.astype(F32)
    del adj_f
    g_share_t = nn(g_one_t, adj), nn(g_two_t, adj)
    grad_b_out = fine_left(nn, g_share_t[0], states0) + fine_left(nn, g_share_t[1], states1)
    rows_scr[...] = grad_b_out
    small_scr[0:32, :] = rows_scr[own_rows, :]
    both_rows = jnp.concatenate(
        [msg_one.astype(F32).T, msg_two.astype(F32).T], axis=1
    )
    d_in_both = jnp.concatenate([d_in1, d_in2], axis=0)
    d_hid_both = jnp.concatenate([d_hid1, d_hid2], axis=0)
    for at, (rows_t, d_both) in enumerate(
        ((both_rows, d_in_both), (both_t.astype(F32), d_hid_both))
    ):
        rows_scr[...] = rows_t[:, :H]
        first = rows_scr[own_rows, :]
        rows_scr[...] = rows_t[:, H:]
        left = jnp.concatenate([first, rows_scr[own_rows, :]], axis=1).astype(BF)
        out = nn(left, d_both)
        for part in range(3):
            row = 32 + at * 96 + part * 32
            small_scr[row : row + 32, :] = out[:, part * H : (part + 1) * H]
    small_scr[224:240, :] = fine_right(nn, feat_own, g_pre)
    small_scr[240:256, :] = jnp.zeros((16, H), F32)
    small_scr[240:241, :] = jnp.sum(g_pre, axis=0, keepdims=True)
    for at, pair_d in enumerate(((d_in1, d_in2), (d_hid1, d_hid2))):
        for part in range(3):
            cols = slice(part * H, (part + 1) * H)
            rows_scr[...] = pair_d[0][:, cols].astype(F32) + pair_d[1][:, cols].astype(F32)
            row = 241 + at * 3 + part
            small_scr[row : row + 1, :] = jnp.sum(rows_scr[own_rows, :], axis=0, keepdims=True)
    for at in range(GROUP):
        high, low = halves(small_scr[at * SMALL : (at + 1) * SMALL, :])
        send_ref[at, H:ROWS, :] = jnp.concatenate([high.astype(F32), low.astype(F32)], axis=0).astype(BF)

    rows_scr[...] = back_zero + fine(nn, nn(adj_t, g_one), b_mat)
    base_ref[...] = rows_scr[own_rows, :]
    grad_t_ref[...] = g_one_t
    pairs_out_ref[...] = pair_h[pl.ds(pl.multiple_of(sect * PAIRS, PAIRS), PAIRS), :]


def sum_kernel(got_ref, out_ref):
    def body(at, total):
        return total + got_ref[at].astype(F32)

    total = lax.fori_loop(1, GROUP, body, got_ref[0].astype(F32), unroll=True)
    small = total[H : H + SMALL] + total[H + SMALL : ROWS]
    high, low = halves(small)
    piece = jnp.concatenate([total[:H].T, high.astype(F32), low.astype(F32)], axis=0).astype(BF)

    def put(at, carry):
        out_ref[at] = piece
        return carry

    lax.fori_loop(0, 2 * GROUP, put, 0, unroll=8)


def states_kernel(sect_ref, base_ref, grad_t_ref, pairs_ref, w_ref, out_ref, d_all, rows_scr):
    sect = sect_ref[0]
    rows_scr[...] = grad_t_ref[...].astype(F32).T
    own = rows_scr[pl.ds(pl.multiple_of(sect * ATOMS, ATOMS), ATOMS), :]
    left = own.T.astype(BF)
    gap = ATOMS + 1

    def body(at, carry):
        right = jnp.concatenate(
            [
                pairs_ref[pl.ds(pl.multiple_of((at * 4 + q) * ATOMS, ATOMS), ATOMS), :]
                for q in range(4)
            ],
            axis=1,
        )
        out = nn(left, right)
        for q in range(4):
            d_all[pl.ds(at * 4 + q, H, stride=gap), :] = out[:, q * H : (q + 1) * H]
        return carry

    lax.fori_loop(0, 8, body, 0, unroll=True)

    def back_body(at, total):
        base = pl.multiple_of(at * 4 * H, 4 * H)
        left = jnp.concatenate(
            [d_all[pl.ds((at * 4 + q) * gap, ATOMS), :].astype(BF) for q in range(4)], axis=1
        )
        right = jnp.concatenate([w_ref[:, pl.ds(base + q * H, H)] for q in range(4)], axis=0)
        return total + nn(left, right)

    out_ref[...] = lax.fori_loop(0, 32, back_body, base_ref[...], unroll=8)


def place_kernel(count, core_ref, got_ref, out_hbm, stage, sems):
    core = core_ref[0]
    steps = [(half, row) for half in range(2) for row in range(8)]

    def copy(at):
        half, row = steps[at]
        section = half * 2 + core
        cols = pl.ds(pl.multiple_of(section * GROUP * H, GROUP * H), GROUP * H)
        return pltpu.make_async_copy(
            stage.at[at % 4], out_hbm.at[pl.ds(row * 16, 16), cols], sems.at[at % 4]
        )

    for at, (half, row) in enumerate(steps):
        if at >= 4:
            copy(at - 4).wait()
        for dev in range(GROUP):
            stage[at % 4, :, dev * H : (dev + 1) * H] = got_ref[
                half * GROUP + dev, row * 16 : (row + 1) * 16, :
            ].astype(F32)
        copy(at).start()
    for at in range(len(steps) - 4, len(steps)):
        copy(at).wait()


def first_kernel(core_ref, got_ref, out_hbm, stage, sems):
    place_kernel(2, core_ref, got_ref, out_hbm, stage, sems)


def second_kernel(
    core_ref, other_ref, mine_ref, far_ref, half_hbm, out_hbm, gb_ref, gi_ref, gh_ref, misc_ref, small, stage, sems
):
    del half_hbm
    place_kernel(2, other_ref, far_ref, out_hbm, stage, sems)
    for which, ref in ((core_ref[0], mine_ref), (other_ref[0], far_ref)):
        for half in range(2):
            base = (half * 2 + which) * (GROUP * SMALL)
            for dev in range(GROUP):
                both = ref[half * GROUP + dev, H:ROWS, :].astype(F32)
                at = pl.multiple_of(base + dev * SMALL, SMALL)
                small[pl.ds(at, SMALL), :] = both[:SMALL] + both[SMALL:]
    misc = jnp.zeros((32, H), F32)
    for sect in range(MB):
        base = sect * GROUP * SMALL
        rows = slice(sect * 32, (sect + 1) * 32)
        gb_ref[rows, :] = small[base : base + 32, :]
        for part in range(3):
            cols = slice(part * H, (part + 1) * H)
            row = base + 32 + part * 32
            gi_ref[rows, cols] = small[row : row + 32, :]
            gh_ref[rows, cols] = small[row + 96 : row + 128, :]
        misc = misc + small[base + 224 : base + 256, :]
    misc_ref[...] = misc


def local(
    node_states,
    edge_features,
    edge_source,
    edge_target,
    edge_live,
    w_edge_in,
    b_edge_in,
    w_edge_out,
    b_edge_out,
    w_input,
    w_hidden,
    b_input,
    b_hidden,
    cotangent,
):
    vmem = pl.BlockSpec(memory_space=pltpu.VMEM)
    smem = pl.BlockSpec(memory_space=pltpu.SMEM)
    hbm = pl.BlockSpec(memory_space=pl.ANY)
    shape = jax.ShapeDtypeStruct
    limit = 60 * 2**20
    core = lax.axis_index("core").astype(jnp.int32)
    sect = (lax.axis_index("zh") * 2 + core).astype(jnp.int32)
    sect = sect.reshape(1)
    mine = core.reshape(1)
    other = 1 - mine
    ends = jnp.stack([edge_source, edge_target, edge_live]).reshape(3, 8, 128)

    send, final, base, grad_t, pairs = pl.pallas_call(
        local_kernel,
        out_shape=(
            shape((GROUP, ROWS, H), BF),
            shape((ATOMS, H), F32),
            shape((ATOMS, H), F32),
            shape((H, NODES), BF),
            shape((PAIRS, H), BF),
        ),
        in_specs=[smem] + [vmem] * 5 + [hbm] + [vmem] * 6,
        out_specs=(vmem,) * 5,
        scratch_shapes=[
            pltpu.VMEM((H, H * H), BF),
            pltpu.VMEM((NODES * GAP, H), F32),
            pltpu.VMEM((NODES * GAP, H), F32),
            pltpu.VMEM((H * GAP, H), F32),
            pltpu.VMEM((OWN * GAP, H), F32),
            pltpu.VMEM((MB * PAIRS, H), BF),
            pltpu.VMEM((NODES, H), F32),
            pltpu.VMEM((GROUP * SMALL, H), F32),
            pltpu.VMEM((PAIRS, H), BF),
            pltpu.SemaphoreType.DMA((8,)),
        ],
        compiler_params=pltpu.CompilerParams(vmem_limit_bytes=limit),
        name="layers",
    )(
        sect,
        node_states,
        edge_features,
        ends,
        w_edge_in,
        b_edge_in.reshape(1, H),
        w_edge_out,
        b_edge_out.reshape(H, H),
        w_input,
        w_hidden,
        b_input.reshape(1, 3 * H),
        b_hidden.reshape(1, 3 * H),
        cotangent,
    )

    got = lax.all_to_all(send, "dp", split_axis=0, concat_axis=0)
    piece = pl.pallas_call(
        sum_kernel,
        out_shape=shape((2 * GROUP, ROWS, H), BF),
        in_specs=[vmem],
        out_specs=vmem,
        compiler_params=pltpu.CompilerParams(vmem_limit_bytes=limit),
        name="sum_parts",
    )(got)
    near = lax.all_to_all(piece, ("zh", "dp"), split_axis=0, concat_axis=0)
    far = lax.ppermute(near, "core", [(0, 1), (1, 0)])

    stage = [pltpu.VMEM((4, 16, GROUP * H), F32), pltpu.SemaphoreType.DMA((4,))]
    half = pl.pallas_call(
        first_kernel,
        out_shape=shape((H, H * H), F32),
        in_specs=[smem, vmem],
        out_specs=hbm,
        scratch_shapes=stage,
        compiler_params=pltpu.CompilerParams(vmem_limit_bytes=limit),
        name="place_near",
    )(mine, near)
    grad_states = pl.pallas_call(
        states_kernel,
        out_shape=shape((ATOMS, H), F32),
        in_specs=[smem] + [vmem] * 4,
        out_specs=vmem,
        scratch_shapes=[pltpu.VMEM((H * (ATOMS + 1), H), F32), pltpu.VMEM((NODES, H), F32)],
        compiler_params=pltpu.CompilerParams(vmem_limit_bytes=limit),
        name="states_back",
    )(sect, base, grad_t, pairs, w_edge_out)
    grad_w_out, grad_b_out, grad_w_in, grad_w_hid, misc = pl.pallas_call(
        second_kernel,
        out_shape=(
            shape((H, H * H), F32),
            shape((H, H), F32),
            shape((H, 3 * H), F32),
            shape((H, 3 * H), F32),
            shape((32, H), F32),
        ),
        in_specs=[smem, smem, vmem, vmem, hbm],
        out_specs=(hbm, vmem, vmem, vmem, vmem),
        scratch_shapes=[pltpu.VMEM((MB * GROUP * SMALL, H), F32)] + stage,
        input_output_aliases={4: 0},
        compiler_params=pltpu.CompilerParams(vmem_limit_bytes=limit),
        name="place_far",
    )(mine, other, near, far, half)
    return (
        final,
        grad_states,
        misc[:16],
        misc[16],
        grad_w_out,
        grad_b_out.reshape(H * H),
        grad_w_in,
        grad_w_hid,
        misc[17:20].reshape(3 * H),
        misc[20:23].reshape(3 * H),
    )


def solution(mesh):
    wide = Mesh(mesh.devices.reshape(2, 2, GROUP), ("zh", "core", "dp"))
    split = P(("dp", "zh", "core"), None)
    in_specs = (
        P("dp", None),
        P(None, "dp"),
        P("dp"),
        P("dp"),
        P("dp"),
        P(),
        P(),
        P(),
        P(),
        P(),
        P(),
        P(),
        P(),
        P("dp", None),
    )
    out_specs = (split, split, P(), P(), P(), P(), P(), P(), P(), P())
    return jax.shard_map(local, mesh=wide, in_specs=in_specs, out_specs=out_specs, check_vma=False)
```

profile of v0, /device:TPU:1, one launch (start us, length us, event | category | flops | bytes accessed | tf_op | source)
XLA Modules:
  0.0 115.0 jit_solution(13687426142660106820)
XLA Ops:
  0.6 1.2 %reshape.57.b_in_ref = f32[1,384]{1,0:T(1,128)} reshape(f32[384]{0:T(512)} %param.25) | data formatting | bytes 3072 | tf_op jit(solution)/shard_map/reshape | solution.py:544
  1.9 1.2 %reshape.58.b_hid_ref = f32[1,384]{1,0:T(1,128)} reshape(f32[384]{0:T(512)} %param.26) | data formatting | bytes 3072 | tf_op jit(solution)/shard_map/reshape | solution.py:545
  3.1 1.3 %pad_add_fusion.ends_ref = s32[3,8,128]{2,1,0:T(8,128)} fusion(s32[1,8,128]{2,1,0:T(8,128)} %bitcast.15, s32[1,8,128]{2,1,0:T(8,128)} %bitcast.16, s32[1,8,128]{2,1,0:T(8,128)} %bitcast.17), kind=kLoop, calls=%fused_computation | loop fusion | flops 6144 | bytes 24576 | tf_op jit(solution)/shard_map/stack | solution.py:506
  4.5 18.5 %layers.1 = (bf16[32,144,128]{2,1,0:T(8,128)(2,1)}, f32[32,128]{1,0:T(8,128)}, f32[32,128]{1,0:T(8,128)}, bf16[128,128]{1,0:T(8,128)(2,1)}, bf16[1024,128]{1,0:T(8,128)(2,1)}) custom-call(s32[1]{0:T(128)} %bitcast.sect_ref, bf16[128,128]{1,0:T(8,128)(2,1)} %states_ref.1, bf16[16,1024]{1,0:T(8,128)(2,1)} %feat_ref.1, s32[3,8,128]{2,1,0:T(8,128)} %pad_add_fusion.ends_ref, ...), custom_call_target="tpu_custom_call" | custom-call | tf_op jit(solution)/shard_map/layers/pallas_call | solution.py:508
  23.0 27.2 %all_to_all.10.got_ref = bf16[32,144,128]{2,1,0:T(8,128)(2,1)} all-to-all(bf16[32,144,128]{2,1,0:T(8,128)(2,1)} %get-tuple-element.24), channel_id=1, replica_groups=mesh['zh'=2,'core'=2,'dp'=32] {'dp'}, dimensions={0} | all-to-all | bytes 2359296 | tf_op jit(solution)/shard_map/all_to_all | solution.py:549
  50.2 3.1 %sum_parts.1 = bf16[64,144,128]{2,1,0:T(8,128)(2,1)} custom-call(bf16[32,144,128]{2,1,0:T(8,128)(2,1)} %all_to_all.10.got_ref), custom_call_target="tpu_custom_call" | custom-call | tf_op jit(solution)/shard_map/sum_parts/pallas_call | solution.py:550
  53.2 37.9 %all_to_all.11.got_ref.mine_ref = bf16[64,144,128]{2,1,0:T(8,128)(2,1)S(1)} all-to-all(bf16[64,144,128]{2,1,0:T(8,128)(2,1)} %sum_parts.1), channel_id=1, replica_groups=mesh['zh'=2,'core'=2,'dp'=32] {'zh','dp'}, dimensions={0} | all-to-all | bytes 4718592 | tf_op jit(solution)/shard_map/all_to_all | solution.py:558
  91.2 0.0 copy-start
  91.2 3.3 %collective-permute-start = (bf16[64,144,128]{2,1,0:T(8,128)(2,1)S(1)}, bf16[64,144,128]{2,1,0:T(8,128)(2,1)}, u32[]{:S(2)}, u32[]{:S(2)}) collective-permute-start(bf16[64,144,128]{2,1,0:T(8,128)(2,1)S(1)} %all_to_all.11.got_ref.mine_ref), channel_id=1, source_target_pairs={{0,32},{32,0},{1,33},{33,1},{2,34},{34,2},{3,35},{35,3},{4,36},{36... | collective-permute-start | bytes 7077896 | tf_op jit(solution)/shard_map/ppermute | solution.py:559
  94.5 5.4 %states_back.1 = f32[32,128]{1,0:T(8,128)} custom-call(s32[1]{0:T(128)} %bitcast.sect_ref, f32[32,128]{1,0:T(8,128)} %get-tuple-element.21.base_ref, bf16[128,128]{1,0:T(8,128)(2,1)} %get-tuple-element.22.grad_t_ref, bf16[1024,128]{1,0:T(8,128)(2,1)} %get-tuple-element.23.pairs_ref, bf16[128,16384]{1,0:T(8,128)(2,1)} %w_ref.1), custom_call_target="tpu_custom_call" | custom-call | tf_op jit(solution)/shard_map/states_back/pallas_call | solution.py:571
  99.9 0.0 copy-done
  99.9 4.8 %place_near.1.half_hbm = f32[128,16384]{1,0:T(8,128)} custom-call(s32[1]{0:T(128)} %bitcast.6.core_ref, bf16[64,144,128]{2,1,0:T(8,128)(2,1)} %copy-done), custom_call_target="tpu_custom_call" | custom-call | tf_op jit(solution)/shard_map/place_near/pallas_call | solution.py:562
  104.8 0.0 collective-permute-done.far_ref
  104.8 6.4 %place_far.1 = (f32[128,16384]{1,0:T(8,128)}, f32[128,128]{1,0:T(8,128)}, f32[128,384]{1,0:T(8,128)}, f32[128,384]{1,0:T(8,128)}, f32[32,128]{1,0:T(8,128)}) custom-call(s32[1]{0:T(128)} %bitcast.6.core_ref, s32[1]{0:T(128)S(6)} %sub.3.other_ref, bf16[64,144,128]{2,1,0:T(8,128)(2,1)} %copy-done, ...), custom_call_target="tpu_custom_call", output_to_operand_aliasing={{0}: (4, {})} | custom-call | tf_op jit(solution)/shard_map/place_far/pallas_call | solution.py:580
  111.2 1.2 %slice_bitcast_fusion.2 = f32[128]{0:T(128)} fusion(f32[32,128]{1,0:T(8,128)} %get-tuple-element.25), kind=kLoop, calls=%fused_computation.3 | loop fusion | bytes 1024 | tf_op jit(solution)/shard_map/squeeze | solution.py:600
  112.4 1.3 %slice_bitcast_fusion = (f32[384]{0:T(512)}, f32[384]{0:T(512)}) fusion(f32[32,128]{1,0:T(8,128)} %get-tuple-element.25), kind=kLoop, calls=%fused_computation.1 | loop fusion | bytes 6144 | tf_op jit(solution)/shard_map/reshape | solution.py:606
  113.7 1.3 %slice.12 = f32[16,128]{1,0:T(8,128)} slice(f32[32,128]{1,0:T(8,128)} %get-tuple-element.25), slice={[0:16], [0:128]} | slice | bytes 16384 | tf_op jit(solution)/shard_map/slice | solution.py:599
Async XLA Ops:
  91.2 8.7 %copy-start = (bf16[64,144,128]{2,1,0:T(8,128)(2,1)}, bf16[64,144,128]{2,1,0:T(8,128)(2,1)S(1)}, u32[]{:S(2)}) copy-start(bf16[64,144,128]{2,1,0:T(8,128)(2,1)S(1)} %all_to_all.11.got_ref.mine_ref) | copy-start | bytes 7077892
  91.2 13.6 %collective-permute-start = (bf16[64,144,128]{2,1,0:T(8,128)(2,1)S(1)}, bf16[64,144,128]{2,1,0:T(8,128)(2,1)}, u32[]{:S(2)}, u32[]{:S(2)}) collective-permute-start(bf16[64,144,128]{2,1,0:T(8,128)(2,1)S(1)} %all_to_all.11.got_ref.mine_ref), channel_id=1, source_target_pairs={{0,32},{32,0},{1,33},{33,1},{2,34},{34,2},{3,35},{35,3},{4,36},{36... | collective-permute-start | bytes 7077896 | tf_op jit(solution)/shard_map/ppermute | solution.py:559
where the time goes:
time: 116 us; the launch traced here: 115 us
  blocking collectives  65.1 us (56%)
  Pallas kernels  38.2 us (33%)
  local copies, waits for them, and re-layouts  6.33 us (5%)
  starting transfers between devices  3.34 us (3%)
  other arithmetic  1.32 us (1%)
    all_to_all x1, blocking collectives, local(): near = lax.all_to_all(piece, ('zh', 'dp'), split_axis=0, concat_axis=0)  37.9 us
    all_to_all x1, blocking collectives, local(): got = lax.all_to_all(send, 'dp', split_axis=0, concat_axis=0)  27.2 us
    pallas_call x1, Pallas kernels, local(): pl.pallas_call(local_kernel, out_shape=(shape((GROUP, ROWS, H), BF), shap...  18.5 us
    pallas_call x1, Pallas kernels, local(): pl.pallas_call(second_kernel, out_shape=(shape((H, H * H), F32), shape((H...  6.38 us
    pallas_call x1, Pallas kernels, local(): pl.pallas_call(states_kernel, out_shape=shape((ATOMS, H), F32), in_specs=...  5.39 us
    pallas_call x1, Pallas kernels, local(): pl.pallas_call(first_kernel, out_shape=shape((H, H * H), F32), in_specs=[...  4.83 us
    ppermute x1, starting transfers between devices, local(): far = lax.ppermute(near, 'core', [(0, 1), (1, 0)])  3.34 us
    pallas_call x1, Pallas kernels, local(): pl.pallas_call(sum_kernel, out_shape=shape((2 * GROUP, ROWS, H), BF), in_...  3.07 us
  transfers between devices with their start and end apart: 1, of which 0 were waited for; matrix products, arithmetic and copies ran while one was open for 0% of the time, Pallas kernels for 9%

commit v1 on v0

--- a/solution.py
+++ b/solution.py
@@ -16,7 +16,7 @@
 PAIRS = ATOMS * ATOMS
 OWN = H // MB
 GAP = 129
-ROWS = 144
+ROWS = 136
 SMALL = 8
 GROUP = 32
 BF = jnp.bfloat16
@@ -87,53 +87,51 @@
     return tn(features, w_edge_in) + b_edge_in
 
 
-def local_kernel(
-    sect_ref,
-    states_ref,
-    feat_ref,
-    ends_ref,
-    w_ein_ref,
-    b_ein_ref,
-    w_hbm,
-    b_mat_ref,
-    w_in_ref,
-    w_hid_ref,
-    b_in_ref,
-    b_hid_ref,
-    cot_ref,
-    send_ref,
-    final_ref,
-    base_ref,
-    grad_t_ref,
-    pairs_out_ref,
-    w_ref,
-    u_one,
-    u_two,
-    d_all,
-    d_own,
-    pair_h,
-    rows_scr,
-    small_scr,
-    q_scr,
-    sems,
-):
+def local_kernel(sect_ref, *refs):
+    ins, refs = refs[:14], refs[14:]
+    (send_ref, final_ref, base_ref, grad_t_ref, pairs_out_ref), refs = refs[:5], refs[5:]
+    held, refs = refs[:14], refs[14:]
+    u_one, u_two, d_all, d_own, pair_h, rows_scr, small_scr, q_scr, sems, w_sems = refs
+    (
+        source_ref,
+        target_ref,
+        live_ref,
+        feat_ref,
+        w_ein_ref,
+        b_ein_ref,
+        states_ref,
+        b_mat_ref,
+        w_in_ref,
+        w_hid_ref,
+        b_in_ref,
+        b_hid_ref,
+        cot_ref,
+        w_ref,
+    ) = held
     sect = sect_ref[0]
     chunk = 2048
+    copies = [
+        pltpu.make_async_copy(ins[at], held[at], sems.at[at]) for at in range(13)
+    ]
 
     def w_copy(at):
         cols = pl.ds(at * chunk, chunk)
-        return pltpu.make_async_copy(w_hbm.at[:, cols], w_ref.at[:, cols], sems.at[at])
-
+        return pltpu.make_async_copy(ins[13].at[:, cols], w_ref.at[:, cols], w_sems.at[at])
+
+    for copy in copies:
+        copy.start()
     for at in range(8):
         w_copy(at).start()
+    for copy in copies:
+        copy.wait()
 
     states0 = states_ref[...]
     w_ein = w_ein_ref[...]
     b_ein = b_ein_ref[...]
     b_mat = b_mat_ref[...]
-    source = ends_ref[0]
-    target = ends_ref[1]
-    live = ends_ref[2]
+    source = source_ref[...]
+    target = target_ref[...]
+    live = live_ref[...]
     pair = jnp.where(live > 0, source * ATOMS + target, -1)
 
     slot = lax.broadcasted_iota(jnp.int32, (PAIRS, H), 0)
@@ -210,8 +208,8 @@
 
     w_in = w_in_ref[...]
     w_hid = w_hid_ref[...]
-    b_in = b_in_ref[...]
-    b_hid = b_hid_ref[...]
+    b_in = jnp.concatenate([b_in_ref[part : part + 1, :] for part in range(3)], axis=1)
+    b_hid = jnp.concatenate([b_hid_ref[part : part + 1, :] for part in range(3)], axis=1)
 
     spread(states0, u_one, True)
     msg_one = gather(states0, u_one)
@@ -333,8 +331,6 @@
     )
     g_pre = tn(hot, q_scr[...]) * slope
 
-    adj_f = adj.astype(F32)
-    del adj_f
     g_share_t = nn(g_one_t, adj), nn(g_two_t, adj)
     grad_b_out = fine_left(nn, g_share_t[0], states0) + fine_left(nn, g_share_t[1], states1)
     rows_scr[...] = grad_b_out
@@ -365,8 +361,7 @@
             row = 241 + at * 3 + part
             small_scr[row : row + 1, :] = jnp.sum(rows_scr[own_rows, :], axis=0, keepdims=True)
     for at in range(GROUP):
-        high, low = halves(small_scr[at * SMALL : (at + 1) * SMALL, :])
-        send_ref[at, H:ROWS, :] = jnp.concatenate([high.astype(F32), low.astype(F32)], axis=0).astype(BF)
+        send_ref[at, H:ROWS, :] = small_scr[at * SMALL : (at + 1) * SMALL, :].astype(BF)
 
     rows_scr[...] = back_zero + fine(nn, nn(adj_t, g_one), b_mat)
     base_ref[...] = rows_scr[own_rows, :]
@@ -379,9 +374,7 @@
         return total + got_ref[at].astype(F32)
 
     total = lax.fori_loop(1, GROUP, body, got_ref[0].astype(F32), unroll=True)
-    small = total[H : H + SMALL] + total[H + SMALL : ROWS]
-    high, low = halves(small)
-    piece = jnp.concatenate([total[:H].T, high.astype(F32), low.astype(F32)], axis=0).astype(BF)
+    piece = jnp.concatenate([total[:H].T, total[H:]], axis=0).astype(BF)
 
     def put(at, carry):
         out_ref[at] = piece
@@ -452,7 +445,7 @@
 
 
 def second_kernel(
-    core_ref, other_ref, mine_ref, far_ref, half_hbm, out_hbm, gb_ref, gi_ref, gh_ref, misc_ref, small, stage, sems
+    core_ref, other_ref, mine_ref, far_ref, half_hbm, out_hbm, gb_ref, gi_ref, gh_ref, ge_ref, be_ref, bi_ref, bh_ref, small, stage, sems
 ):
     del half_hbm
     place_kernel(2, other_ref, far_ref, out_hbm, stage, sems)
@@ -460,9 +453,8 @@
         for half in range(2):
             base = (half * 2 + which) * (GROUP * SMALL)
             for dev in range(GROUP):
-                both = ref[half * GROUP + dev, H:ROWS, :].astype(F32)
                 at = pl.multiple_of(base + dev * SMALL, SMALL)
-                small[pl.ds(at, SMALL), :] = both[:SMALL] + both[SMALL:]
+                small[pl.ds(at, SMALL), :] = ref[half * GROUP + dev, H:ROWS, :].astype(F32)
     misc = jnp.zeros((32, H), F32)
     for sect in range(MB):
         base = sect * GROUP * SMALL
@@ -474,7 +466,48 @@
             gi_ref[rows, cols] = small[row : row + 32, :]
             gh_ref[rows, cols] = small[row + 96 : row + 128, :]
         misc = misc + small[base + 224 : base + 256, :]
-    misc_ref[...] = misc
+    ge_ref[...] = misc[0:16]
+    be_ref[...] = misc[16:17]
+    bi_ref[...] = misc[17:20]
+    bh_ref[...] = misc[20:23]
+
+
+VMEM_SPEC = pl.BlockSpec(memory_space=pltpu.VMEM)
+SMEM_SPEC = pl.BlockSpec(memory_space=pltpu.SMEM)
+ANY_SPEC = pl.BlockSpec(memory_space=pl.ANY)
+BIG = 60 * 2**20
+LOW = 8 * 2**20
+shape = jax.ShapeDtypeStruct
+
+
+def run_layers(sect, operands):
+    return pl.pallas_call(
+        local_kernel,
+        out_shape=(
+            shape((GROUP, ROWS, H), BF),
+            shape((ATOMS, H), F32),
+            shape((ATOMS, H), F32),
+            shape((H, NODES), BF),
+            shape((PAIRS, H), BF),
+        ),
+        in_specs=[SMEM_SPEC] + [ANY_SPEC] * 14,
+        out_specs=(VMEM_SPEC,) * 5,
+        scratch_shapes=[pltpu.VMEM(v.shape, v.dtype) for v in operands]
+        + [
+            pltpu.VMEM((NODES * GAP, H), F32),
+            pltpu.VMEM((NODES * GAP, H), F32),
+            pltpu.VMEM((H * GAP, H), F32),
+            pltpu.VMEM((OWN * GAP, H), F32),
+            pltpu.VMEM((MB * PAIRS, H), BF),
+            pltpu.VMEM((NODES, H), F32),
+            pltpu.VMEM((GROUP * SMALL, H), F32),
+            pltpu.VMEM((PAIRS, H), BF),
+            pltpu.SemaphoreType.DMA((13,)),
+            pltpu.SemaphoreType.DMA((8,)),
+        ],
+        compiler_params=pltpu.CompilerParams(vmem_limit_bytes=BIG),
+        name="layers",
+    )(sect, *operands)
 
 
 def local(
@@ -493,117 +526,91 @@
     b_hidden,
     cotangent,
 ):
-    vmem = pl.BlockSpec(memory_space=pltpu.VMEM)
-    smem = pl.BlockSpec(memory_space=pltpu.SMEM)
-    hbm = pl.BlockSpec(memory_space=pl.ANY)
-    shape = jax.ShapeDtypeStruct
-    limit = 60 * 2**20
     core = lax.axis_index("core").astype(jnp.int32)
     sect = (lax.axis_index("zh") * 2 + core).astype(jnp.int32)
     sect = sect.reshape(1)
     mine = core.reshape(1)
     other = 1 - mine
-    ends = jnp.stack([edge_source, edge_target, edge_live]).reshape(3, 8, 128)
-
-    send, final, base, grad_t, pairs = pl.pallas_call(
-        local_kernel,
-        out_shape=(
-            shape((GROUP, ROWS, H), BF),
-            shape((ATOMS, H), F32),
-            shape((ATOMS, H), F32),
-            shape((H, NODES), BF),
-            shape((PAIRS, H), BF),
-        ),
-        in_specs=[smem] + [vmem] * 5 + [hbm] + [vmem] * 6,
-        out_specs=(vmem,) * 5,
-        scratch_shapes=[
-            pltpu.VMEM((H, H * H), BF),
-            pltpu.VMEM((NODES * GAP, H), F32),
-            pltpu.VMEM((NODES * GAP, H), F32),
-            pltpu.VMEM((H * GAP, H), F32),
-            pltpu.VMEM((OWN * GAP, H), F32),
-            pltpu.VMEM((MB * PAIRS, H), BF),
-            pltpu.VMEM((NODES, H), F32),
-            pltpu.VMEM((GROUP * SMALL, H), F32),
-            pltpu.VMEM((PAIRS, H), BF),
-            pltpu.SemaphoreType.DMA((8,)),
-        ],
-        compiler_params=pltpu.CompilerParams(vmem_limit_bytes=limit),
-        name="layers",
-    )(
-        sect,
-        node_states,
+    operands = [v.reshape(8, 128) for v in (edge_source, edge_target, edge_live)] + [
         edge_features,
-        ends,
         w_edge_in,
         b_edge_in.reshape(1, H),
-        w_edge_out,
+        node_states,
         b_edge_out.reshape(H, H),
         w_input,
         w_hidden,
-        b_input.reshape(1, 3 * H),
-        b_hidden.reshape(1, 3 * H),
+        b_input.reshape(3, H),
+        b_hidden.reshape(3, H),
         cotangent,
-    )
-
+        w_edge_out,
+    ]
+
+    send, final, base, grad_t, pairs = run_layers(sect, operands)
     got = lax.all_to_all(send, "dp", split_axis=0, concat_axis=0)
     piece = pl.pallas_call(
         sum_kernel,
         out_shape=shape((2 * GROUP, ROWS, H), BF),
-        in_specs=[vmem],
-        out_specs=vmem,
-        compiler_params=pltpu.CompilerParams(vmem_limit_bytes=limit),
+        in_specs=[VMEM_SPEC],
+        out_specs=VMEM_SPEC,
+        compiler_params=pltpu.CompilerParams(vmem_limit_bytes=LOW),
         name="sum_parts",
     )(got)
+    grad_states = pl.pallas_call(
+        states_kernel,
+        out_shape=shape((ATOMS, H), F32),
+        in_specs=[SMEM_SPEC] + [VMEM_SPEC] * 4,
+        out_specs=VMEM_SPEC,
+        scratch_shapes=[pltpu.VMEM((H * (ATOMS + 1), H), F32), pltpu.VMEM((NODES, H), F32)],
+        compiler_params=pltpu.CompilerParams(vmem_limit_bytes=LOW),
+        cost_estimate=pl.CostEstimate(
+            flops=2 * ATOMS * H * H * H, bytes_accessed=2 * H * H * H, transcendentals=0
+        ),
+        name="states_back",
+    )(sect, base, grad_t, pairs, w_edge_out)
     near = lax.all_to_all(piece, ("zh", "dp"), split_axis=0, concat_axis=0)
+    near, grad_states = lax.optimization_barrier((near, grad_states))
     far = lax.ppermute(near, "core", [(0, 1), (1, 0)])
 
     stage = [pltpu.VMEM((4, 16, GROUP * H), F32), pltpu.SemaphoreType.DMA((4,))]
     half = pl.pallas_call(
         first_kernel,
         out_shape=shape((H, H * H), F32),
-        in_specs=[smem, vmem],
-        out_specs=hbm,
+        in_specs=[SMEM_SPEC, VMEM_SPEC],
+        out_specs=ANY_SPEC,
         scratch_shapes=stage,
-        compiler_params=pltpu.CompilerParams(vmem_limit_bytes=limit),
+        compiler_params=pltpu.CompilerParams(vmem_limit_bytes=LOW),
         name="place_near",
     )(mine, near)
-    grad_states = pl.pallas_call(
-        states_kernel,
-        out_shape=shape((ATOMS, H), F32),
-        in_specs=[smem] + [vmem] * 4,
-        out_specs=vmem,
-        scratch_shapes=[pltpu.VMEM((H * (ATOMS + 1), H), F32), pltpu.VMEM((NODES, H), F32)],
-        compiler_params=pltpu.CompilerParams(vmem_limit_bytes=limit),
-        name="states_back",
-    )(sect, base, grad_t, pairs, w_edge_out)
-    grad_w_out, grad_b_out, grad_w_in, grad_w_hid, misc = pl.pallas_call(
+    grad_w_out, grad_b_out, grad_w_in, grad_w_hid, grad_ein, grad_bein, grad_bin, grad_bhid = pl.pallas_call(
         second_kernel,
         out_shape=(
             shape((H, H * H), F32),
             shape((H, H), F32),
             shape((H, 3 * H), F32),
             shape((H, 3 * H), F32),
-            shape((32, H), F32),
+            shape((16, H), F32),
+            shape((1, H), F32),
+            shape((3, H), F32),
+            shape((3, H), F32),
         ),
-        in_specs=[smem, smem, vmem, vmem, hbm],
-        out_specs=(hbm, vmem, vmem, vmem, vmem),
+        in_specs=[SMEM_SPEC, SMEM_SPEC, VMEM_SPEC, VMEM_SPEC, ANY_SPEC],
+        out_specs=(ANY_SPEC,) + (VMEM_SPEC,) * 7,
         scratch_shapes=[pltpu.VMEM((MB * GROUP * SMALL, H), F32)] + stage,
         input_output_aliases={4: 0},
-        compiler_params=pltpu.CompilerParams(vmem_limit_bytes=limit),
+        compiler_params=pltpu.CompilerParams(vmem_limit_bytes=LOW),
         name="place_far",
     )(mine, other, near, far, half)
     return (
         final,
         grad_states,
-        misc[:16],
-        misc[16],
+        grad_ein,
+        grad_bein.reshape(H),
         grad_w_out,
         grad_b_out.reshape(H * H),
         grad_w_in,
         grad_w_hid,
-        misc[17:20].reshape(3 * H),
-        misc[20:23].reshape(3 * H),
+        grad_bin.reshape(3 * H),
+        grad_bhid.reshape(3 * H),
     )
 
 

time: 116 us -> 96.6 us (0.83)
  blocking collectives: 65.1 us -> 26.7 us
  waiting for transfers between devices: 0.01 us -> 24.4 us
  Pallas kernels: 38.2 us -> 30.3 us
  starting transfers between devices: 3.34 us -> 10.7 us
  local copies, waits for them, and re-layouts: 6.33 us -> 3.55 us
  other arithmetic: 1.32 us -> 0 us
    all_to_all x1 -> x0, blocking collectives: 37.9 us -> none  [local(): near = lax.all_to_all(piece, ('zh', 'dp'), split_axis=0, concat_axis=0)]
    all_to_all x0 -> x1, waiting for transfers between devices: none -> 23.6 us  [local(): near = lax.all_to_all(piece, ('zh', 'dp'), split_axis=0, concat_axis=0)]
    all_to_all x0 -> x1, starting transfers between devices: none -> 7.24 us  [local(): near = lax.all_to_all(piece, ('zh', 'dp'), split_axis=0, concat_axis=0)]
    reshape x3 -> x0, local copies, waits for them, and re-layouts: 3.83 us -> none  [the longest x1 1.34 us: local(): misc[20:23].reshape(3 * H)]
    unnamed x2 -> x10, local copies, waits for them, and re-layouts: 0.01 us -> 3.55 us
    pallas_call x1, Pallas kernels: 3.07 us -> 0.39 us  [local(): pl.pallas_call(sum_kernel, out_shape=shape((2 * GROUP, ROWS, H), BF), in_...]
    pallas_call x1, Pallas kernels: 6.38 us -> 4 us  [local(): pl.pallas_call(second_kernel, out_shape=(shape((H, H * H), F32), shape((H...]
    pallas_call x1, Pallas kernels: 5.39 us -> 3.06 us  [local(): pl.pallas_call(states_kernel, out_shape=shape((ATOMS, H), F32), in_specs=...]
  transfers between devices with their start and end apart: 1 -> 2, of which waited for: 0 -> 2; matrix products, arithmetic and copies ran while one was open for 0% -> 0% of each run, Pallas kernels for 9% -> 6%
where the time goes in v1:
time: 96.6 us; the launch traced here: 96.3 us
  Pallas kernels  30.3 us (31%)
  blocking collectives  26.7 us (28%)
  waiting for transfers between devices  24.4 us (25%)
  starting transfers between devices  10.7 us (11%)
  local copies, waits for them, and re-layouts  3.55 us (4%)
    all_to_all x1, blocking collectives, local(): got = lax.all_to_all(send, 'dp', split_axis=0, concat_axis=0)  26.7 us
    all_to_all x1, waiting for transfers between devices, local(): near = lax.all_to_all(piece, ('zh', 'dp'), split_axis=0, concat_axis=0)  23.6 us
    pallas_call x1, Pallas kernels, run_layers(): pl.pallas_call(local_kernel, out_shape=(shape((GROUP, ROWS, H), BF), shap...  19.7 us
    all_to_all x1, starting transfers between devices, local(): near = lax.all_to_all(piece, ('zh', 'dp'), split_axis=0, concat_axis=0)  7.24 us
    pallas_call x1, Pallas kernels, local(): pl.pallas_call(second_kernel, out_shape=(shape((H, H * H), F32), shape((H...  4 us
    unnamed x10, local copies, waits for them, and re-layouts  3.55 us
    ppermute x1, starting transfers between devices, local(): far = lax.ppermute(near, 'core', [(0, 1), (1, 0)])  3.44 us
    pallas_call x1, Pallas kernels, local(): pl.pallas_call(first_kernel, out_shape=shape((H, H * H), F32), in_specs=[...  3.17 us
  transfers between devices with their start and end apart: 2, of which 2 were waited for; matrix products, arithmetic and copies ran while one was open for 0% of the time, Pallas kernels for 6%

profile of v1, /device:TPU:1, one launch (start us, length us, event | category | flops | bytes accessed | tf_op | source)
XLA Modules:
  0.0 96.3 jit_solution(9860077577052926761)
XLA Ops:
  0.7 19.7 %layers.1 = (bf16[32,136,128]{2,1,0:T(8,128)(2,1)}, f32[32,128]{1,0:T(8,128)}, f32[32,128]{1,0:T(8,128)}, bf16[128,128]{1,0:T(8,128)(2,1)}, bf16[1024,128]{1,0:T(8,128)(2,1)}) custom-call(s32[1]{0:T(128)} %bitcast.sect_ref, s32[8,128]{1,0:T(8,128)} %bitcast.14, s32[8,128]{1,0:T(8,128)} %bitcast.15, s32[8,128]{1,0:T(8,128)} %bitcast.16, ...), custom_call_target="tpu_custom_call" | custom-call | tf_op jit(solution)/shard_map/layers/pallas_call | solution.py:484
  20.3 26.7 %all_to_all.10.got_ref = bf16[32,136,128]{2,1,0:T(8,128)(2,1)S(1)} all-to-all(bf16[32,136,128]{2,1,0:T(8,128)(2,1)} %get-tuple-element.26), channel_id=1, replica_groups=mesh['zh'=2,'core'=2,'dp'=32] {'dp'}, dimensions={0} | all-to-all | bytes 2228224 | tf_op jit(solution)/shard_map/all_to_all | solution.py:549
  47.0 0.4 sum_parts.1
  47.4 0.0 copy-start.1
  47.4 1.4 %copy-done.1 = bf16[64,136,128]{2,1,0:T(8,128)(2,1)} copy-done((bf16[64,136,128]{2,1,0:T(8,128)(2,1)}, bf16[64,136,128]{2,1,0:T(8,128)(2,1)S(1)}, u32[]{:S(2)}) %copy-start.1) | copy-done | bytes 2228248
  48.8 0.0 copy-start.2
  48.8 0.0 copy-start.3
  48.8 0.0 copy-start.4
  48.8 7.2 %all-to-all-start.1 = ((bf16[64,136,128]{2,1,0:T(8,128)(2,1)}), bf16[64,136,128]{2,1,0:T(8,128)(2,1)S(1)}, u32[]{:S(2)}, u32[]{:S(2)}) async-start(bf16[64,136,128]{2,1,0:T(8,128)(2,1)} %copy-done.1), calls=%async_computation.1 | async-start | bytes 4456448 | tf_op jit(solution)/shard_map/all_to_all | solution.py:570
  56.0 0.0 copy-done.2
  56.0 0.0 copy-done.3
  56.0 0.0 copy-done.4
  56.0 0.0 copy-start
  56.1 2.2 %copy-done = bf16[128,16384]{1,0:T(8,128)(2,1)S(1)} copy-done((bf16[128,16384]{1,0:T(8,128)(2,1)S(1)}, bf16[128,16384]{1,0:T(8,128)(2,1)}, u32[]{:S(2)}) %copy-start) | copy-done | bytes 4194328
  58.2 3.1 %states_back.1 = f32[32,128]{1,0:T(8,128)} custom-call(s32[1]{0:T(128)} %bitcast.sect_ref, f32[32,128]{1,0:T(8,128)S(1)} %copy-done.4, bf16[128,128]{1,0:T(8,128)(2,1)S(1)} %copy-done.3, bf16[1024,128]{1,0:T(8,128)(2,1)S(1)} %copy-done.2, bf16[128,16384]{1,0:T(8,128)(2,1)S(1)} %copy-done), custom_call_target="tpu_custom_call" | custom-call | flops 134217728 | bytes 4194304 | tf_op jit(solution)/shard_map/states_back/pallas_call | solution.py:558
  61.3 23.6 %all-to-all-done.1.got_ref.mine_ref = bf16[64,136,128]{2,1,0:T(8,128)(2,1)S(1)} async-done(((bf16[64,136,128]{2,1,0:T(8,128)(2,1)}), bf16[64,136,128]{2,1,0:T(8,128)(2,1)S(1)}, u32[]{:S(2)}, u32[]{:S(2)}) %all-to-all-start.1) | async-done | bytes 2228256 | tf_op jit(solution)/shard_map/all_to_all | solution.py:570
  84.9 3.4 %collective-permute-start = (bf16[64,136,128]{2,1,0:T(8,128)(2,1)S(1)}, bf16[64,136,128]{2,1,0:T(8,128)(2,1)S(1)}, u32[]{:S(2)}, u32[]{:S(2)}) collective-permute-start(bf16[64,136,128]{2,1,0:T(8,128)(2,1)S(1)} %all-to-all-done.1.got_ref.mine_ref), channel_id=1, source_target_pairs={{0,32},{32,0},{1,33},{33,1},{2,34},{34,2},{3,35},{35,3},{4,36},{36... | collective-permute-start | bytes 6684680 | tf_op jit(solution)/shard_map/ppermute | solution.py:572
  88.3 3.2 %place_near.1.half_hbm = f32[128,16384]{1,0:T(8,128)} custom-call(s32[1]{0:T(128)} %bitcast.8.core_ref, bf16[64,136,128]{2,1,0:T(8,128)(2,1)S(1)} %all-to-all-done.1.got_ref.mine_ref), custom_call_target="tpu_custom_call" | custom-call | tf_op jit(solution)/shard_map/place_near/pallas_call | solution.py:575
  91.5 0.8 collective-permute-done.far_ref
  92.3 4.0 %place_far.1 = (f32[128,16384]{1,0:T(8,128)}, f32[128,128]{1,0:T(8,128)}, f32[128,384]{1,0:T(8,128)}, f32[128,384]{1,0:T(8,128)}, f32[16,128]{1,0:T(8,128)}, /*i...) custom-call(s32[1]{0:T(128)} %bitcast.8.core_ref, ...), custom_call_target="tpu_custom_call", output_to_operand_aliasing={{0}: (4, {})} | custom-call | tf_op jit(solution)/shard_map/place_far/pallas_call | solution.py:584
Async XLA Ops:
  47.4 1.4 %copy-start.1 = (bf16[64,136,128]{2,1,0:T(8,128)(2,1)}, bf16[64,136,128]{2,1,0:T(8,128)(2,1)S(1)}, u32[]{:S(2)}) copy-start(bf16[64,136,128]{2,1,0:T(8,128)(2,1)S(1)} %sum_parts.1) | copy-start | bytes 6684676
  48.8 7.3 %copy-start.2 = (bf16[1024,128]{1,0:T(8,128)(2,1)S(1)}, bf16[1024,128]{1,0:T(8,128)(2,1)}, u32[]{:S(2)}) copy-start(bf16[1024,128]{1,0:T(8,128)(2,1)} %get-tuple-element.29.pairs_ref) | copy-start | bytes 786436
  48.8 7.3 %copy-start.3 = (bf16[128,128]{1,0:T(8,128)(2,1)S(1)}, bf16[128,128]{1,0:T(8,128)(2,1)}, u32[]{:S(2)}) copy-start(bf16[128,128]{1,0:T(8,128)(2,1)} %get-tuple-element.28.grad_t_ref) | copy-start | bytes 98308
  48.8 7.3 %copy-start.4 = (f32[32,128]{1,0:T(8,128)S(1)}, f32[32,128]{1,0:T(8,128)}, u32[]{:S(2)}) copy-start(f32[32,128]{1,0:T(8,128)} %get-tuple-element.27.base_ref) | copy-start | bytes 49156
  48.8 36.1 %all-to-all-start.1 = ((bf16[64,136,128]{2,1,0:T(8,128)(2,1)}), bf16[64,136,128]{2,1,0:T(8,128)(2,1)S(1)}, u32[]{:S(2)}, u32[]{:S(2)}) async-start(bf16[64,136,128]{2,1,0:T(8,128)(2,1)} %copy-done.1), calls=%async_computation.1 | async-start | bytes 4456448 | tf_op jit(solution)/shard_map/all_to_all | solution.py:570
  56.0 2.2 %copy-start = (bf16[128,16384]{1,0:T(8,128)(2,1)S(1)}, bf16[128,16384]{1,0:T(8,128)(2,1)}, u32[]{:S(2)}) copy-start(bf16[128,16384]{1,0:T(8,128)(2,1)} %w_ref.1) | copy-start | bytes 12582916
  84.9 7.4 %collective-permute-start = (bf16[64,136,128]{2,1,0:T(8,128)(2,1)S(1)}, bf16[64,136,128]{2,1,0:T(8,128)(2,1)S(1)}, u32[]{:S(2)}, u32[]{:S(2)}) collective-permute-start(bf16[64,136,128]{2,1,0:T(8,128)(2,1)S(1)} %all-to-all-done.1.got_ref.mine_ref), channel_id=1, source_target_pairs={{0,32},{32,0},{1,33},{33,1},{2,34},{34,2},{3,35},{35,3},{4,36},{36... | collective-permute-start | bytes 6684680 | tf_op jit(solution)/shard_map/ppermute | solution.py:572

commit v2 on v1

--- a/solution.py
+++ b/solution.py
@@ -19,6 +19,9 @@
 ROWS = 136
 SMALL = 8
 GROUP = 32
+HALF = H // 2
+CUTS = (0, 16, 32, 48, 64)
+RUNS = 4
 BF = jnp.bfloat16
 F32 = jnp.float32
 
@@ -369,15 +372,20 @@
     pairs_out_ref[...] = pair_h[pl.ds(pl.multiple_of(sect * PAIRS, PAIRS), PAIRS), :]
 
 
-def sum_kernel(got_ref, out_ref):
+def sum_kernel(place_ref, got_ref, out_ref, two):
+    shift = place_ref[2]
+
     def body(at, total):
         return total + got_ref[at].astype(F32)
 
     total = lax.fori_loop(1, GROUP, body, got_ref[0].astype(F32), unroll=True)
-    piece = jnp.concatenate([total[:H].T, total[H:]], axis=0).astype(BF)
+    rows = total[:H].T
+    for part in range(2):
+        half_rows = rows[part * HALF : (part + 1) * HALF]
+        two[part] = jnp.concatenate([half_rows, total[H:]], axis=0).astype(BF)
 
     def put(at, carry):
-        out_ref[at] = piece
+        out_ref[at] = two[jnp.bitwise_and(jnp.right_shift(at, shift), 1)]
         return carry
 
     lax.fori_loop(0, 2 * GROUP, put, 0, unroll=8)
@@ -416,45 +424,68 @@
     out_ref[...] = lax.fori_loop(0, 32, back_body, base_ref[...], unroll=8)
 
 
-def place_kernel(count, core_ref, got_ref, out_hbm, stage, sems):
-    core = core_ref[0]
-    steps = [(half, row) for half in range(2) for row in range(8)]
-
-    def copy(at):
-        half, row = steps[at]
-        section = half * 2 + core
-        cols = pl.ds(pl.multiple_of(section * GROUP * H, GROUP * H), GROUP * H)
-        return pltpu.make_async_copy(
-            stage.at[at % 4], out_hbm.at[pl.ds(row * 16, 16), cols], sems.at[at % 4]
-        )
-
-    for at, (half, row) in enumerate(steps):
-        if at >= 4:
-            copy(at - 4).wait()
-        for dev in range(GROUP):
-            stage[at % 4, :, dev * H : (dev + 1) * H] = got_ref[
-                half * GROUP + dev, row * 16 : (row + 1) * 16, :
-            ].astype(F32)
-        copy(at).start()
-    for at in range(len(steps) - 4, len(steps)):
-        copy(at).wait()
-
-
-def first_kernel(core_ref, got_ref, out_hbm, stage, sems):
-    place_kernel(2, core_ref, got_ref, out_hbm, stage, sems)
-
-
-def second_kernel(
-    core_ref, other_ref, mine_ref, far_ref, half_hbm, out_hbm, gb_ref, gi_ref, gh_ref, ge_ref, be_ref, bi_ref, bh_ref, small, stage, sems
+def place_rows(place_ref, other_core, other_half, parts, out_hbm, stage, sem):
+    core = jnp.bitwise_xor(place_ref[3], 1) if other_core else place_ref[3]
+    copies = []
+    for run, (ref, first) in enumerate(parts):
+        bit = place_ref[run // 2]
+        if other_half:
+            bit = jnp.bitwise_xor(bit, 1)
+        low, high = CUTS[run], CUTS[run + 1]
+        half = low // GROUP
+        at_col = (half * 2 + core) * (GROUP * H) + (low - half * GROUP) * H
+        width = (high - low) * H
+        for part in range(2):
+            for dev in range(low, high):
+                for row in range(part * 32, part * 32 + 32, 16):
+                    stage[row : row + 16, dev * H : (dev + 1) * H] = ref[
+                        dev - first, row : row + 16, :
+                    ].astype(F32)
+            copies.append(
+                pltpu.make_async_copy(
+                    stage.at[pl.ds(part * 32, 32), pl.ds(low * H, width)],
+                    out_hbm.at[
+                        pl.ds(pl.multiple_of(bit * HALF + part * 32, 32), 32),
+                        pl.ds(pl.multiple_of(at_col, H), width),
+                    ],
+                    sem.at[len(copies)],
+                )
+            )
+            copies[-1].start()
+    for copy in copies:
+        copy.wait()
+
+
+def place_own(place_ref, near_ref, out_hbm, stage, sems):
+    place_rows(place_ref, False, False, [(near_ref, 0)] * RUNS, out_hbm, stage, sems)
+
+
+def place_core(
+    place_ref,
+    near_ref,
+    far_ref,
+    part_hbm,
+    out_hbm,
+    gb_ref,
+    gi_ref,
+    gh_ref,
+    ge_ref,
+    be_ref,
+    bi_ref,
+    bh_ref,
+    small,
+    stage,
+    sems,
 ):
-    del half_hbm
-    place_kernel(2, other_ref, far_ref, out_hbm, stage, sems)
-    for which, ref in ((core_ref[0], mine_ref), (other_ref[0], far_ref)):
+    del part_hbm
+    place_rows(place_ref, True, False, [(far_ref, 0)] * RUNS, out_hbm, stage, sems)
+    core = place_ref[3]
+    for which, ref in ((core, near_ref), (1 - core, far_ref)):
         for half in range(2):
             base = (half * 2 + which) * (GROUP * SMALL)
             for dev in range(GROUP):
                 at = pl.multiple_of(base + dev * SMALL, SMALL)
-                small[pl.ds(at, SMALL), :] = ref[half * GROUP + dev, H:ROWS, :].astype(F32)
+                small[pl.ds(at, SMALL), :] = ref[half * GROUP + dev, HALF:, :].astype(F32)
     misc = jnp.zeros((32, H), F32)
     for sect in range(MB):
         base = sect * GROUP * SMALL
@@ -470,6 +501,12 @@
     be_ref[...] = misc[16:17]
     bi_ref[...] = misc[17:20]
     bh_ref[...] = misc[20:23]
+
+
+def place_rest(other_core, place_ref, *refs):
+    out_hbm, stage, sems = refs[RUNS + 1 :]
+    parts = list(zip(refs[:RUNS], CUTS))
+    place_rows(place_ref, other_core, True, parts, out_hbm, stage, sems)
 
 
 VMEM_SPEC = pl.BlockSpec(memory_space=pltpu.VMEM)
@@ -510,6 +547,16 @@
     )(sect, *operands)
 
 
+def neighbours(axis, side):
+    pairs = []
+    for index in range(2 * GROUP):
+        spot = [index % 4, index // 4 % 4, index // 16]
+        step = 1 if spot[axis] % 2 == side else -1
+        spot[axis] = (spot[axis] + step) % 4
+        pairs.append((index, spot[2] * 16 + spot[1] * 4 + spot[0]))
+    return pairs
+
+
 def local(
     node_states,
     edge_features,
@@ -529,8 +576,9 @@
     core = lax.axis_index("core").astype(jnp.int32)
     sect = (lax.axis_index("zh") * 2 + core).astype(jnp.int32)
     sect = sect.reshape(1)
-    mine = core.reshape(1)
-    other = 1 - mine
+    dp = lax.axis_index("dp").astype(jnp.int32)
+    zh = lax.axis_index("zh").astype(jnp.int32)
+    place = jnp.stack([dp & 1, (dp >> 2) & 1, zh * 2, core])
     operands = [v.reshape(8, 128) for v in (edge_source, edge_target, edge_live)] + [
         edge_features,
         w_edge_in,
@@ -546,15 +594,6 @@
     ]
 
     send, final, base, grad_t, pairs = run_layers(sect, operands)
-    got = lax.all_to_all(send, "dp", split_axis=0, concat_axis=0)
-    piece = pl.pallas_call(
-        sum_kernel,
-        out_shape=shape((2 * GROUP, ROWS, H), BF),
-        in_specs=[VMEM_SPEC],
-        out_specs=VMEM_SPEC,
-        compiler_params=pltpu.CompilerParams(vmem_limit_bytes=LOW),
-        name="sum_parts",
-    )(got)
     grad_states = pl.pallas_call(
         states_kernel,
         out_shape=shape((ATOMS, H), F32),
@@ -567,39 +606,76 @@
         ),
         name="states_back",
     )(sect, base, grad_t, pairs, w_edge_out)
+    got = lax.all_to_all(send, "dp", split_axis=0, concat_axis=0)
+    got, grad_states = lax.optimization_barrier((got, grad_states))
+    piece = pl.pallas_call(
+        sum_kernel,
+        out_shape=shape((2 * GROUP, HALF + SMALL, H), BF),
+        in_specs=[SMEM_SPEC, VMEM_SPEC],
+        out_specs=VMEM_SPEC,
+        scratch_shapes=[pltpu.VMEM((2, HALF + SMALL, H), BF)],
+        compiler_params=pltpu.CompilerParams(vmem_limit_bytes=LOW),
+        name="sum_parts",
+    )(place, got)
     near = lax.all_to_all(piece, ("zh", "dp"), split_axis=0, concat_axis=0)
-    near, grad_states = lax.optimization_barrier((near, grad_states))
     far = lax.ppermute(near, "core", [(0, 1), (1, 0)])
-
-    stage = [pltpu.VMEM((4, 16, GROUP * H), F32), pltpu.SemaphoreType.DMA((4,))]
-    half = pl.pallas_call(
-        first_kernel,
-        out_shape=shape((H, H * H), F32),
+    rest = [
+        lax.ppermute(
+            near[CUTS[run] : CUTS[run + 1], :HALF], ("zh", "dp"), neighbours(run // 2, run % 2)
+        )
+        for run in range(RUNS)
+    ]
+    stage = [pltpu.VMEM((HALF, 2 * GROUP * H), F32), pltpu.SemaphoreType.DMA((2 * RUNS,))]
+    params = pltpu.CompilerParams(vmem_limit_bytes=LOW)
+    cost = pl.CostEstimate(flops=0, bytes_accessed=6 * 2**20, transcendentals=0)
+    whole = shape((H, H * H), F32)
+    out = pl.pallas_call(
+        place_own,
+        out_shape=whole,
         in_specs=[SMEM_SPEC, VMEM_SPEC],
         out_specs=ANY_SPEC,
         scratch_shapes=stage,
-        compiler_params=pltpu.CompilerParams(vmem_limit_bytes=LOW),
-        name="place_near",
-    )(mine, near)
-    grad_w_out, grad_b_out, grad_w_in, grad_w_hid, grad_ein, grad_bein, grad_bin, grad_bhid = pl.pallas_call(
-        second_kernel,
-        out_shape=(
-            shape((H, H * H), F32),
-            shape((H, H), F32),
-            shape((H, 3 * H), F32),
-            shape((H, 3 * H), F32),
-            shape((16, H), F32),
-            shape((1, H), F32),
-            shape((3, H), F32),
-            shape((3, H), F32),
-        ),
-        in_specs=[SMEM_SPEC, SMEM_SPEC, VMEM_SPEC, VMEM_SPEC, ANY_SPEC],
-        out_specs=(ANY_SPEC,) + (VMEM_SPEC,) * 7,
-        scratch_shapes=[pltpu.VMEM((MB * GROUP * SMALL, H), F32)] + stage,
-        input_output_aliases={4: 0},
-        compiler_params=pltpu.CompilerParams(vmem_limit_bytes=LOW),
-        name="place_far",
-    )(mine, other, near, far, half)
+        compiler_params=params,
+        cost_estimate=cost,
+        name="place_own",
+    )(place, near)
+    out, grad_b_out, grad_w_in, grad_w_hid, grad_ein, grad_bein, grad_bin, grad_bhid = (
+        pl.pallas_call(
+            place_core,
+            out_shape=(
+                whole,
+                shape((H, H), F32),
+                shape((H, 3 * H), F32),
+                shape((H, 3 * H), F32),
+                shape((16, H), F32),
+                shape((1, H), F32),
+                shape((3, H), F32),
+                shape((3, H), F32),
+            ),
+            in_specs=[SMEM_SPEC, VMEM_SPEC, VMEM_SPEC, ANY_SPEC],
+            out_specs=(ANY_SPEC,) + (VMEM_SPEC,) * 7,
+            scratch_shapes=[pltpu.VMEM((MB * GROUP * SMALL, H), F32)] + stage,
+            input_output_aliases={3: 0},
+            compiler_params=params,
+            cost_estimate=cost,
+            name="place_core",
+        )(place, near, far, out)
+    )
+    rest, out = lax.optimization_barrier((rest, out))
+    far_rest = [lax.ppermute(part, "core", [(0, 1), (1, 0)]) for part in rest]
+    for other_core, parts in ((False, rest), (True, far_rest)):
+        out = pl.pallas_call(
+            functools.partial(place_rest, other_core),
+            out_shape=whole,
+            in_specs=[SMEM_SPEC] + [VMEM_SPEC] * RUNS + [ANY_SPEC],
+            out_specs=ANY_SPEC,
+            scratch_shapes=stage,
+            input_output_aliases={RUNS + 1: 0},
+            compiler_params=params,
+            cost_estimate=cost,
+            name="place_rest",
+        )(place, *parts, out)
+    grad_w_out = out
     return (
         final,
         grad_states,

time: 96.6 us -> 92.1 us (0.953)
  waiting for transfers between devices: 24.4 us -> 13.9 us
  starting transfers between devices: 10.7 us -> 16.8 us
  Pallas kernels: 30.3 us -> 32.2 us
  local copies, waits for them, and re-layouts: 3.55 us -> 2.32 us
  blocking collectives: 26.7 us -> 25.6 us
    all_to_all x1, waiting for transfers between devices: 23.6 us -> 10.8 us  [local(): got = lax.all_to_all(send, 'dp', split_axis=0, concat_axis=0)]
    ppermute x0 -> x8, starting transfers between devices: none -> 4 us  [the longest x4 2.06 us: local(): lax.ppermute(near[CUTS[run]:CUTS[run + 1], :HALF], ('zh', 'dp'), neighbou...]
    ppermute x0 -> x8, waiting for transfers between devices: none -> 3.11 us  [the longest x4 3.1 us: local(): lax.ppermute(near[CUTS[run]:CUTS[run + 1], :HALF], ('zh', 'dp'), neighbou...]
    all_to_all x1, starting transfers between devices: 7.24 us -> 9.36 us  [local(): got = lax.all_to_all(send, 'dp', split_axis=0, concat_axis=0)]
    pallas_call x3 -> x5, Pallas kernels: 7.55 us -> 9.46 us  [the longest x2 3.87 us: local(): pl.pallas_call(functools.partial(place_rest, other_core), out_shape=whole...]
    unnamed x10 -> x8, local copies, waits for them, and re-layouts: 3.55 us -> 2.2 us
    all_to_all x1, blocking collectives: 26.7 us -> 25.6 us  [local(): near = lax.all_to_all(piece, ('zh', 'dp'), split_axis=0, concat_axis=0)]
  transfers between devices with their start and end apart: 2 -> 10, of which waited for: 2 -> 4; matrix products, arithmetic and copies ran while one was open for 0% -> 0% of each run, Pallas kernels for 6% -> 11%
where the time goes in v2:
time: 92.1 us; the launch traced here: 91.8 us
  Pallas kernels  32.2 us (35%)
  blocking collectives  25.6 us (28%)
  starting transfers between devices  16.8 us (18%)
  waiting for transfers between devices  13.9 us (15%)
  local copies, waits for them, and re-layouts  2.32 us (3%)
  between operations  0.98 us (1%)
    all_to_all x1, blocking collectives, local(): near = lax.all_to_all(piece, ('zh', 'dp'), split_axis=0, concat_axis=0)  25.6 us
    pallas_call x1, Pallas kernels, run_layers(): pl.pallas_call(local_kernel, out_shape=(shape((GROUP, ROWS, H), BF), shap...  19.7 us
    all_to_all x1, waiting for transfers between devices, local(): got = lax.all_to_all(send, 'dp', split_axis=0, concat_axis=0)  10.8 us
    all_to_all x1, starting transfers between devices, local(): got = lax.all_to_all(send, 'dp', split_axis=0, concat_axis=0)  9.36 us
    pallas_call x2, Pallas kernels, local(): pl.pallas_call(functools.partial(place_rest, other_core), out_shape=whole...  3.87 us
    ppermute x1, starting transfers between devices, local(): far = lax.ppermute(near, 'core', [(0, 1), (1, 0)])  3.41 us
    ppermute x4, waiting for transfers between devices, local(): lax.ppermute(near[CUTS[run]:CUTS[run + 1], :HALF], ('zh', 'dp'), neighbou...  3.1 us
    pallas_call x1, Pallas kernels, local(): pl.pallas_call(states_kernel, out_shape=shape((ATOMS, H), F32), in_specs=...  3.06 us
  transfers between devices with their start and end apart: 10, of which 4 were waited for; matrix products, arithmetic and copies ran while one was open for 0% of the time, Pallas kernels for 11%

profile of v2, /device:TPU:1, one launch (start us, length us, event | category | flops | bytes accessed | tf_op | source)
XLA Modules:
  0.0 91.8 jit_solution(169405264240747608)
XLA Ops:
  0.7 19.7 %layers.1 = (bf16[32,136,128]{2,1,0:T(8,128)(2,1)}, f32[32,128]{1,0:T(8,128)}, f32[32,128]{1,0:T(8,128)}, bf16[128,128]{1,0:T(8,128)(2,1)}, bf16[1024,128]{1,0:T(8,128)(2,1)}) custom-call(s32[1]{0:T(128)} %bitcast.sect_ref, s32[8,128]{1,0:T(8,128)} %bitcast.17, s32[8,128]{1,0:T(8,128)} %bitcast.18, s32[8,128]{1,0:T(8,128)} %bitcast.19, ...), custom_call_target="tpu_custom_call" | custom-call | tf_op jit(solution)/shard_map/layers/pallas_call | solution.py:521
  20.3 0.0 copy-start.2
  20.3 0.0 copy-start.3
  20.4 9.4 %all-to-all-start = ((bf16[32,136,128]{2,1,0:T(8,128)(2,1)}), bf16[32,136,128]{2,1,0:T(8,128)(2,1)S(1)}, u32[]{:S(2)}, u32[]{:S(2)}) async-start(bf16[32,136,128]{2,1,0:T(8,128)(2,1)} %get-tuple-element.31), calls=%async_computation | async-start | bytes 2228224 | tf_op jit(solution)/shard_map/all_to_all | solution.py:609
  29.8 0.0 copy-start
  29.8 2.2 %copy-done = bf16[128,16384]{1,0:T(8,128)(2,1)S(1)} copy-done((bf16[128,16384]{1,0:T(8,128)(2,1)S(1)}, bf16[128,16384]{1,0:T(8,128)(2,1)}, u32[]{:S(2)}) %copy-start) | copy-done | bytes 4194328
  32.0 3.1 %states_back.1 = f32[32,128]{1,0:T(8,128)} custom-call(s32[1]{0:T(128)} %bitcast.sect_ref, f32[32,128]{1,0:T(8,128)S(1)} %copy-done.3, bf16[128,128]{1,0:T(8,128)(2,1)S(1)} %copy-done.2, bf16[1024,128]{1,0:T(8,128)(2,1)S(1)} %copy-done.1, bf16[128,16384]{1,0:T(8,128)(2,1)S(1)} %copy-done), custom_call_target="tpu_custom_call" | custom-call | flops 134217728 | bytes 4194304 | tf_op jit(solution)/shard_map/states_back/pallas_call | solution.py:597
  35.0 0.1 pad_add_fusion.place_ref
  35.1 10.8 %all-to-all-done.got_ref = bf16[32,136,128]{2,1,0:T(8,128)(2,1)S(1)} async-done(((bf16[32,136,128]{2,1,0:T(8,128)(2,1)}), bf16[32,136,128]{2,1,0:T(8,128)(2,1)S(1)}, u32[]{:S(2)}, u32[]{:S(2)}) %all-to-all-start) | async-done | bytes 1114144 | tf_op jit(solution)/shard_map/all_to_all | solution.py:609
  45.9 0.9 sum_parts.1
  46.8 25.6 %all_to_all.10.near_ref = bf16[64,72,128]{2,1,0:T(8,128)(2,1)S(1)} all-to-all(bf16[64,72,128]{2,1,0:T(8,128)(2,1)S(1)} %sum_parts.1), channel_id=1, replica_groups=mesh['zh'=2,'core'=2,'dp'=32] {'zh','dp'}, dimensions={0} | all-to-all | bytes 2359296 | tf_op jit(solution)/shard_map/all_to_all | solution.py:620
  72.4 3.4 %collective-permute-start = (bf16[64,72,128]{2,1,0:T(8,128)(2,1)S(1)}, bf16[64,72,128]{2,1,0:T(8,128)(2,1)S(1)}, u32[]{:S(2)}, u32[]{:S(2)}) collective-permute-start(bf16[64,72,128]{2,1,0:T(8,128)(2,1)S(1)} %all_to_all.10.near_ref), channel_id=1, source_target_pairs={{0,32},{32,0},{1,33},{33,1},{2,34},{34,2},{3,35},{35,3},{4,36},{36... | collective-permute-start | bytes 3538952 | tf_op jit(solution)/shard_map/ppermute | solution.py:621
  75.8 0.1 fusion
  75.9 0.4 collective-permute-start.1
  76.3 1.0 %collective-permute-start.2 = (bf16[16,64,128]{2,1,0:T(8,128)(2,1)S(1)}, bf16[16,64,128]{2,1,0:T(8,128)(2,1)S(1)}, u32[]{:S(2)}, u32[]{:S(2)}) collective-permute-start(bf16[16,64,128]{2,1,0:T(8,128)(2,1)S(1)} %get-tuple-element.52), channel_id=1, source_target_pairs={{0,3},{1,2},{2,1},{3,0},{4,7},{5,6},{6,5},{7,4},{8,11},{9,10},{10,... | collective-permute-start | bytes 786440 | tf_op jit(solution)/shard_map/ppermute | solution.py:623
  77.3 0.0 collective-permute-start.3
  77.3 0.7 collective-permute-start.4
  78.0 1.9 %place_own.1.part_hbm = f32[128,16384]{1,0:T(8,128)} custom-call(s32[4]{0:T(128)S(1)} %pad_add_fusion.place_ref, bf16[64,72,128]{2,1,0:T(8,128)(2,1)S(1)} %all_to_all.10.near_ref), custom_call_target="tpu_custom_call" | custom-call | bytes 6291456 | tf_op jit(solution)/shard_map/place_own/pallas_call | solution.py:632
  79.9 2.8 %place_core.1 = (f32[128,16384]{1,0:T(8,128)}, f32[128,128]{1,0:T(8,128)}, f32[128,384]{1,0:T(8,128)}, f32[128,384]{1,0:T(8,128)}, f32[16,128]{1,0:T(8,128)}, /*...) custom-call(s32[4]{0:T(128)S(1)} %pad_add_fusion.place_ref, ...), custom_call_target="tpu_custom_call", output_to_operand_aliasing={{0}: (3, {})} | custom-call | bytes 6291456 | tf_op jit(solution)/shard_map/place_core/pallas_call | solution.py:643
  82.7 1.2 %collective-permute-done.1.refs_0_ = bf16[16,64,128]{2,1,0:T(8,128)(2,1)S(1)} collective-permute-done((bf16[16,64,128]{2,1,0:T(8,128)(2,1)S(1)}, bf16[16,64,128]{2,1,0:T(8,128)(2,1)S(1)}, u32[]{:S(2)}, u32[]{:S(2)}) %collective-permute-start.1) | collective-permute-done | bytes 262176 | tf_op jit(solution)/shard_map/ppermute | solution.py:623
  83.9 1.2 %collective-permute-done.2.refs_1_ = bf16[16,64,128]{2,1,0:T(8,128)(2,1)S(1)} collective-permute-done((bf16[16,64,128]{2,1,0:T(8,128)(2,1)S(1)}, bf16[16,64,128]{2,1,0:T(8,128)(2,1)S(1)}, u32[]{:S(2)}, u32[]{:S(2)}) %collective-permute-start.2) | collective-permute-done | bytes 262176 | tf_op jit(solution)/shard_map/ppermute | solution.py:623
  85.1 0.0 collective-permute-done.3.refs_2_
  85.1 0.7 collective-permute-done.4.refs_3_
  85.8 1.4 %collective-permute-start.5 = (bf16[16,64,128]{2,1,0:T(8,128)(2,1)S(1)}, bf16[16,64,128]{2,1,0:T(8,128)(2,1)S(1)}, u32[]{:S(2)}, u32[]{:S(2)}) collective-permute-start(bf16[16,64,128]{2,1,0:T(8,128)(2,1)S(1)} %collective-permute-done.1.refs_0_), channel_id=1, source_target_pairs={{0,32},{32,0},{1,33},{33,1},{2,34},{34,2},{3,35},{35,3},{4,36},{36... | collective-permute-start | bytes 786440 | tf_op jit(solution)/shard_map/ppermute | solution.py:665
  87.2 0.0 collective-permute-start.6
  87.2 0.5 collective-permute-start.7
  87.7 0.0 collective-permute-start.8
  87.7 1.9 %place_rest.2.refs_4_ = f32[128,16384]{1,0:T(8,128)} custom-call(s32[4]{0:T(128)S(1)} %pad_add_fusion.place_ref, bf16[16,64,128]{2,1,0:T(8,128)(2,1)S(1)} %collective-permute-done.1.refs_0_, bf16[16,64,128]{2,1,0:T(8,128)(2,1)S(1)} %collective-permute-done.2.refs_1_, ...), custom_call_target="tpu_custom_call", output_to_operand_aliasing={{}: (5, {})} | custom-call | bytes 6291456 | tf_op jit(solution)/shard_map/place_rest/pallas_call | solution.py:667
  89.7 0.0 collective-permute-done.5.refs_0_
  89.7 0.0 collective-permute-done.6.refs_1_
  89.7 0.0 collective-permute-done.8.refs_3_
  89.7 1.9 %place_rest.3 = f32[128,16384]{1,0:T(8,128)} custom-call(s32[4]{0:T(128)S(1)} %pad_add_fusion.place_ref, bf16[16,64,128]{2,1,0:T(8,128)(2,1)S(1)} %collective-permute-done.5.refs_0_, bf16[16,64,128]{2,1,0:T(8,128)(2,1)S(1)} %collective-permute-done.6.refs_1_, ...), custom_call_target="tpu_custom_call", output_to_operand_aliasing={{}: (5, {})} | custom-call | bytes 6291456 | tf_op jit(solution)/shard_map/place_rest/pallas_call | solution.py:667
  (6 shorter events, 0.0 us)
Async XLA Ops:
  20.3 9.4 %copy-start.1 = (bf16[1024,128]{1,0:T(8,128)(2,1)S(1)}, bf16[1024,128]{1,0:T(8,128)(2,1)}, u32[]{:S(2)}) copy-start(bf16[1024,128]{1,0:T(8,128)(2,1)} %get-tuple-element.34.pairs_ref) | copy-start | bytes 786436
  20.3 9.4 %copy-start.2 = (bf16[128,128]{1,0:T(8,128)(2,1)S(1)}, bf16[128,128]{1,0:T(8,128)(2,1)}, u32[]{:S(2)}) copy-start(bf16[128,128]{1,0:T(8,128)(2,1)} %get-tuple-element.33.grad_t_ref) | copy-start | bytes 98308
  20.3 9.4 %copy-start.3 = (f32[32,128]{1,0:T(8,128)S(1)}, f32[32,128]{1,0:T(8,128)}, u32[]{:S(2)}) copy-start(f32[32,128]{1,0:T(8,128)} %get-tuple-element.32.base_ref) | copy-start | bytes 49156
  20.4 25.6 %all-to-all-start = ((bf16[32,136,128]{2,1,0:T(8,128)(2,1)}), bf16[32,136,128]{2,1,0:T(8,128)(2,1)S(1)}, u32[]{:S(2)}, u32[]{:S(2)}) async-start(bf16[32,136,128]{2,1,0:T(8,128)(2,1)} %get-tuple-element.31), calls=%async_computation | async-start | bytes 2228224 | tf_op jit(solution)/shard_map/all_to_all | solution.py:609
  29.8 2.2 %copy-start = (bf16[128,16384]{1,0:T(8,128)(2,1)S(1)}, bf16[128,16384]{1,0:T(8,128)(2,1)}, u32[]{:S(2)}) copy-start(bf16[128,16384]{1,0:T(8,128)(2,1)} %w_ref.1) | copy-start | bytes 12582916
  72.4 7.6 %collective-permute-start = (bf16[64,72,128]{2,1,0:T(8,128)(2,1)S(1)}, bf16[64,72,128]{2,1,0:T(8,128)(2,1)S(1)}, u32[]{:S(2)}, u32[]{:S(2)}) collective-permute-start(bf16[64,72,128]{2,1,0:T(8,128)(2,1)S(1)} %all_to_all.10.near_ref), channel_id=1, source_target_pairs={{0,32},{32,0},{1,33},{33,1},{2,34},{34,2},{3,35},{35,3},{4,36},{36... | collective-permute-start | bytes 3538952 | tf_op jit(solution)/shard_map/ppermute | solution.py:621
  75.9 8.0 %collective-permute-start.1 = (bf16[16,64,128]{2,1,0:T(8,128)(2,1)S(1)}, bf16[16,64,128]{2,1,0:T(8,128)(2,1)S(1)}, u32[]{:S(2)}, u32[]{:S(2)}) collective-permute-start(bf16[16,64,128]{2,1,0:T(8,128)(2,1)S(1)} %get-tuple-element.53), channel_id=1, source_target_pairs={{0,1},{1,0},{2,3},{3,2},{4,5},{5,4},{6,7},{7,6},{8,9},{9,8},{10,11... | collective-permute-start | bytes 786440 | tf_op jit(solution)/shard_map/ppermute | solution.py:623
  76.3 8.8 %collective-permute-start.2 = (bf16[16,64,128]{2,1,0:T(8,128)(2,1)S(1)}, bf16[16,64,128]{2,1,0:T(8,128)(2,1)S(1)}, u32[]{:S(2)}, u32[]{:S(2)}) collective-permute-start(bf16[16,64,128]{2,1,0:T(8,128)(2,1)S(1)} %get-tuple-element.52), channel_id=1, source_target_pairs={{0,3},{1,2},{2,1},{3,0},{4,7},{5,6},{6,5},{7,4},{8,11},{9,10},{10,... | collective-permute-start | bytes 786440 | tf_op jit(solution)/shard_map/ppermute | solution.py:623
  77.3 7.8 %collective-permute-start.3 = (bf16[16,64,128]{2,1,0:T(8,128)(2,1)S(1)}, bf16[16,64,128]{2,1,0:T(8,128)(2,1)S(1)}, u32[]{:S(2)}, u32[]{:S(2)}) collective-permute-start(bf16[16,64,128]{2,1,0:T(8,128)(2,1)S(1)} %get-tuple-element.51), channel_id=1, source_target_pairs={{0,4},{1,5},{2,6},{3,7},{4,0},{5,1},{6,2},{7,3},{8,12},{9,13},{10,... | collective-permute-start | bytes 786440 | tf_op jit(solution)/shard_map/ppermute | solution.py:623
  77.3 8.5 %collective-permute-start.4 = (bf16[16,64,128]{2,1,0:T(8,128)(2,1)S(1)}, bf16[16,64,128]{2,1,0:T(8,128)(2,1)S(1)}, u32[]{:S(2)}, u32[]{:S(2)}) collective-permute-start(bf16[16,64,128]{2,1,0:T(8,128)(2,1)S(1)} %get-tuple-element.50), channel_id=1, source_target_pairs={{0,12},{1,13},{2,14},{3,15},{4,8},{5,9},{6,10},{7,11},{8,4},{9,5},... | collective-permute-start | bytes 786440 | tf_op jit(solution)/shard_map/ppermute | solution.py:623
  85.8 3.9 %collective-permute-start.5 = (bf16[16,64,128]{2,1,0:T(8,128)(2,1)S(1)}, bf16[16,64,128]{2,1,0:T(8,128)(2,1)S(1)}, u32[]{:S(2)}, u32[]{:S(2)}) collective-permute-start(bf16[16,64,128]{2,1,0:T(8,128)(2,1)S(1)} %collective-permute-done.1.refs_0_), channel_id=1, source_target_pairs={{0,32},{32,0},{1,33},{33,1},{2,34},{34,2},{3,35},{35,3},{4,36},{36... | collective-permute-start | bytes 786440 | tf_op jit(solution)/shard_map/ppermute | solution.py:665
  87.2 2.5 %collective-permute-start.6 = (bf16[16,64,128]{2,1,0:T(8,128)(2,1)S(1)}, bf16[16,64,128]{2,1,0:T(8,128)(2,1)S(1)}, u32[]{:S(2)}, u32[]{:S(2)}) collective-permute-start(bf16[16,64,128]{2,1,0:T(8,128)(2,1)S(1)} %collective-permute-done.2.refs_1_), channel_id=1, source_target_pairs={{0,32},{32,0},{1,33},{33,1},{2,34},{34,2},{3,35},{35,3},{4,36},{36... | collective-permute-start | bytes 786440 | tf_op jit(solution)/shard_map/ppermute | solution.py:665
  87.2 2.5 %collective-permute-start.7 = (bf16[16,64,128]{2,1,0:T(8,128)(2,1)S(1)}, bf16[16,64,128]{2,1,0:T(8,128)(2,1)S(1)}, u32[]{:S(2)}, u32[]{:S(2)}) collective-permute-start(bf16[16,64,128]{2,1,0:T(8,128)(2,1)S(1)} %collective-permute-done.3.refs_2_), channel_id=1, source_target_pairs={{0,32},{32,0},{1,33},{33,1},{2,34},{34,2},{3,35},{35,3},{4,36},{36... | collective-permute-start | bytes 786440 | tf_op jit(solution)/shard_map/ppermute | solution.py:665
  87.7 2.0 %collective-permute-start.8 = (bf16[16,64,128]{2,1,0:T(8,128)(2,1)S(1)}, bf16[16,64,128]{2,1,0:T(8,128)(2,1)S(1)}, u32[]{:S(2)}, u32[]{:S(2)}) collective-permute-start(bf16[16,64,128]{2,1,0:T(8,128)(2,1)S(1)} %collective-permute-done.4.refs_3_), channel_id=1, source_target_pairs={{0,32},{32,0},{1,33},{33,1},{2,34},{34,2},{3,35},{35,3},{4,36},{36... | collective-permute-start | bytes 786440 | tf_op jit(solution)/shard_map/ppermute | solution.py:665

commit v3 on v2

--- a/solution.py
+++ b/solution.py
@@ -22,6 +22,7 @@
 HALF = H // 2
 CUTS = (0, 16, 32, 48, 64)
 RUNS = 4
+W_PARTS = 1
 BF = jnp.bfloat16
 F32 = jnp.float32
 
@@ -112,7 +113,7 @@
         w_ref,
     ) = held
     sect = sect_ref[0]
-    chunk = 2048
+    chunk = H * H // W_PARTS
     copies = [
         pltpu.make_async_copy(ins[at], held[at], sems.at[at]) for at in range(13)
     ]
@@ -123,7 +124,7 @@
 
     for copy in copies:
         copy.start()
-    for at in range(8):
+    for at in range(W_PARTS):
         w_copy(at).start()
     for copy in copies:
         copy.wait()
@@ -138,17 +139,20 @@
     pair = jnp.where(live > 0, source * ATOMS + target, -1)
 
     slot = lax.broadcasted_iota(jnp.int32, (PAIRS, H), 0)
-    for mol in range(MB):
+
+    def hot_pairs(first, second):
+        return jnp.concatenate(
+            [jnp.where(slot == row, 1.0, 0.0).astype(BF) for row in (first, second)], axis=1
+        )
+
+    def pair_rows(mol):
         pre = edge_front(feat_ref[:, mol * EPM : (mol + 1) * EPM], w_ein, b_ein)
         hidden = (pre * sigmoid(pre)).astype(BF)
-        hot = jnp.concatenate(
-            [
-                jnp.where(slot == pair[2 * mol + part : 2 * mol + part + 1, :], 1.0, 0.0).astype(BF)
-                for part in range(2)
-            ],
-            axis=1,
-        )
+        hot = hot_pairs(pair[2 * mol : 2 * mol + 1, :], pair[2 * mol + 1 : 2 * mol + 2, :])
         pair_h[mol * PAIRS : (mol + 1) * PAIRS, :] = nn(hot, hidden).astype(BF)
+
+    for mol in range(MB):
+        pair_rows(mol)
 
     node = lax.broadcasted_iota(jnp.int32, (NODES, H), 0)
     hot_t, hot_s = [], []
@@ -173,17 +177,17 @@
                 u_ref[pl.ds(at * 4 + q, NODES, stride=GAP), :] = out[:, q * H : (q + 1) * H]
 
         if wait:
-            for at in range(8):
+            for at in range(W_PARTS):
                 w_copy(at).wait()
-                for inner in range(4):
-                    step(at * 4 + inner)
+            for at in range(32):
+                step(at)
         else:
 
             def body(at, carry):
                 step(at)
                 return carry
 
-            lax.fori_loop(0, 32, body, 0, unroll=8)
+            lax.fori_loop(0, 32, body, 0, unroll=True)
 
     def u_rows(u_ref, at):
         return u_ref[pl.ds(at * GAP, H), :].astype(BF)
@@ -255,7 +259,7 @@
         right = jnp.concatenate([w_ref[:, pl.ds(base + q * H, H)] for q in range(4)], axis=0)
         return total + nn(left, right)
 
-    back_msg = lax.fori_loop(0, 32, back_body, jnp.zeros((NODES, H), F32), unroll=8)
+    back_msg = lax.fori_loop(0, 32, back_body, jnp.zeros((NODES, H), F32), unroll=True)
     share = nn(adj_t, g_two)
     grad_one = back_one + back_msg + fine(nn, share, b_mat)
 
@@ -288,15 +292,23 @@
     def own_body(at, carry):
         right = jnp.concatenate(
             [
-                d_own[pl.ds(at * GAP, NODES), :].astype(BF),
-                d_all[pl.ds((sect * OWN + at) * GAP, NODES), :].astype(BF),
+                jnp.concatenate(
+                    [
+                        d_own[pl.ds((at * 2 + q) * GAP, NODES), :].astype(BF),
+                        d_all[pl.ds((sect * OWN + at * 2 + q) * GAP, NODES), :].astype(BF),
+                    ],
+                    axis=0,
+                )
+                for q in range(2)
             ],
-            axis=0,
+            axis=1,
         )
-        send_ref[at, 0:H, :] = nn(both_t, right).astype(BF)
+        out = nn(both_t, right).astype(BF)
+        for q in range(2):
+            send_ref[at * 2 + q, 0:H, :] = out[:, q * H : (q + 1) * H]
         return carry
 
-    lax.fori_loop(0, OWN, own_body, 0, unroll=8)
+    lax.fori_loop(0, OWN // 2, own_body, 0, unroll=True)
 
     rows_scr[...] = g_one.astype(F32)
     g1 = rows_scr[own_rows, :].astype(BF)
@@ -320,7 +332,7 @@
             ]
         return carry
 
-    lax.fori_loop(0, 16, q_body, 0, unroll=8)
+    lax.fori_loop(0, 16, q_body, 0, unroll=True)
     own_cols = pl.ds(pl.multiple_of(sect * EPM, EPM), EPM)
     feat_own = feat_ref[:, own_cols]
     pre_own = edge_front(feat_own, w_ein, b_ein)
@@ -328,10 +340,7 @@
     slope = sig * (1.0 + pre_own * (1.0 - sig))
     rows_scr[0:8, :] = pair.astype(F32)
     pair_own = rows_scr[pl.ds(sect * 2, 2), :].astype(jnp.int32)
-    hot = jnp.concatenate(
-        [jnp.where(slot == pair_own[part : part + 1, :], 1.0, 0.0).astype(BF) for part in range(2)],
-        axis=1,
-    )
+    hot = hot_pairs(pair_own[0:1, :], pair_own[1:2, :])
     g_pre = tn(hot, q_scr[...]) * slope
 
     g_share_t = nn(g_one_t, adj), nn(g_two_t, adj)
@@ -421,7 +430,7 @@
         right = jnp.concatenate([w_ref[:, pl.ds(base + q * H, H)] for q in range(4)], axis=0)
         return total + nn(left, right)
 
-    out_ref[...] = lax.fori_loop(0, 32, back_body, base_ref[...], unroll=8)
+    out_ref[...] = lax.fori_loop(0, 32, back_body, base_ref[...], unroll=True)
 
 
 def place_rows(place_ref, other_core, other_half, parts, out_hbm, stage, sem):
@@ -540,7 +549,7 @@
             pltpu.VMEM((GROUP * SMALL, H), F32),
             pltpu.VMEM((PAIRS, H), BF),
             pltpu.SemaphoreType.DMA((13,)),
-            pltpu.SemaphoreType.DMA((8,)),
+            pltpu.SemaphoreType.DMA((W_PARTS,)),
         ],
         compiler_params=pltpu.CompilerParams(vmem_limit_bytes=BIG),
         name="layers",

time: 92.1 us -> 86.7 us (0.941)
  Pallas kernels: 32.2 us -> 25.5 us
  waiting for transfers between devices: 13.9 us -> 15.2 us
    pallas_call x1, Pallas kernels: 19.7 us -> 14.2 us  [run_layers(): pl.pallas_call(local_kernel, out_shape=(shape((GROUP, ROWS, H), BF), shap...]
    all_to_all x1, waiting for transfers between devices: 10.8 us -> 12.1 us  [local(): got = lax.all_to_all(send, 'dp', split_axis=0, concat_axis=0)]
    pallas_call x1, Pallas kernels: 3.06 us -> 1.83 us  [local(): pl.pallas_call(states_kernel, out_shape=shape((ATOMS, H), F32), in_specs=...]
  transfers between devices with their start and end apart: 10 -> 10, of which waited for: 4 -> 4; matrix products, arithmetic and copies ran while one was open for 0% -> 0% of each run, Pallas kernels for 11% -> 10%
where the time goes in v3:
time: 86.7 us; the launch traced here: 86.4 us
  blocking collectives  25.6 us (30%)
  Pallas kernels  25.5 us (29%)
  starting transfers between devices  16.8 us (19%)
  waiting for transfers between devices  15.2 us (18%)
  local copies, waits for them, and re-layouts  2.32 us (3%)
  between operations  0.98 us (1%)
    all_to_all x1, blocking collectives, local(): near = lax.all_to_all(piece, ('zh', 'dp'), split_axis=0, concat_axis=0)  25.6 us
    pallas_call x1, Pallas kernels, run_layers(): pl.pallas_call(local_kernel, out_shape=(shape((GROUP, ROWS, H), BF), shap...  14.2 us
    all_to_all x1, waiting for transfers between devices, local(): got = lax.all_to_all(send, 'dp', split_axis=0, concat_axis=0)  12.1 us
    all_to_all x1, starting transfers between devices, local(): got = lax.all_to_all(send, 'dp', split_axis=0, concat_axis=0)  9.36 us
    pallas_call x2, Pallas kernels, local(): pl.pallas_call(functools.partial(place_rest, other_core), out_shape=whole...  3.87 us
    ppermute x1, starting transfers between devices, local(): far = lax.ppermute(near, 'core', [(0, 1), (1, 0)])  3.39 us
    ppermute x4, waiting for transfers between devices, local(): lax.ppermute(near[CUTS[run]:CUTS[run + 1], :HALF], ('zh', 'dp'), neighbou...  3.09 us
    pallas_call x1, Pallas kernels, local(): pl.pallas_call(place_core, out_shape=(whole, shape((H, H), F32), shape((H...  2.77 us
  transfers between devices with their start and end apart: 10, of which 4 were waited for; matrix products, arithmetic and copies ran while one was open for 0% of the time, Pallas kernels for 10%

profile of v3, /device:TPU:1, one launch (start us, length us, event | category | flops | bytes accessed | tf_op | source)
XLA Modules:
  0.0 86.4 jit_solution(11327803571692685223)
XLA Ops:
  0.7 14.2 %layers.1 = (bf16[32,136,128]{2,1,0:T(8,128)(2,1)}, f32[32,128]{1,0:T(8,128)}, f32[32,128]{1,0:T(8,128)}, bf16[128,128]{1,0:T(8,128)(2,1)}, bf16[1024,128]{1,0:T(8,128)(2,1)}) custom-call(s32[1]{0:T(128)} %bitcast.sect_ref, s32[8,128]{1,0:T(8,128)} %bitcast.17, s32[8,128]{1,0:T(8,128)} %bitcast.18, s32[8,128]{1,0:T(8,128)} %bitcast.19, ...), custom_call_target="tpu_custom_call" | custom-call | tf_op jit(solution)/shard_map/layers/pallas_call | solution.py:530
  14.9 0.0 copy-start.2
  14.9 0.0 copy-start.3
  14.9 9.4 %all-to-all-start = ((bf16[32,136,128]{2,1,0:T(8,128)(2,1)}), bf16[32,136,128]{2,1,0:T(8,128)(2,1)S(1)}, u32[]{:S(2)}, u32[]{:S(2)}) async-start(bf16[32,136,128]{2,1,0:T(8,128)(2,1)} %get-tuple-element.31), calls=%async_computation | async-start | bytes 2228224 | tf_op jit(solution)/shard_map/all_to_all | solution.py:618
  24.3 0.0 copy-start
  24.3 2.2 %copy-done = bf16[128,16384]{1,0:T(8,128)(2,1)S(1)} copy-done((bf16[128,16384]{1,0:T(8,128)(2,1)S(1)}, bf16[128,16384]{1,0:T(8,128)(2,1)}, u32[]{:S(2)}) %copy-start) | copy-done | bytes 4194328
  26.5 1.8 %states_back.1 = f32[32,128]{1,0:T(8,128)} custom-call(s32[1]{0:T(128)} %bitcast.sect_ref, f32[32,128]{1,0:T(8,128)S(1)} %copy-done.3, bf16[128,128]{1,0:T(8,128)(2,1)S(1)} %copy-done.2, bf16[1024,128]{1,0:T(8,128)(2,1)S(1)} %copy-done.1, bf16[128,16384]{1,0:T(8,128)(2,1)S(1)} %copy-done), custom_call_target="tpu_custom_call" | custom-call | flops 134217728 | bytes 4194304 | tf_op jit(solution)/shard_map/states_back/pallas_call | solution.py:606
  28.3 0.1 pad_add_fusion.place_ref
  28.4 12.1 %all-to-all-done.got_ref = bf16[32,136,128]{2,1,0:T(8,128)(2,1)S(1)} async-done(((bf16[32,136,128]{2,1,0:T(8,128)(2,1)}), bf16[32,136,128]{2,1,0:T(8,128)(2,1)S(1)}, u32[]{:S(2)}, u32[]{:S(2)}) %all-to-all-start) | async-done | bytes 1114144 | tf_op jit(solution)/shard_map/all_to_all | solution.py:618
  40.4 0.9 %sum_parts.1 = bf16[64,72,128]{2,1,0:T(8,128)(2,1)S(1)} custom-call(s32[4]{0:T(128)S(1)} %pad_add_fusion.place_ref, bf16[32,136,128]{2,1,0:T(8,128)(2,1)S(1)} %all-to-all-done.got_ref), custom_call_target="tpu_custom_call" | custom-call | tf_op jit(solution)/shard_map/sum_parts/pallas_call | solution.py:620
  41.3 25.6 %all_to_all.10.near_ref = bf16[64,72,128]{2,1,0:T(8,128)(2,1)S(1)} all-to-all(bf16[64,72,128]{2,1,0:T(8,128)(2,1)S(1)} %sum_parts.1), channel_id=1, replica_groups=mesh['zh'=2,'core'=2,'dp'=32] {'zh','dp'}, dimensions={0} | all-to-all | bytes 2359296 | tf_op jit(solution)/shard_map/all_to_all | solution.py:629
  66.9 3.4 %collective-permute-start = (bf16[64,72,128]{2,1,0:T(8,128)(2,1)S(1)}, bf16[64,72,128]{2,1,0:T(8,128)(2,1)S(1)}, u32[]{:S(2)}, u32[]{:S(2)}) collective-permute-start(bf16[64,72,128]{2,1,0:T(8,128)(2,1)S(1)} %all_to_all.10.near_ref), channel_id=1, source_target_pairs={{0,32},{32,0},{1,33},{33,1},{2,34},{34,2},{3,35},{35,3},{4,36},{36... | collective-permute-start | bytes 3538952 | tf_op jit(solution)/shard_map/ppermute | solution.py:630
  70.3 0.1 fusion
  70.5 0.4 collective-permute-start.1
  70.8 1.0 %collective-permute-start.2 = (bf16[16,64,128]{2,1,0:T(8,128)(2,1)S(1)}, bf16[16,64,128]{2,1,0:T(8,128)(2,1)S(1)}, u32[]{:S(2)}, u32[]{:S(2)}) collective-permute-start(bf16[16,64,128]{2,1,0:T(8,128)(2,1)S(1)} %get-tuple-element.52), channel_id=1, source_target_pairs={{0,3},{1,2},{2,1},{3,0},{4,7},{5,6},{6,5},{7,4},{8,11},{9,10},{10,... | collective-permute-start | bytes 786440 | tf_op jit(solution)/shard_map/ppermute | solution.py:632
  71.8 0.0 collective-permute-start.3
  71.8 0.7 collective-permute-start.4
  72.5 1.9 %place_own.1.part_hbm = f32[128,16384]{1,0:T(8,128)} custom-call(s32[4]{0:T(128)S(1)} %pad_add_fusion.place_ref, bf16[64,72,128]{2,1,0:T(8,128)(2,1)S(1)} %all_to_all.10.near_ref), custom_call_target="tpu_custom_call" | custom-call | bytes 6291456 | tf_op jit(solution)/shard_map/place_own/pallas_call | solution.py:641
  74.5 0.0 collective-permute-done.far_ref
  74.5 2.8 %place_core.1 = (f32[128,16384]{1,0:T(8,128)}, f32[128,128]{1,0:T(8,128)}, f32[128,384]{1,0:T(8,128)}, f32[128,384]{1,0:T(8,128)}, f32[16,128]{1,0:T(8,128)}, /*...) custom-call(s32[4]{0:T(128)S(1)} %pad_add_fusion.place_ref, ...), custom_call_target="tpu_custom_call", output_to_operand_aliasing={{0}: (3, {})} | custom-call | bytes 6291456 | tf_op jit(solution)/shard_map/place_core/pallas_call | solution.py:652
  77.3 1.2 %collective-permute-done.1.refs_0_ = bf16[16,64,128]{2,1,0:T(8,128)(2,1)S(1)} collective-permute-done((bf16[16,64,128]{2,1,0:T(8,128)(2,1)S(1)}, bf16[16,64,128]{2,1,0:T(8,128)(2,1)S(1)}, u32[]{:S(2)}, u32[]{:S(2)}) %collective-permute-start.1) | collective-permute-done | bytes 262176 | tf_op jit(solution)/shard_map/ppermute | solution.py:632
  78.5 1.2 %collective-permute-done.2.refs_1_ = bf16[16,64,128]{2,1,0:T(8,128)(2,1)S(1)} collective-permute-done((bf16[16,64,128]{2,1,0:T(8,128)(2,1)S(1)}, bf16[16,64,128]{2,1,0:T(8,128)(2,1)S(1)}, u32[]{:S(2)}, u32[]{:S(2)}) %collective-permute-start.2) | collective-permute-done | bytes 262176 | tf_op jit(solution)/shard_map/ppermute | solution.py:632
  79.7 0.0 collective-permute-done.3.refs_2_
  79.7 0.7 collective-permute-done.4.refs_3_
  80.4 1.4 %collective-permute-start.5 = (bf16[16,64,128]{2,1,0:T(8,128)(2,1)S(1)}, bf16[16,64,128]{2,1,0:T(8,128)(2,1)S(1)}, u32[]{:S(2)}, u32[]{:S(2)}) collective-permute-start(bf16[16,64,128]{2,1,0:T(8,128)(2,1)S(1)} %collective-permute-done.1.refs_0_), channel_id=1, source_target_pairs={{0,32},{32,0},{1,33},{33,1},{2,34},{34,2},{3,35},{35,3},{4,36},{36... | collective-permute-start | bytes 786440 | tf_op jit(solution)/shard_map/ppermute | solution.py:674
  81.8 0.0 collective-permute-start.6
  81.8 0.5 collective-permute-start.7
  82.3 0.0 collective-permute-start.8
  82.3 1.9 %place_rest.2.refs_4_ = f32[128,16384]{1,0:T(8,128)} custom-call(s32[4]{0:T(128)S(1)} %pad_add_fusion.place_ref, bf16[16,64,128]{2,1,0:T(8,128)(2,1)S(1)} %collective-permute-done.1.refs_0_, bf16[16,64,128]{2,1,0:T(8,128)(2,1)S(1)} %collective-permute-done.2.refs_1_, ...), custom_call_target="tpu_custom_call", output_to_operand_aliasing={{}: (5, {})} | custom-call | bytes 6291456 | tf_op jit(solution)/shard_map/place_rest/pallas_call | solution.py:676
  84.2 0.0 collective-permute-done.5.refs_0_
  84.3 0.0 collective-permute-done.8.refs_3_
  84.3 1.9 %place_rest.3 = f32[128,16384]{1,0:T(8,128)} custom-call(s32[4]{0:T(128)S(1)} %pad_add_fusion.place_ref, bf16[16,64,128]{2,1,0:T(8,128)(2,1)S(1)} %collective-permute-done.5.refs_0_, bf16[16,64,128]{2,1,0:T(8,128)(2,1)S(1)} %collective-permute-done.6.refs_1_, ...), custom_call_target="tpu_custom_call", output_to_operand_aliasing={{}: (5, {})} | custom-call | bytes 6291456 | tf_op jit(solution)/shard_map/place_rest/pallas_call | solution.py:676
  (6 shorter events, 0.0 us)
Async XLA Ops:
  14.9 9.4 %copy-start.1 = (bf16[1024,128]{1,0:T(8,128)(2,1)S(1)}, bf16[1024,128]{1,0:T(8,128)(2,1)}, u32[]{:S(2)}) copy-start(bf16[1024,128]{1,0:T(8,128)(2,1)} %get-tuple-element.34.pairs_ref) | copy-start | bytes 786436
  14.9 9.4 %copy-start.2 = (bf16[128,128]{1,0:T(8,128)(2,1)S(1)}, bf16[128,128]{1,0:T(8,128)(2,1)}, u32[]{:S(2)}) copy-start(bf16[128,128]{1,0:T(8,128)(2,1)} %get-tuple-element.33.grad_t_ref) | copy-start | bytes 98308
  14.9 9.4 %copy-start.3 = (f32[32,128]{1,0:T(8,128)S(1)}, f32[32,128]{1,0:T(8,128)}, u32[]{:S(2)}) copy-start(f32[32,128]{1,0:T(8,128)} %get-tuple-element.32.base_ref) | copy-start | bytes 49156
  14.9 25.6 %all-to-all-start = ((bf16[32,136,128]{2,1,0:T(8,128)(2,1)}), bf16[32,136,128]{2,1,0:T(8,128)(2,1)S(1)}, u32[]{:S(2)}, u32[]{:S(2)}) async-start(bf16[32,136,128]{2,1,0:T(8,128)(2,1)} %get-tuple-element.31), calls=%async_computation | async-start | bytes 2228224 | tf_op jit(solution)/shard_map/all_to_all | solution.py:618
  24.3 2.2 %copy-start = (bf16[128,16384]{1,0:T(8,128)(2,1)S(1)}, bf16[128,16384]{1,0:T(8,128)(2,1)}, u32[]{:S(2)}) copy-start(bf16[128,16384]{1,0:T(8,128)(2,1)} %w_ref.1) | copy-start | bytes 12582916
  66.9 7.5 %collective-permute-start = (bf16[64,72,128]{2,1,0:T(8,128)(2,1)S(1)}, bf16[64,72,128]{2,1,0:T(8,128)(2,1)S(1)}, u32[]{:S(2)}, u32[]{:S(2)}) collective-permute-start(bf16[64,72,128]{2,1,0:T(8,128)(2,1)S(1)} %all_to_all.10.near_ref), channel_id=1, source_target_pairs={{0,32},{32,0},{1,33},{33,1},{2,34},{34,2},{3,35},{35,3},{4,36},{36... | collective-permute-start | bytes 3538952 | tf_op jit(solution)/shard_map/ppermute | solution.py:630
  70.5 8.0 %collective-permute-start.1 = (bf16[16,64,128]{2,1,0:T(8,128)(2,1)S(1)}, bf16[16,64,128]{2,1,0:T(8,128)(2,1)S(1)}, u32[]{:S(2)}, u32[]{:S(2)}) collective-permute-start(bf16[16,64,128]{2,1,0:T(8,128)(2,1)S(1)} %get-tuple-element.53), channel_id=1, source_target_pairs={{0,1},{1,0},{2,3},{3,2},{4,5},{5,4},{6,7},{7,6},{8,9},{9,8},{10,11... | collective-permute-start | bytes 786440 | tf_op jit(solution)/shard_map/ppermute | solution.py:632
  70.8 8.8 %collective-permute-start.2 = (bf16[16,64,128]{2,1,0:T(8,128)(2,1)S(1)}, bf16[16,64,128]{2,1,0:T(8,128)(2,1)S(1)}, u32[]{:S(2)}, u32[]{:S(2)}) collective-permute-start(bf16[16,64,128]{2,1,0:T(8,128)(2,1)S(1)} %get-tuple-element.52), channel_id=1, source_target_pairs={{0,3},{1,2},{2,1},{3,0},{4,7},{5,6},{6,5},{7,4},{8,11},{9,10},{10,... | collective-permute-start | bytes 786440 | tf_op jit(solution)/shard_map/ppermute | solution.py:632
  71.8 7.8 %collective-permute-start.3 = (bf16[16,64,128]{2,1,0:T(8,128)(2,1)S(1)}, bf16[16,64,128]{2,1,0:T(8,128)(2,1)S(1)}, u32[]{:S(2)}, u32[]{:S(2)}) collective-permute-start(bf16[16,64,128]{2,1,0:T(8,128)(2,1)S(1)} %get-tuple-element.51), channel_id=1, source_target_pairs={{0,4},{1,5},{2,6},{3,7},{4,0},{5,1},{6,2},{7,3},{8,12},{9,13},{10,... | collective-permute-start | bytes 786440 | tf_op jit(solution)/shard_map/ppermute | solution.py:632
  71.8 8.5 %collective-permute-start.4 = (bf16[16,64,128]{2,1,0:T(8,128)(2,1)S(1)}, bf16[16,64,128]{2,1,0:T(8,128)(2,1)S(1)}, u32[]{:S(2)}, u32[]{:S(2)}) collective-permute-start(bf16[16,64,128]{2,1,0:T(8,128)(2,1)S(1)} %get-tuple-element.50), channel_id=1, source_target_pairs={{0,12},{1,13},{2,14},{3,15},{4,8},{5,9},{6,10},{7,11},{8,4},{9,5},... | collective-permute-start | bytes 786440 | tf_op jit(solution)/shard_map/ppermute | solution.py:632
  80.4 3.9 %collective-permute-start.5 = (bf16[16,64,128]{2,1,0:T(8,128)(2,1)S(1)}, bf16[16,64,128]{2,1,0:T(8,128)(2,1)S(1)}, u32[]{:S(2)}, u32[]{:S(2)}) collective-permute-start(bf16[16,64,128]{2,1,0:T(8,128)(2,1)S(1)} %collective-permute-done.1.refs_0_), channel_id=1, source_target_pairs={{0,32},{32,0},{1,33},{33,1},{2,34},{34,2},{3,35},{35,3},{4,36},{36... | collective-permute-start | bytes 786440 | tf_op jit(solution)/shard_map/ppermute | solution.py:674
  81.8 2.5 %collective-permute-start.6 = (bf16[16,64,128]{2,1,0:T(8,128)(2,1)S(1)}, bf16[16,64,128]{2,1,0:T(8,128)(2,1)S(1)}, u32[]{:S(2)}, u32[]{:S(2)}) collective-permute-start(bf16[16,64,128]{2,1,0:T(8,128)(2,1)S(1)} %collective-permute-done.2.refs_1_), channel_id=1, source_target_pairs={{0,32},{32,0},{1,33},{33,1},{2,34},{34,2},{3,35},{35,3},{4,36},{36... | collective-permute-start | bytes 786440 | tf_op jit(solution)/shard_map/ppermute | solution.py:674
  81.8 2.5 %collective-permute-start.7 = (bf16[16,64,128]{2,1,0:T(8,128)(2,1)S(1)}, bf16[16,64,128]{2,1,0:T(8,128)(2,1)S(1)}, u32[]{:S(2)}, u32[]{:S(2)}) collective-permute-start(bf16[16,64,128]{2,1,0:T(8,128)(2,1)S(1)} %collective-permute-done.3.refs_2_), channel_id=1, source_target_pairs={{0,32},{32,0},{1,33},{33,1},{2,34},{34,2},{3,35},{35,3},{4,36},{36... | collective-permute-start | bytes 786440 | tf_op jit(solution)/shard_map/ppermute | solution.py:674
  82.3 2.0 %collective-permute-start.8 = (bf16[16,64,128]{2,1,0:T(8,128)(2,1)S(1)}, bf16[16,64,128]{2,1,0:T(8,128)(2,1)S(1)}, u32[]{:S(2)}, u32[]{:S(2)}) collective-permute-start(bf16[16,64,128]{2,1,0:T(8,128)(2,1)S(1)} %collective-permute-done.4.refs_3_), channel_id=1, source_target_pairs={{0,32},{32,0},{1,33},{33,1},{2,34},{34,2},{3,35},{35,3},{4,36},{36... | collective-permute-start | bytes 786440 | tf_op jit(solution)/shard_map/ppermute | solution.py:674

commit v4 on v3

--- a/solution.py
+++ b/solution.py
@@ -19,12 +19,23 @@
 ROWS = 136
 SMALL = 8
 GROUP = 32
-HALF = H // 2
-CUTS = (0, 16, 32, 48, 64)
-RUNS = 4
+CLASS = 8
+AXES = 3
 W_PARTS = 1
 BF = jnp.bfloat16
 F32 = jnp.float32
+
+
+def spot_of(dp):
+    return dp % 4, dp // 4 % 4, dp // 16
+
+
+def slot_of(dp):
+    x, y, z = spot_of(dp)
+    return ((x + z) % 2 * 2 + (y + z) % 2) * CLASS + z * 4 + y // 2 * 2 + x // 2
+
+
+DP_AT = sorted(range(GROUP), key=slot_of)
 
 
 def nn(left, right):
@@ -289,7 +300,7 @@
 
     both_t = jnp.concatenate([states0.astype(F32).T, states1.astype(F32).T], axis=1).astype(BF)
 
-    def own_body(at, carry):
+    for at in range(OWN // 2):
         right = jnp.concatenate(
             [
                 jnp.concatenate(
@@ -305,10 +316,7 @@
         )
         out = nn(both_t, right).astype(BF)
         for q in range(2):
-            send_ref[at * 2 + q, 0:H, :] = out[:, q * H : (q + 1) * H]
-        return carry
-
-    lax.fori_loop(0, OWN // 2, own_body, 0, unroll=True)
+            send_ref[DP_AT[at * 2 + q], 0:H, :] = out[:, q * H : (q + 1) * H]
 
     rows_scr[...] = g_one.astype(F32)
     g1 = rows_scr[own_rows, :].astype(BF)
@@ -373,7 +381,7 @@
             row = 241 + at * 3 + part
             small_scr[row : row + 1, :] = jnp.sum(rows_scr[own_rows, :], axis=0, keepdims=True)
     for at in range(GROUP):
-        send_ref[at, H:ROWS, :] = small_scr[at * SMALL : (at + 1) * SMALL, :].astype(BF)
+        send_ref[DP_AT[at], H:ROWS, :] = small_scr[at * SMALL : (at + 1) * SMALL, :].astype(BF)
 
     rows_scr[...] = back_zero + fine(nn, nn(adj_t, g_one), b_mat)
     base_ref[...] = rows_scr[own_rows, :]
@@ -381,23 +389,15 @@
     pairs_out_ref[...] = pair_h[pl.ds(pl.multiple_of(sect * PAIRS, PAIRS), PAIRS), :]
 
 
-def sum_kernel(place_ref, got_ref, out_ref, two):
-    shift = place_ref[2]
-
+def sum_kernel(got_ref, out_ref):
     def body(at, total):
         return total + got_ref[at].astype(F32)
 
     total = lax.fori_loop(1, GROUP, body, got_ref[0].astype(F32), unroll=True)
-    rows = total[:H].T
-    for part in range(2):
-        half_rows = rows[part * HALF : (part + 1) * HALF]
-        two[part] = jnp.concatenate([half_rows, total[H:]], axis=0).astype(BF)
-
-    def put(at, carry):
-        out_ref[at] = two[jnp.bitwise_and(jnp.right_shift(at, shift), 1)]
-        return carry
-
-    lax.fori_loop(0, 2 * GROUP, put, 0, unroll=8)
+    piece = jnp.concatenate([total[:H].T, total[H:]], axis=0).astype(BF)
+
+    for at in range(2 * CLASS):
+        out_ref[at] = piece
 
 
 def states_kernel(sect_ref, base_ref, grad_t_ref, pairs_ref, w_ref, out_ref, d_all, rows_scr):
@@ -433,89 +433,88 @@
     out_ref[...] = lax.fori_loop(0, 32, back_body, base_ref[...], unroll=True)
 
 
-def place_rows(place_ref, other_core, other_half, parts, out_hbm, stage, sem):
-    core = jnp.bitwise_xor(place_ref[3], 1) if other_core else place_ref[3]
+def place_rows(place_ref, parts, out_hbm, stage, sem):
     copies = []
-    for run, (ref, first) in enumerate(parts):
-        bit = place_ref[run // 2]
-        if other_half:
-            bit = jnp.bitwise_xor(bit, 1)
-        low, high = CUTS[run], CUTS[run + 1]
-        half = low // GROUP
-        at_col = (half * 2 + core) * (GROUP * H) + (low - half * GROUP) * H
-        width = (high - low) * H
-        for part in range(2):
-            for dev in range(low, high):
-                for row in range(part * 32, part * 32 + 32, 16):
-                    stage[row : row + 16, dev * H : (dev + 1) * H] = ref[
-                        dev - first, row : row + 16, :
+    for part, (ref, other_core, change) in enumerate(parts):
+        core, kind = place_of(place_ref, other_core, change)
+        for half in range(2):
+            at_col = ((half * 2 + core) * GROUP + kind * CLASS) * H
+            low = (part * 2 + half) * CLASS * H
+            cols = pl.ds(low, CLASS * H)
+            for dev in range(CLASS):
+                for row in range(0, H, 16):
+                    stage[row : row + 16, low + dev * H : low + (dev + 1) * H] = ref[
+                        half * CLASS + dev, row : row + 16, :
                     ].astype(F32)
             copies.append(
                 pltpu.make_async_copy(
-                    stage.at[pl.ds(part * 32, 32), pl.ds(low * H, width)],
-                    out_hbm.at[
-                        pl.ds(pl.multiple_of(bit * HALF + part * 32, 32), 32),
-                        pl.ds(pl.multiple_of(at_col, H), width),
-                    ],
+                    stage.at[:, cols],
+                    out_hbm.at[:, pl.ds(pl.multiple_of(at_col, CLASS * H), CLASS * H)],
                     sem.at[len(copies)],
                 )
             )
             copies[-1].start()
-    for copy in copies:
+    return copies
+
+
+def place_of(place_ref, other_core, change):
+    core, kind = place_ref[0], place_ref[1]
+    return (1 - core if other_core else core), jnp.bitwise_xor(kind, change)
+
+
+CHANGES = (2, 1, 3)
+
+
+def place_own(place_ref, near_ref, far_ref, out_hbm, stage, sems):
+    parts = [(near_ref, False, 0), (far_ref, True, 0)]
+    for copy in place_rows(place_ref, parts, out_hbm, stage, sems):
         copy.wait()
 
 
-def place_own(place_ref, near_ref, out_hbm, stage, sems):
-    place_rows(place_ref, False, False, [(near_ref, 0)] * RUNS, out_hbm, stage, sems)
-
-
-def place_core(
-    place_ref,
-    near_ref,
-    far_ref,
-    part_hbm,
-    out_hbm,
-    gb_ref,
-    gi_ref,
-    gh_ref,
-    ge_ref,
-    be_ref,
-    bi_ref,
-    bh_ref,
-    small,
-    stage,
-    sems,
-):
-    del part_hbm
-    place_rows(place_ref, True, False, [(far_ref, 0)] * RUNS, out_hbm, stage, sems)
-    core = place_ref[3]
-    for which, ref in ((core, near_ref), (1 - core, far_ref)):
-        for half in range(2):
-            base = (half * 2 + which) * (GROUP * SMALL)
-            for dev in range(GROUP):
-                at = pl.multiple_of(base + dev * SMALL, SMALL)
-                small[pl.ds(at, SMALL), :] = ref[half * GROUP + dev, HALF:, :].astype(F32)
+def place_rest(place_ref, *refs):
+    out_hbm, stage, sems = refs[AXES + 1 :]
+    parts = [(ref, False, change) for ref, change in zip(refs, CHANGES)]
+    for copy in place_rows(place_ref, parts, out_hbm, stage, sems):
+        copy.wait()
+
+
+def place_last(place_ref, near_ref, far_ref, *refs):
+    rest, far_rest, refs = refs[:AXES], refs[AXES : 2 * AXES], refs[2 * AXES + 1 :]
+    out_hbm, *ends = refs[:8]
+    stage, sems, small, gb, gi, gh, ge, be, bi, bh, end_sems = refs[8:]
+    own = [(near_ref, False, 0), (far_ref, True, 0)]
+    own += [(ref, False, change) for ref, change in zip(rest, CHANGES)]
+    last = [(ref, True, change) for ref, change in zip(far_rest, CHANGES)]
+    copies = place_rows(place_ref, last, out_hbm, stage, sems)
+    for ref, other_core, change in own + last:
+        core, kind = place_of(place_ref, other_core, change)
+        for at in range(2 * CLASS):
+            block = ((at // CLASS) * 2 + core) * GROUP + kind * CLASS + at % CLASS
+            row = pl.multiple_of(block * SMALL, SMALL)
+            small[pl.ds(row, SMALL), :] = ref[at, H:ROWS, :].astype(F32)
     misc = jnp.zeros((32, H), F32)
     for sect in range(MB):
         base = sect * GROUP * SMALL
         rows = slice(sect * 32, (sect + 1) * 32)
-        gb_ref[rows, :] = small[base : base + 32, :]
+        gb[rows, :] = small[base : base + 32, :]
         for part in range(3):
             cols = slice(part * H, (part + 1) * H)
             row = base + 32 + part * 32
-            gi_ref[rows, cols] = small[row : row + 32, :]
-            gh_ref[rows, cols] = small[row + 96 : row + 128, :]
+            gi[rows, cols] = small[row : row + 32, :]
+            gh[rows, cols] = small[row + 96 : row + 128, :]
         misc = misc + small[base + 224 : base + 256, :]
-    ge_ref[...] = misc[0:16]
-    be_ref[...] = misc[16:17]
-    bi_ref[...] = misc[17:20]
-    bh_ref[...] = misc[20:23]
-
-
-def place_rest(other_core, place_ref, *refs):
-    out_hbm, stage, sems = refs[RUNS + 1 :]
-    parts = list(zip(refs[:RUNS], CUTS))
-    place_rows(place_ref, other_core, True, parts, out_hbm, stage, sems)
+    ge[...] = misc[0:16]
+    be[...] = misc[16:17]
+    bi[...] = misc[17:20]
+    bh[...] = misc[20:23]
+    end_copies = [
+        pltpu.make_async_copy(here, there, end_sems.at[at])
+        for at, (here, there) in enumerate(zip((gb, gi, gh, ge, be, bi, bh), ends))
+    ]
+    for copy in end_copies:
+        copy.start()
+    for copy in copies + end_copies:
+        copy.wait()
 
 
 VMEM_SPEC = pl.BlockSpec(memory_space=pltpu.VMEM)
@@ -540,10 +539,10 @@
         out_specs=(VMEM_SPEC,) * 5,
         scratch_shapes=[pltpu.VMEM(v.shape, v.dtype) for v in operands]
         + [
-            pltpu.VMEM((NODES * GAP, H), F32),
-            pltpu.VMEM((NODES * GAP, H), F32),
-            pltpu.VMEM((H * GAP, H), F32),
-            pltpu.VMEM((OWN * GAP, H), F32),
+            pltpu.VMEM(((NODES + 1) * GAP, H), F32),
+            pltpu.VMEM(((NODES + 1) * GAP, H), F32),
+            pltpu.VMEM(((H + 1) * GAP, H), F32),
+            pltpu.VMEM(((OWN + 1) * GAP, H), F32),
             pltpu.VMEM((MB * PAIRS, H), BF),
             pltpu.VMEM((NODES, H), F32),
             pltpu.VMEM((GROUP * SMALL, H), F32),
@@ -556,13 +555,21 @@
     )(sect, *operands)
 
 
-def neighbours(axis, side):
+def neighbours(axis):
     pairs = []
-    for index in range(2 * GROUP):
-        spot = [index % 4, index // 4 % 4, index // 16]
-        step = 1 if spot[axis] % 2 == side else -1
-        spot[axis] = (spot[axis] + step) % 4
-        pairs.append((index, spot[2] * 16 + spot[1] * 4 + spot[0]))
+    for zh in range(2):
+        for core in range(2):
+            for dp in range(GROUP):
+                x, y, z = spot_of(dp)
+                spot = [x, y, zh * 2 + z]
+                spot[axis] = (spot[axis] + (-1 if core else 1)) % 4
+                x, y, z = spot
+                pairs.append(
+                    (
+                        z // 2 * 64 + core * GROUP + z % 2 * 16 + y * 4 + x,
+                        zh * 64 + core * GROUP + dp,
+                    )
+                )
     return pairs
 
 
@@ -586,8 +593,8 @@
     sect = (lax.axis_index("zh") * 2 + core).astype(jnp.int32)
     sect = sect.reshape(1)
     dp = lax.axis_index("dp").astype(jnp.int32)
-    zh = lax.axis_index("zh").astype(jnp.int32)
-    place = jnp.stack([dp & 1, (dp >> 2) & 1, zh * 2, core])
+    z = dp >> 4
+    place = jnp.stack([core, ((dp + z) & 1) * 2 + (((dp >> 2) + z) & 1)])
     operands = [v.reshape(8, 128) for v in (edge_source, edge_target, edge_live)] + [
         edge_features,
         w_edge_in,
@@ -608,7 +615,7 @@
         out_shape=shape((ATOMS, H), F32),
         in_specs=[SMEM_SPEC] + [VMEM_SPEC] * 4,
         out_specs=VMEM_SPEC,
-        scratch_shapes=[pltpu.VMEM((H * (ATOMS + 1), H), F32), pltpu.VMEM((NODES, H), F32)],
+        scratch_shapes=[pltpu.VMEM(((H + 1) * (ATOMS + 1), H), F32), pltpu.VMEM((NODES, H), F32)],
         compiler_params=pltpu.CompilerParams(vmem_limit_bytes=LOW),
         cost_estimate=pl.CostEstimate(
             flops=2 * ATOMS * H * H * H, bytes_accessed=2 * H * H * H, transcendentals=0
@@ -619,72 +626,79 @@
     got, grad_states = lax.optimization_barrier((got, grad_states))
     piece = pl.pallas_call(
         sum_kernel,
-        out_shape=shape((2 * GROUP, HALF + SMALL, H), BF),
-        in_specs=[SMEM_SPEC, VMEM_SPEC],
+        out_shape=shape((2 * CLASS, ROWS, H), BF),
+        in_specs=[VMEM_SPEC],
         out_specs=VMEM_SPEC,
-        scratch_shapes=[pltpu.VMEM((2, HALF + SMALL, H), BF)],
         compiler_params=pltpu.CompilerParams(vmem_limit_bytes=LOW),
         name="sum_parts",
-    )(place, got)
-    near = lax.all_to_all(piece, ("zh", "dp"), split_axis=0, concat_axis=0)
-    far = lax.ppermute(near, "core", [(0, 1), (1, 0)])
-    rest = [
-        lax.ppermute(
-            near[CUTS[run] : CUTS[run + 1], :HALF], ("zh", "dp"), neighbours(run // 2, run % 2)
-        )
-        for run in range(RUNS)
+    )(got)
+    classes = [
+        [zh * 64 + c * GROUP + DP_AT[kind * CLASS + at] for zh in range(2) for at in range(CLASS)]
+        for c in range(2)
+        for kind in range(4)
     ]
-    stage = [pltpu.VMEM((HALF, 2 * GROUP * H), F32), pltpu.SemaphoreType.DMA((2 * RUNS,))]
+    near = lax.all_to_all(
+        piece, ("zh", "core", "dp"), split_axis=0, concat_axis=0, axis_index_groups=classes
+    )
+    swap = [(0, 1), (1, 0)]
+    far = lax.ppermute(near, "core", swap)
+    rest = [lax.ppermute(near, ("zh", "core", "dp"), neighbours(axis)) for axis in range(AXES)]
+
     params = pltpu.CompilerParams(vmem_limit_bytes=LOW)
     cost = pl.CostEstimate(flops=0, bytes_accessed=6 * 2**20, transcendentals=0)
+
+    def stage(parts):
+        return [pltpu.VMEM((H, parts * 2 * CLASS * H), F32), pltpu.SemaphoreType.DMA((2 * parts,))]
+
     whole = shape((H, H * H), F32)
     out = pl.pallas_call(
         place_own,
         out_shape=whole,
-        in_specs=[SMEM_SPEC, VMEM_SPEC],
+        in_specs=[SMEM_SPEC, VMEM_SPEC, VMEM_SPEC],
         out_specs=ANY_SPEC,
-        scratch_shapes=stage,
+        scratch_shapes=stage(2),
         compiler_params=params,
         cost_estimate=cost,
         name="place_own",
-    )(place, near)
-    out, grad_b_out, grad_w_in, grad_w_hid, grad_ein, grad_bein, grad_bin, grad_bhid = (
+    )(place, near, far)
+    rest, out = lax.optimization_barrier((rest, out))
+    far_rest = [lax.ppermute(part, "core", swap) for part in rest]
+    out = pl.pallas_call(
+        place_rest,
+        out_shape=whole,
+        in_specs=[SMEM_SPEC] + [VMEM_SPEC] * AXES + [ANY_SPEC],
+        out_specs=ANY_SPEC,
+        scratch_shapes=stage(AXES),
+        input_output_aliases={AXES + 1: 0},
+        compiler_params=params,
+        cost_estimate=cost,
+        name="place_rest",
+    )(place, *rest, out)
+    ends = [
+        shape((H, H), F32),
+        shape((H, 3 * H), F32),
+        shape((H, 3 * H), F32),
+        shape((16, H), F32),
+        shape((1, H), F32),
+        shape((3, H), F32),
+        shape((3, H), F32),
+    ]
+    grad_w_out, grad_b_out, grad_w_in, grad_w_hid, grad_ein, grad_bein, grad_bin, grad_bhid = (
         pl.pallas_call(
-            place_core,
-            out_shape=(
-                whole,
-                shape((H, H), F32),
-                shape((H, 3 * H), F32),
-                shape((H, 3 * H), F32),
-                shape((16, H), F32),
-                shape((1, H), F32),
-                shape((3, H), F32),
-                shape((3, H), F32),
-            ),
-            in_specs=[SMEM_SPEC, VMEM_SPEC, VMEM_SPEC, ANY_SPEC],
-            out_specs=(ANY_SPEC,) + (VMEM_SPEC,) * 7,
-            scratch_shapes=[pltpu.VMEM((MB * GROUP * SMALL, H), F32)] + stage,
-            input_output_aliases={3: 0},
+            place_last,
+            out_shape=[whole] + ends,
+            in_specs=[SMEM_SPEC] + [VMEM_SPEC] * (2 * AXES + 2) + [ANY_SPEC],
+            out_specs=[ANY_SPEC] * 8,
+            scratch_shapes=stage(AXES)
+            + [pltpu.VMEM((MB * GROUP * SMALL, H), F32)]
+            + [pltpu.VMEM(v.shape, v.dtype) for v in ends]
+            + [pltpu.SemaphoreType.DMA((7,))],
+            input_output_aliases={2 * AXES + 3: 0},
             compiler_params=params,
             cost_estimate=cost,
-            name="place_core",
-        )(place, near, far, out)
+            name="place_last",
+        )(place, near, far, *rest, *far_rest, out)
     )
-    rest, out = lax.optimization_barrier((rest, out))
-    far_rest = [lax.ppermute(part, "core", [(0, 1), (1, 0)]) for part in rest]
-    for other_core, parts in ((False, rest), (True, far_rest)):
-        out = pl.pallas_call(
-            functools.partial(place_rest, other_core),
-            out_shape=whole,
-            in_specs=[SMEM_SPEC] + [VMEM_SPEC] * RUNS + [ANY_SPEC],
-            out_specs=ANY_SPEC,
-            scratch_shapes=stage,
-            input_output_aliases={RUNS + 1: 0},
-            compiler_params=params,
-            cost_estimate=cost,
-            name="place_rest",
-        )(place, *parts, out)
-    grad_w_out = out
     return (
         final,
         grad_states,

time: 86.7 us -> 80.2 us (0.925)
  blocking collectives: 25.6 us -> 18.6 us
  Pallas kernels: 25.5 us -> 23 us
  local copies, waits for them, and re-layouts: 2.32 us -> 4.61 us
  waiting for transfers between devices: 15.2 us -> 16.5 us
    all_to_all x1, blocking collectives: 25.6 us -> 18.6 us  [local(): lax.all_to_all(piece, ('zh', 'core', 'dp'), split_axis=0, concat_axis=0,...]
    ppermute x9 -> x7, waiting for transfers between devices: 3.1 us -> 6.8 us  [the longest x3 6.38 us: local(): lax.ppermute(near, ('zh', 'core', 'dp'), neighbours(axis))]
    pallas_call x4 -> x3, Pallas kernels: 7.53 us -> 5.06 us  [the longest x1 2.54 us: local(): pl.pallas_call(place_last, out_shape=[whole] + ends, in_specs=[SMEM_SPEC]...]
    unnamed x8, local copies, waits for them, and re-layouts: 2.2 us -> 4.61 us
    all_to_all x1, waiting for transfers between devices: 12.1 us -> 9.74 us  [local(): got = lax.all_to_all(send, 'dp', split_axis=0, concat_axis=0)]
    ppermute x9 -> x7, starting transfers between devices: 7.4 us -> 6.73 us  [the longest x1 3.37 us: local(): far = lax.ppermute(near, 'core', swap)]
  transfers between devices with their start and end apart: 10 -> 8, of which waited for: 4 -> 5; matrix products, arithmetic and copies ran while one was open for 0% -> 0% of each run, Pallas kernels for 10% -> 8%
where the time goes in v4:
time: 80.2 us; the launch traced here: 79.7 us
  Pallas kernels  23 us (29%)
  blocking collectives  18.6 us (23%)
  waiting for transfers between devices  16.5 us (21%)
  starting transfers between devices  16 us (20%)
  local copies, waits for them, and re-layouts  4.61 us (6%)
  between operations  0.89 us (1%)
    all_to_all x1, blocking collectives, local(): lax.all_to_all(piece, ('zh', 'core', 'dp'), split_axis=0, concat_axis=0,...  18.6 us
    pallas_call x1, Pallas kernels, run_layers(): pl.pallas_call(local_kernel, out_shape=(shape((GROUP, ROWS, H), BF), shap...  14.2 us
    all_to_all x1, waiting for transfers between devices, local(): got = lax.all_to_all(send, 'dp', split_axis=0, concat_axis=0)  9.74 us
    all_to_all x1, starting transfers between devices, local(): got = lax.all_to_all(send, 'dp', split_axis=0, concat_axis=0)  9.23 us
    ppermute x3, waiting for transfers between devices, local(): lax.ppermute(near, ('zh', 'core', 'dp'), neighbours(axis))  6.38 us
    unnamed x8, local copies, waits for them, and re-layouts  4.61 us
    ppermute x1, starting transfers between devices, local(): far = lax.ppermute(near, 'core', swap)  3.37 us
    pallas_call x1, Pallas kernels, local(): pl.pallas_call(place_last, out_shape=[whole] + ends, in_specs=[SMEM_SPEC]...  2.54 us
  transfers between devices with their start and end apart: 8, of which 5 were waited for; matrix products, arithmetic and copies ran while one was open for 0% of the time, Pallas kernels for 8%

profile of v4, /device:TPU:1, one launch (start us, length us, event | category | flops | bytes accessed | tf_op | source)
XLA Modules:
  0.0 79.7 jit_solution(12677896983999476076)
XLA Ops:
  0.7 14.2 %layers.1 = (bf16[32,136,128]{2,1,0:T(8,128)(2,1)}, f32[32,128]{1,0:T(8,128)}, f32[32,128]{1,0:T(8,128)}, bf16[128,128]{1,0:T(8,128)(2,1)}, bf16[1024,128]{1,0:T(8,128)(2,1)}) custom-call(s32[1]{0:T(128)} %bitcast.sect_ref, s32[8,128]{1,0:T(8,128)} %bitcast.15, s32[8,128]{1,0:T(8,128)} %bitcast.16, s32[8,128]{1,0:T(8,128)} %bitcast.17, ...), custom_call_target="tpu_custom_call" | custom-call | tf_op jit(solution)/shard_map/layers/pallas_call | solution.py:529
  14.9 9.2 %all-to-all-start = ((bf16[32,136,128]{2,1,0:T(8,128)(2,1)}), bf16[32,136,128]{2,1,0:T(8,128)(2,1)S(1)}, u32[]{:S(2)}, u32[]{:S(2)}) async-start(bf16[32,136,128]{2,1,0:T(8,128)(2,1)} %get-tuple-element.30), calls=%async_computation | async-start | bytes 2228224 | tf_op jit(solution)/shard_map/all_to_all | solution.py:625
  24.1 0.0 copy-start
  24.1 2.2 %copy-done = bf16[128,16384]{1,0:T(8,128)(2,1)S(1)} copy-done((bf16[128,16384]{1,0:T(8,128)(2,1)S(1)}, bf16[128,16384]{1,0:T(8,128)(2,1)}, u32[]{:S(2)}) %copy-start) | copy-done | bytes 4194328
  26.3 0.0 copy-start.1
  26.3 0.9 %copy-done.1 = bf16[1024,128]{1,0:T(8,128)(2,1)S(1)} copy-done((bf16[1024,128]{1,0:T(8,128)(2,1)S(1)}, bf16[1024,128]{1,0:T(8,128)(2,1)}, u32[]{:S(2)}) %copy-start.1) | copy-done | bytes 262168
  27.3 0.0 copy-start.2
  27.3 0.8 copy-done.2
  28.0 0.0 copy-start.3
  28.0 0.7 copy-done.3
  28.7 1.8 %states_back.1 = f32[32,128]{1,0:T(8,128)} custom-call(s32[1]{0:T(128)} %bitcast.sect_ref, f32[32,128]{1,0:T(8,128)S(1)} %copy-done.3, bf16[128,128]{1,0:T(8,128)(2,1)S(1)} %copy-done.2, bf16[1024,128]{1,0:T(8,128)(2,1)S(1)} %copy-done.1, bf16[128,16384]{1,0:T(8,128)(2,1)S(1)} %copy-done), custom_call_target="tpu_custom_call" | custom-call | flops 134217728 | bytes 4194304 | tf_op jit(solution)/shard_map/states_back/pallas_call | solution.py:613
  30.6 9.7 %all-to-all-done.got_ref = bf16[32,136,128]{2,1,0:T(8,128)(2,1)S(1)} async-done(((bf16[32,136,128]{2,1,0:T(8,128)(2,1)}), bf16[32,136,128]{2,1,0:T(8,128)(2,1)S(1)}, u32[]{:S(2)}, u32[]{:S(2)}) %all-to-all-start) | async-done | bytes 1114144 | tf_op jit(solution)/shard_map/all_to_all | solution.py:625
  40.3 0.2 sum_parts.1
  40.5 18.6 %all_to_all.10.near_ref = bf16[16,136,128]{2,1,0:T(8,128)(2,1)S(1)} all-to-all(bf16[16,136,128]{2,1,0:T(8,128)(2,1)S(1)} %sum_parts.1), channel_id=1, replica_groups={{0,2,8,10,21,23,29,31,64,66,72,74,85,87,93,95},{4,6,12,14,17,19,25,27,6..., dimensions={0} | all-to-all | bytes 1114112 | tf_op jit(solution)/shard_map/all_to_all | solution.py:640
  59.1 3.4 %collective-permute-start = (bf16[16,136,128]{2,1,0:T(8,128)(2,1)S(1)}, bf16[16,136,128]{2,1,0:T(8,128)(2,1)S(1)}, u32[]{:S(2)}, u32[]{:S(2)}) collective-permute-start(bf16[16,136,128]{2,1,0:T(8,128)(2,1)S(1)} %all_to_all.10.near_ref), channel_id=1, source_target_pairs={{0,32},{32,0},{1,33},{33,1},{2,34},{34,2},{3,35},{35,3},{4,36},{36... | collective-permute-start | bytes 1671176 | tf_op jit(solution)/shard_map/ppermute | solution.py:644
  62.5 0.0 collective-permute-start.3
  62.5 0.3 collective-permute-start.2
  62.8 1.1 %collective-permute-start.1 = (bf16[16,136,128]{2,1,0:T(8,128)(2,1)S(1)}, bf16[16,136,128]{2,1,0:T(8,128)(2,1)S(1)}, u32[]{:S(2)}, u32[]{:S(2)}) collective-permute-start(bf16[16,136,128]{2,1,0:T(8,128)(2,1)S(1)} %all_to_all.10.near_ref), channel_id=1, source_target_pairs={{1,0},{2,1},{3,2},{0,3},{5,4},{6,5},{7,6},{4,7},{9,8},{10,9},{11,1... | collective-permute-start | bytes 1671176 | tf_op jit(solution)/shard_map/ppermute | solution.py:645
  63.9 0.1 pad_add_fusion.place_ref
  64.0 0.1 collective-permute-done.far_ref
  64.1 1.9 %place_own.1.refs_3_ = f32[128,16384]{1,0:T(8,128)} custom-call(s32[2]{0:T(128)S(1)} %pad_add_fusion.place_ref, bf16[16,136,128]{2,1,0:T(8,128)(2,1)S(1)} %all_to_all.10.near_ref, bf16[16,136,128]{2,1,0:T(8,128)(2,1)S(1)} %collective-permute-done.far_ref), custom_call_target="tpu_custom_call" | custom-call | bytes 6291456 | tf_op jit(solution)/shard_map/place_own/pallas_call | solution.py:654
  66.0 6.1 %collective-permute-done.3.refs_2_ = bf16[16,136,128]{2,1,0:T(8,128)(2,1)S(1)} collective-permute-done((bf16[16,136,128]{2,1,0:T(8,128)(2,1)S(1)}, bf16[16,136,128]{2,1,0:T(8,128)(2,1)S(1)}, u32[]{:S(2)}, u32[]{:S(2)}) %collective-permute-start.3) | collective-permute-done | bytes 557088 | tf_op jit(solution)/shard_map/ppermute | solution.py:645
  72.1 0.0 collective-permute-done.2.refs_1_
  72.1 0.3 collective-permute-done.1.refs_0_
  72.4 1.4 %collective-permute-start.4 = (bf16[16,136,128]{2,1,0:T(8,128)(2,1)S(1)}, bf16[16,136,128]{2,1,0:T(8,128)(2,1)S(1)}, u32[]{:S(2)}, u32[]{:S(2)}) collective-permute-start(bf16[16,136,128]{2,1,0:T(8,128)(2,1)S(1)} %collective-permute-done.1.refs_0_), channel_id=1, source_target_pairs={{0,32},{32,0},{1,33},{33,1},{2,34},{34,2},{3,35},{35,3},{4,36},{36... | collective-permute-start | bytes 1671176 | tf_op jit(solution)/shard_map/ppermute | solution.py:665
  73.8 0.0 collective-permute-start.5
  73.8 0.5 collective-permute-start.6
  74.3 2.3 %place_rest.1.refs_6_ = f32[128,16384]{1,0:T(8,128)} custom-call(s32[2]{0:T(128)S(1)} %pad_add_fusion.place_ref, bf16[16,136,128]{2,1,0:T(8,128)(2,1)S(1)} %collective-permute-done.1.refs_0_, bf16[16,136,128]{2,1,0:T(8,128)(2,1)S(1)} %collective-permute-done.2.refs_1_, ...), custom_call_target="tpu_custom_call", output_to_operand_aliasing={{}: (4, {})} | custom-call | bytes 6291456 | tf_op jit(solution)/shard_map/place_rest/pallas_call | solution.py:666
  76.6 0.0 collective-permute-done.4.refs_3_
  76.7 0.0 collective-permute-done.5.refs_4_
  76.7 0.3 collective-permute-done.6.refs_5_
  77.0 2.5 %place_last.1 = (f32[128,16384]{1,0:T(8,128)}, f32[128,128]{1,0:T(8,128)}, f32[128,384]{1,0:T(8,128)}, f32[128,384]{1,0:T(8,128)}, f32[16,128]{1,0:T(8,128)}, /*...) custom-call(s32[2]{0:T(128)S(1)} %pad_add_fusion.place_ref, ...), custom_call_target="tpu_custom_call", output_to_operand_aliasing={{0}: (9, {})} | custom-call | bytes 6291456 | tf_op jit(solution)/shard_map/place_last/pallas_call | solution.py:687
Async XLA Ops:
  14.9 25.4 %all-to-all-start = ((bf16[32,136,128]{2,1,0:T(8,128)(2,1)}), bf16[32,136,128]{2,1,0:T(8,128)(2,1)S(1)}, u32[]{:S(2)}, u32[]{:S(2)}) async-start(bf16[32,136,128]{2,1,0:T(8,128)(2,1)} %get-tuple-element.30), calls=%async_computation | async-start | bytes 2228224 | tf_op jit(solution)/shard_map/all_to_all | solution.py:625
  24.1 2.2 %copy-start = (bf16[128,16384]{1,0:T(8,128)(2,1)S(1)}, bf16[128,16384]{1,0:T(8,128)(2,1)}, u32[]{:S(2)}) copy-start(bf16[128,16384]{1,0:T(8,128)(2,1)} %w_ref.1) | copy-start | bytes 12582916
  26.3 0.9 %copy-start.1 = (bf16[1024,128]{1,0:T(8,128)(2,1)S(1)}, bf16[1024,128]{1,0:T(8,128)(2,1)}, u32[]{:S(2)}) copy-start(bf16[1024,128]{1,0:T(8,128)(2,1)} %get-tuple-element.33.pairs_ref) | copy-start | bytes 786436
  27.3 0.8 copy-start.2
  28.0 0.7 copy-start.3
  59.1 4.9 %collective-permute-start = (bf16[16,136,128]{2,1,0:T(8,128)(2,1)S(1)}, bf16[16,136,128]{2,1,0:T(8,128)(2,1)S(1)}, u32[]{:S(2)}, u32[]{:S(2)}) collective-permute-start(bf16[16,136,128]{2,1,0:T(8,128)(2,1)S(1)} %all_to_all.10.near_ref), channel_id=1, source_target_pairs={{0,32},{32,0},{1,33},{33,1},{2,34},{34,2},{3,35},{35,3},{4,36},{36... | collective-permute-start | bytes 1671176 | tf_op jit(solution)/shard_map/ppermute | solution.py:644
  62.5 9.6 %collective-permute-start.3 = (bf16[16,136,128]{2,1,0:T(8,128)(2,1)S(1)}, bf16[16,136,128]{2,1,0:T(8,128)(2,1)S(1)}, u32[]{:S(2)}, u32[]{:S(2)}) collective-permute-start(bf16[16,136,128]{2,1,0:T(8,128)(2,1)S(1)} %all_to_all.10.near_ref), channel_id=1, source_target_pairs={{16,0},{17,1},{18,2},{19,3},{20,4},{21,5},{22,6},{23,7},{24,8},{25... | collective-permute-start | bytes 1671176 | tf_op jit(solution)/shard_map/ppermute | solution.py:645
  62.5 9.6 %collective-permute-start.2 = (bf16[16,136,128]{2,1,0:T(8,128)(2,1)S(1)}, bf16[16,136,128]{2,1,0:T(8,128)(2,1)S(1)}, u32[]{:S(2)}, u32[]{:S(2)}) collective-permute-start(bf16[16,136,128]{2,1,0:T(8,128)(2,1)S(1)} %all_to_all.10.near_ref), channel_id=1, source_target_pairs={{4,0},{5,1},{6,2},{7,3},{8,4},{9,5},{10,6},{11,7},{12,8},{13,9},{1... | collective-permute-start | bytes 1671176 | tf_op jit(solution)/shard_map/ppermute | solution.py:645
  62.8 9.6 %collective-permute-start.1 = (bf16[16,136,128]{2,1,0:T(8,128)(2,1)S(1)}, bf16[16,136,128]{2,1,0:T(8,128)(2,1)S(1)}, u32[]{:S(2)}, u32[]{:S(2)}) collective-permute-start(bf16[16,136,128]{2,1,0:T(8,128)(2,1)S(1)} %all_to_all.10.near_ref), channel_id=1, source_target_pairs={{1,0},{2,1},{3,2},{0,3},{5,4},{6,5},{7,6},{4,7},{9,8},{10,9},{11,1... | collective-permute-start | bytes 1671176 | tf_op jit(solution)/shard_map/ppermute | solution.py:645
  72.4 4.2 %collective-permute-start.4 = (bf16[16,136,128]{2,1,0:T(8,128)(2,1)S(1)}, bf16[16,136,128]{2,1,0:T(8,128)(2,1)S(1)}, u32[]{:S(2)}, u32[]{:S(2)}) collective-permute-start(bf16[16,136,128]{2,1,0:T(8,128)(2,1)S(1)} %collective-permute-done.1.refs_0_), channel_id=1, source_target_pairs={{0,32},{32,0},{1,33},{33,1},{2,34},{34,2},{3,35},{35,3},{4,36},{36... | collective-permute-start | bytes 1671176 | tf_op jit(solution)/shard_map/ppermute | solution.py:665
  73.8 2.8 %collective-permute-start.5 = (bf16[16,136,128]{2,1,0:T(8,128)(2,1)S(1)}, bf16[16,136,128]{2,1,0:T(8,128)(2,1)S(1)}, u32[]{:S(2)}, u32[]{:S(2)}) collective-permute-start(bf16[16,136,128]{2,1,0:T(8,128)(2,1)S(1)} %collective-permute-done.2.refs_1_), channel_id=1, source_target_pairs={{0,32},{32,0},{1,33},{33,1},{2,34},{34,2},{3,35},{35,3},{4,36},{36... | collective-permute-start | bytes 1671176 | tf_op jit(solution)/shard_map/ppermute | solution.py:665
  73.8 3.2 %collective-permute-start.6 = (bf16[16,136,128]{2,1,0:T(8,128)(2,1)S(1)}, bf16[16,136,128]{2,1,0:T(8,128)(2,1)S(1)}, u32[]{:S(2)}, u32[]{:S(2)}) collective-permute-start(bf16[16,136,128]{2,1,0:T(8,128)(2,1)S(1)} %collective-permute-done.3.refs_2_), channel_id=1, source_target_pairs={{0,32},{32,0},{1,33},{33,1},{2,34},{34,2},{3,35},{35,3},{4,36},{36... | collective-permute-start | bytes 1671176 | tf_op jit(solution)/shard_map/ppermute | solution.py:665

commit v5 on v4

--- a/solution.py
+++ b/solution.py
@@ -102,7 +102,7 @@
     return tn(features, w_edge_in) + b_edge_in
 
 
-def local_kernel(sect_ref, *refs):
+def local_kernel(*refs):
     ins, refs = refs[:14], refs[14:]
     (send_ref, final_ref, base_ref, grad_t_ref, pairs_out_ref), refs = refs[:5], refs[5:]
     held, refs = refs[:14], refs[14:]
@@ -123,7 +123,7 @@
         cot_ref,
         w_ref,
     ) = held
-    sect = sect_ref[0]
+    sect = section()
     chunk = H * H // W_PARTS
     copies = [
         pltpu.make_async_copy(ins[at], held[at], sems.at[at]) for at in range(13)
@@ -400,8 +400,8 @@
         out_ref[at] = piece
 
 
-def states_kernel(sect_ref, base_ref, grad_t_ref, pairs_ref, w_ref, out_ref, d_all, rows_scr):
-    sect = sect_ref[0]
+def states_kernel(base_ref, grad_t_ref, pairs_ref, w_ref, out_ref, d_all, rows_scr):
+    sect = section()
     rows_scr[...] = grad_t_ref[...].astype(F32).T
     own = rows_scr[pl.ds(pl.multiple_of(sect * ATOMS, ATOMS), ATOMS), :]
     left = own.T.astype(BF)
@@ -433,10 +433,10 @@
     out_ref[...] = lax.fori_loop(0, 32, back_body, base_ref[...], unroll=True)
 
 
-def place_rows(place_ref, parts, out_hbm, stage, sem):
+def place_rows(parts, out_hbm, stage, sem):
     copies = []
     for part, (ref, other_core, change) in enumerate(parts):
-        core, kind = place_of(place_ref, other_core, change)
+        core, kind = place_of(other_core, change)
         for half in range(2):
             at_col = ((half * 2 + core) * GROUP + kind * CLASS) * H
             low = (part * 2 + half) * CLASS * H
@@ -457,37 +457,41 @@
     return copies
 
 
-def place_of(place_ref, other_core, change):
-    core, kind = place_ref[0], place_ref[1]
+def place_of(other_core, change):
+    core, dp = lax.axis_index("core"), lax.axis_index("dp")
+    z = jnp.right_shift(dp, 4)
+    kind = jnp.bitwise_and(dp + z, 1) * 2 + jnp.bitwise_and(jnp.right_shift(dp, 2) + z, 1)
     return (1 - core if other_core else core), jnp.bitwise_xor(kind, change)
 
 
+def section():
+    return lax.axis_index("zh") * 2 + lax.axis_index("core")
+
+
 CHANGES = (2, 1, 3)
 
 
-def place_own(place_ref, near_ref, far_ref, out_hbm, stage, sems):
-    parts = [(near_ref, False, 0), (far_ref, True, 0)]
-    for copy in place_rows(place_ref, parts, out_hbm, stage, sems):
+OWN_PARTS = ((False, 0), (True, 0))
+REST = tuple((False, change) for change in CHANGES)
+FAR_REST = tuple((True, change) for change in CHANGES)
+
+
+def place_some(kinds, first, *refs):
+    count = len(kinds)
+    out_hbm, stage, sems = refs[count + (0 if first else 1) :]
+    parts = [(ref,) + kind for ref, kind in zip(refs, kinds)]
+    for copy in place_rows(parts, out_hbm, stage, sems):
         copy.wait()
 
 
-def place_rest(place_ref, *refs):
-    out_hbm, stage, sems = refs[AXES + 1 :]
-    parts = [(ref, False, change) for ref, change in zip(refs, CHANGES)]
-    for copy in place_rows(place_ref, parts, out_hbm, stage, sems):
-        copy.wait()
-
-
-def place_last(place_ref, near_ref, far_ref, *refs):
-    rest, far_rest, refs = refs[:AXES], refs[AXES : 2 * AXES], refs[2 * AXES + 1 :]
+def place_last(*refs):
+    blocks, refs = refs[:8], refs[9:]
     out_hbm, *ends = refs[:8]
     stage, sems, small, gb, gi, gh, ge, be, bi, bh, end_sems = refs[8:]
-    own = [(near_ref, False, 0), (far_ref, True, 0)]
-    own += [(ref, False, change) for ref, change in zip(rest, CHANGES)]
-    last = [(ref, True, change) for ref, change in zip(far_rest, CHANGES)]
-    copies = place_rows(place_ref, last, out_hbm, stage, sems)
-    for ref, other_core, change in own + last:
-        core, kind = place_of(place_ref, other_core, change)
+    blocks = [(ref,) + kind for ref, kind in zip(blocks, OWN_PARTS + REST + FAR_REST)]
+    copies = place_rows(blocks[6:], out_hbm, stage, sems)
+    for ref, other_core, change in blocks:
+        core, kind = place_of(other_core, change)
         for at in range(2 * CLASS):
             block = ((at // CLASS) * 2 + core) * GROUP + kind * CLASS + at % CLASS
             row = pl.multiple_of(block * SMALL, SMALL)
@@ -518,14 +522,13 @@
 
 
 VMEM_SPEC = pl.BlockSpec(memory_space=pltpu.VMEM)
-SMEM_SPEC = pl.BlockSpec(memory_space=pltpu.SMEM)
 ANY_SPEC = pl.BlockSpec(memory_space=pl.ANY)
 BIG = 60 * 2**20
 LOW = 8 * 2**20
 shape = jax.ShapeDtypeStruct
 
 
-def run_layers(sect, operands):
+def run_layers(operands):
     return pl.pallas_call(
         local_kernel,
         out_shape=(
@@ -535,7 +538,7 @@
             shape((H, NODES), BF),
             shape((PAIRS, H), BF),
         ),
-        in_specs=[SMEM_SPEC] + [ANY_SPEC] * 14,
+        in_specs=[ANY_SPEC] * 14,
         out_specs=(VMEM_SPEC,) * 5,
         scratch_shapes=[pltpu.VMEM(v.shape, v.dtype) for v in operands]
         + [
@@ -552,7 +555,7 @@
         ],
         compiler_params=pltpu.CompilerParams(vmem_limit_bytes=BIG),
         name="layers",
-    )(sect, *operands)
+    )(*operands)
 
 
 def neighbours(axis):
@@ -589,12 +592,6 @@
     b_hidden,
     cotangent,
 ):
-    core = lax.axis_index("core").astype(jnp.int32)
-    sect = (lax.axis_index("zh") * 2 + core).astype(jnp.int32)
-    sect = sect.reshape(1)
-    dp = lax.axis_index("dp").astype(jnp.int32)
-    z = dp >> 4
-    place = jnp.stack([core, ((dp + z) & 1) * 2 + (((dp >> 2) + z) & 1)])
     operands = [v.reshape(8, 128) for v in (edge_source, edge_target, edge_live)] + [
         edge_features,
         w_edge_in,
@@ -609,11 +606,11 @@
         w_edge_out,
     ]
 
-    send, final, base, grad_t, pairs = run_layers(sect, operands)
+    send, final, base, grad_t, pairs = run_layers(operands)
     grad_states = pl.pallas_call(
         states_kernel,
         out_shape=shape((ATOMS, H), F32),
-        in_specs=[SMEM_SPEC] + [VMEM_SPEC] * 4,
+        in_specs=[VMEM_SPEC] * 4,
         out_specs=VMEM_SPEC,
         scratch_shapes=[pltpu.VMEM(((H + 1) * (ATOMS + 1), H), F32), pltpu.VMEM((NODES, H), F32)],
         compiler_params=pltpu.CompilerParams(vmem_limit_bytes=LOW),
@@ -621,7 +618,7 @@
             flops=2 * ATOMS * H * H * H, bytes_accessed=2 * H * H * H, transcendentals=0
         ),
         name="states_back",
-    )(sect, base, grad_t, pairs, w_edge_out)
+    )(base, grad_t, pairs, w_edge_out)
     got = lax.all_to_all(send, "dp", split_axis=0, concat_axis=0)
     got, grad_states = lax.optimization_barrier((got, grad_states))
     piece = pl.pallas_call(
@@ -651,29 +648,32 @@
         return [pltpu.VMEM((H, parts * 2 * CLASS * H), F32), pltpu.SemaphoreType.DMA((2 * parts,))]
 
     whole = shape((H, H * H), F32)
-    out = pl.pallas_call(
-        place_own,
-        out_shape=whole,
-        in_specs=[SMEM_SPEC, VMEM_SPEC, VMEM_SPEC],
-        out_specs=ANY_SPEC,
-        scratch_shapes=stage(2),
-        compiler_params=params,
-        cost_estimate=cost,
-        name="place_own",
-    )(place, near, far)
-    rest, out = lax.optimization_barrier((rest, out))
-    far_rest = [lax.ppermute(part, "core", swap) for part in rest]
-    out = pl.pallas_call(
-        place_rest,
-        out_shape=whole,
-        in_specs=[SMEM_SPEC] + [VMEM_SPEC] * AXES + [ANY_SPEC],
-        out_specs=ANY_SPEC,
-        scratch_shapes=stage(AXES),
-        input_output_aliases={AXES + 1: 0},
-        compiler_params=params,
-        cost_estimate=cost,
-        name="place_rest",
-    )(place, *rest, out)
+
+    def place_blocks(kinds, blocks, out, name):
+        count = len(kinds)
+        first = out is None
+        return pl.pallas_call(
+            functools.partial(place_some, kinds, first),
+            out_shape=whole,
+            in_specs=[VMEM_SPEC] * count + ([] if first else [ANY_SPEC]),
+            out_specs=ANY_SPEC,
+            scratch_shapes=stage(count),
+            input_output_aliases={} if first else {count: 0},
+            compiler_params=params,
+            cost_estimate=cost,
+            name=name,
+        )(*blocks, *([] if first else [out]))
+
+    out = place_blocks(OWN_PARTS, (near, far), None, "place_own")
+    rest[0], out = lax.optimization_barrier((rest[0], out))
+    far_rest = [lax.ppermute(rest[0], "core", swap)]
+    out = place_blocks(REST[:1], rest[:1], out, "place_x")
+    for axis in (1, 2):
+        rest[axis], out = lax.optimization_barrier((rest[axis], out))
+        far_rest.append(lax.ppermute(rest[axis], "core", swap))
+    out = place_blocks(
+        REST[1:] + FAR_REST[:1], (rest[1], rest[2], far_rest[0]), out, "place_y_z_far_x"
+    )
     ends = [
         shape((H, H), F32),
         shape((H, 3 * H), F32),
@@ -687,17 +687,17 @@
         pl.pallas_call(
             place_last,
             out_shape=[whole] + ends,
-            in_specs=[SMEM_SPEC] + [VMEM_SPEC] * (2 * AXES + 2) + [ANY_SPEC],
+            in_specs=[VMEM_SPEC] * (2 * AXES + 2) + [ANY_SPEC],
             out_specs=[ANY_SPEC] * 8,
-            scratch_shapes=stage(AXES)
+            scratch_shapes=stage(2)
             + [pltpu.VMEM((MB * GROUP * SMALL, H), F32)]
             + [pltpu.VMEM(v.shape, v.dtype) for v in ends]
             + [pltpu.SemaphoreType.DMA((7,))],
-            input_output_aliases={2 * AXES + 3: 0},
+            input_output_aliases={2 * AXES + 2: 0},
             compiler_params=params,
             cost_estimate=cost,
             name="place_last",
-        )(place, near, far, *rest, *far_rest, out)
+        )(near, far, *rest, *far_rest, out)
     )
     return (
         final,

time: 80.2 us -> 78.5 us (0.979)
  starting transfers between devices: 16 us -> 14.5 us
  Pallas kernels: 23 us -> 22.1 us
    ppermute x3, starting transfers between devices: 1.94 us -> 0.51 us  [the longest x2 0.51 us: local(): far_rest.append(lax.ppermute(rest[axis], 'core', swap))]
    pallas_call x3 -> x4, Pallas kernels: 6.77 us -> 5.83 us  [the longest x3 4.2 us: place_blocks(): pl.pallas_call(functools.partial(place_some, kinds, first), out_shape=who...]
where the time goes in v5:
time: 78.5 us; the launch traced here: 78 us
  Pallas kernels  22.1 us (28%)
  blocking collectives  18.6 us (24%)
  waiting for transfers between devices  17.3 us (22%)
  starting transfers between devices  14.5 us (18%)
  local copies, waits for them, and re-layouts  4.61 us (6%)
  between operations  0.89 us (1%)
    all_to_all x1, blocking collectives, local(): lax.all_to_all(piece, ('zh', 'core', 'dp'), split_axis=0, concat_axis=0,...  18.6 us
    pallas_call x1, Pallas kernels, run_layers(): pl.pallas_call(local_kernel, out_shape=(shape((GROUP, ROWS, H), BF), shap...  14.2 us
    all_to_all x1, waiting for transfers between devices, local(): got = lax.all_to_all(send, 'dp', split_axis=0, concat_axis=0)  9.74 us
    all_to_all x1, starting transfers between devices, local(): got = lax.all_to_all(send, 'dp', split_axis=0, concat_axis=0)  9.23 us
    ppermute x3, waiting for transfers between devices, local(): lax.ppermute(near, ('zh', 'core', 'dp'), neighbours(axis))  6.97 us
    unnamed x8, local copies, waits for them, and re-layouts  4.61 us
    pallas_call x3, Pallas kernels, place_blocks(): pl.pallas_call(functools.partial(place_some, kinds, first), out_shape=who...  4.2 us
    ppermute x1, starting transfers between devices, local(): far = lax.ppermute(near, 'core', swap)  3.36 us
  transfers between devices with their start and end apart: 8, of which 5 were waited for; matrix products, arithmetic and copies ran while one was open for 0% of the time, Pallas kernels for 8%

profile of v5, /device:TPU:1, one launch (start us, length us, event | category | flops | bytes accessed | tf_op | source)
XLA Modules:
  0.0 78.0 jit_solution(5308263594553648414)
XLA Ops:
  0.6 14.2 %layers.1 = (bf16[32,136,128]{2,1,0:T(8,128)(2,1)}, f32[32,128]{1,0:T(8,128)}, f32[32,128]{1,0:T(8,128)}, bf16[128,128]{1,0:T(8,128)(2,1)}, bf16[1024,128]{1,0:T(8,128)(2,1)}) custom-call(s32[8,128]{1,0:T(8,128)} %bitcast.12, s32[8,128]{1,0:T(8,128)} %bitcast.13, s32[8,128]{1,0:T(8,128)} %bitcast.14, bf16[16,1024]{1,0:T(8,128)(2,1)} %refs_3_.1, ...), custom_call_target="tpu_custom_call" | custom-call | tf_op jit(solution)/shard_map/layers/pallas_call | solution.py:532
  14.9 9.2 %all-to-all-start = ((bf16[32,136,128]{2,1,0:T(8,128)(2,1)}), bf16[32,136,128]{2,1,0:T(8,128)(2,1)S(1)}, u32[]{:S(2)}, u32[]{:S(2)}) async-start(bf16[32,136,128]{2,1,0:T(8,128)(2,1)} %get-tuple-element.32), calls=%async_computation | async-start | bytes 2228224 | tf_op jit(solution)/shard_map/all_to_all | solution.py:622
  24.1 0.0 copy-start
  24.1 2.2 %copy-done = bf16[128,16384]{1,0:T(8,128)(2,1)S(1)} copy-done((bf16[128,16384]{1,0:T(8,128)(2,1)S(1)}, bf16[128,16384]{1,0:T(8,128)(2,1)}, u32[]{:S(2)}) %copy-start) | copy-done | bytes 4194328
  26.3 0.0 copy-start.1
  26.3 0.9 %copy-done.1 = bf16[1024,128]{1,0:T(8,128)(2,1)S(1)} copy-done((bf16[1024,128]{1,0:T(8,128)(2,1)S(1)}, bf16[1024,128]{1,0:T(8,128)(2,1)}, u32[]{:S(2)}) %copy-start.1) | copy-done | bytes 262168
  27.2 0.0 copy-start.2
  27.2 0.8 copy-done.2
  28.0 0.0 copy-start.3
  28.0 0.7 copy-done.3
  28.7 1.8 %states_back.1 = f32[32,128]{1,0:T(8,128)} custom-call(f32[32,128]{1,0:T(8,128)S(1)} %copy-done.3, bf16[128,128]{1,0:T(8,128)(2,1)S(1)} %copy-done.2, bf16[1024,128]{1,0:T(8,128)(2,1)S(1)} %copy-done.1, bf16[128,16384]{1,0:T(8,128)(2,1)S(1)} %copy-done), custom_call_target="tpu_custom_call" | custom-call | flops 134217728 | bytes 4194304 | tf_op jit(solution)/shard_map/states_back/pallas_call | solution.py:610
  30.5 9.7 %all-to-all-done.got_ref = bf16[32,136,128]{2,1,0:T(8,128)(2,1)S(1)} async-done(((bf16[32,136,128]{2,1,0:T(8,128)(2,1)}), bf16[32,136,128]{2,1,0:T(8,128)(2,1)S(1)}, u32[]{:S(2)}, u32[]{:S(2)}) %all-to-all-start) | async-done | bytes 1114144 | tf_op jit(solution)/shard_map/all_to_all | solution.py:622
  40.3 0.2 sum_parts.1
  40.5 18.6 %all_to_all.10.refs_0_ = bf16[16,136,128]{2,1,0:T(8,128)(2,1)S(1)} all-to-all(bf16[16,136,128]{2,1,0:T(8,128)(2,1)S(1)} %sum_parts.1), channel_id=1, replica_groups={{0,2,8,10,21,23,29,31,64,66,72,74,85,87,93,95},{4,6,12,14,17,19,25,27,6..., dimensions={0} | all-to-all | bytes 1114112 | tf_op jit(solution)/shard_map/all_to_all | solution.py:637
  59.1 3.4 %collective-permute-start = (bf16[16,136,128]{2,1,0:T(8,128)(2,1)S(1)}, bf16[16,136,128]{2,1,0:T(8,128)(2,1)S(1)}, u32[]{:S(2)}, u32[]{:S(2)}) collective-permute-start(bf16[16,136,128]{2,1,0:T(8,128)(2,1)S(1)} %all_to_all.10.refs_0_), channel_id=1, source_target_pairs={{0,32},{32,0},{1,33},{33,1},{2,34},{34,2},{3,35},{35,3},{4,36},{36... | collective-permute-start | bytes 1671176 | tf_op jit(solution)/shard_map/ppermute | solution.py:641
  62.5 0.5 collective-permute-start.1
  63.0 0.9 %collective-permute-start.2 = (bf16[16,136,128]{2,1,0:T(8,128)(2,1)S(1)}, bf16[16,136,128]{2,1,0:T(8,128)(2,1)S(1)}, u32[]{:S(2)}, u32[]{:S(2)}) collective-permute-start(bf16[16,136,128]{2,1,0:T(8,128)(2,1)S(1)} %all_to_all.10.refs_0_), channel_id=1, source_target_pairs={{4,0},{5,1},{6,2},{7,3},{8,4},{9,5},{10,6},{11,7},{12,8},{13,9},{1... | collective-permute-start | bytes 1671176 | tf_op jit(solution)/shard_map/ppermute | solution.py:642
  63.9 0.0 collective-permute-start.3
  63.9 0.2 collective-permute-done.refs_1_
  64.0 1.4 %place_own.1.refs_1_ = f32[128,16384]{1,0:T(8,128)} custom-call(bf16[16,136,128]{2,1,0:T(8,128)(2,1)S(1)} %all_to_all.10.refs_0_, bf16[16,136,128]{2,1,0:T(8,128)(2,1)S(1)} %collective-permute-done.refs_1_), custom_call_target="tpu_custom_call" | custom-call | bytes 6291456 | tf_op jit(solution)/shard_map/place_own/pallas_call | solution.py:655
  65.4 6.6 %collective-permute-done.1.refs_0_.refs_2_ = bf16[16,136,128]{2,1,0:T(8,128)(2,1)S(1)} collective-permute-done((bf16[16,136,128]{2,1,0:T(8,128)(2,1)S(1)}, bf16[16,136,128]{2,1,0:T(8,128)(2,1)S(1)}, u32[]{:S(2)}, u32[]{:S(2)}) %collective-permute-start.1) | collective-permute-done | bytes 557088 | tf_op jit(solution)/shard_map/ppermute | solution.py:642
  72.1 0.0 collective-permute-start.4
  72.1 1.0 %place_x.1.refs_3_ = f32[128,16384]{1,0:T(8,128)} custom-call(bf16[16,136,128]{2,1,0:T(8,128)(2,1)S(1)} %collective-permute-done.1.refs_0_.refs_2_, f32[128,16384]{1,0:T(8,128)} %place_own.1.refs_1_), custom_call_target="tpu_custom_call", output_to_operand_aliasing={{}: (1, {})} | custom-call | bytes 6291456 | tf_op jit(solution)/shard_map/place_x/pallas_call | solution.py:655
  73.1 0.0 collective-permute-done.2.refs_0_.refs_3_
  73.1 0.4 collective-permute-done.3.refs_1_.refs_4_
  73.5 0.2 collective-permute-start.6
  73.7 0.3 collective-permute-start.5
  74.0 0.0 collective-permute-done.4.refs_2_.refs_5_
  74.0 1.8 %place_y_z_far_x.1.refs_8_ = f32[128,16384]{1,0:T(8,128)} custom-call(bf16[16,136,128]{2,1,0:T(8,128)(2,1)S(1)} %collective-permute-done.2.refs_0_.refs_3_, bf16[16,136,128]{2,1,0:T(8,128)(2,1)S(1)} %collective-permute-done.3.refs_1_.refs_4_, bf16[16,136,128]{2,1,0:T(8,128)(2,1)S(1)} %collective-permute-done.4.refs_2_.refs_5_, ...), custom_call_target="tpu_custom_call", output_to_operand_aliasing={{}: (3, {})} | custom-call | bytes 6291456 | tf_op jit(solution)/shard_map/place_y_z_far_x/pallas_call | solution.py:655
  75.8 0.0 collective-permute-done.6.refs_7_
  75.8 0.4 collective-permute-done.5.refs_6_
  76.2 1.6 %place_last.1 = (f32[128,16384]{1,0:T(8,128)}, f32[128,128]{1,0:T(8,128)}, f32[128,384]{1,0:T(8,128)}, f32[128,384]{1,0:T(8,128)}, f32[16,128]{1,0:T(8,128)}, /*...) custom-call(bf16[16,136,128]{2,1,0:T(8,128)(2,1)S(1)} %all_to_all.10.refs_0_, ...), custom_call_target="tpu_custom_call", output_to_operand_aliasing={{0}: (8, {})} | custom-call | bytes 6291456 | tf_op jit(solution)/shard_map/place_last/pallas_call | solution.py:687
Async XLA Ops:
  14.9 25.4 %all-to-all-start = ((bf16[32,136,128]{2,1,0:T(8,128)(2,1)}), bf16[32,136,128]{2,1,0:T(8,128)(2,1)S(1)}, u32[]{:S(2)}, u32[]{:S(2)}) async-start(bf16[32,136,128]{2,1,0:T(8,128)(2,1)} %get-tuple-element.32), calls=%async_computation | async-start | bytes 2228224 | tf_op jit(solution)/shard_map/all_to_all | solution.py:622
  24.1 2.2 %copy-start = (bf16[128,16384]{1,0:T(8,128)(2,1)S(1)}, bf16[128,16384]{1,0:T(8,128)(2,1)}, u32[]{:S(2)}) copy-start(bf16[128,16384]{1,0:T(8,128)(2,1)} %w_ref.1) | copy-start | bytes 12582916
  26.3 0.9 %copy-start.1 = (bf16[1024,128]{1,0:T(8,128)(2,1)S(1)}, bf16[1024,128]{1,0:T(8,128)(2,1)}, u32[]{:S(2)}) copy-start(bf16[1024,128]{1,0:T(8,128)(2,1)} %get-tuple-element.35.pairs_ref) | copy-start | bytes 786436
  27.2 0.8 copy-start.2
  28.0 0.7 copy-start.3
  59.1 4.9 %collective-permute-start = (bf16[16,136,128]{2,1,0:T(8,128)(2,1)S(1)}, bf16[16,136,128]{2,1,0:T(8,128)(2,1)S(1)}, u32[]{:S(2)}, u32[]{:S(2)}) collective-permute-start(bf16[16,136,128]{2,1,0:T(8,128)(2,1)S(1)} %all_to_all.10.refs_0_), channel_id=1, source_target_pairs={{0,32},{32,0},{1,33},{33,1},{2,34},{34,2},{3,35},{35,3},{4,36},{36... | collective-permute-start | bytes 1671176 | tf_op jit(solution)/shard_map/ppermute | solution.py:641
  62.5 9.6 %collective-permute-start.1 = (bf16[16,136,128]{2,1,0:T(8,128)(2,1)S(1)}, bf16[16,136,128]{2,1,0:T(8,128)(2,1)S(1)}, u32[]{:S(2)}, u32[]{:S(2)}) collective-permute-start(bf16[16,136,128]{2,1,0:T(8,128)(2,1)S(1)} %all_to_all.10.refs_0_), channel_id=1, source_target_pairs={{1,0},{2,1},{3,2},{0,3},{5,4},{6,5},{7,6},{4,7},{9,8},{10,9},{11,1... | collective-permute-start | bytes 1671176 | tf_op jit(solution)/shard_map/ppermute | solution.py:642
  63.0 10.1 %collective-permute-start.2 = (bf16[16,136,128]{2,1,0:T(8,128)(2,1)S(1)}, bf16[16,136,128]{2,1,0:T(8,128)(2,1)S(1)}, u32[]{:S(2)}, u32[]{:S(2)}) collective-permute-start(bf16[16,136,128]{2,1,0:T(8,128)(2,1)S(1)} %all_to_all.10.refs_0_), channel_id=1, source_target_pairs={{4,0},{5,1},{6,2},{7,3},{8,4},{9,5},{10,6},{11,7},{12,8},{13,9},{1... | collective-permute-start | bytes 1671176 | tf_op jit(solution)/shard_map/ppermute | solution.py:642
  63.9 9.6 %collective-permute-start.3 = (bf16[16,136,128]{2,1,0:T(8,128)(2,1)S(1)}, bf16[16,136,128]{2,1,0:T(8,128)(2,1)S(1)}, u32[]{:S(2)}, u32[]{:S(2)}) collective-permute-start(bf16[16,136,128]{2,1,0:T(8,128)(2,1)S(1)} %all_to_all.10.refs_0_), channel_id=1, source_target_pairs={{16,0},{17,1},{18,2},{19,3},{20,4},{21,5},{22,6},{23,7},{24,8},{25... | collective-permute-start | bytes 1671176 | tf_op jit(solution)/shard_map/ppermute | solution.py:642
  72.1 2.0 %collective-permute-start.4 = (bf16[16,136,128]{2,1,0:T(8,128)(2,1)S(1)}, bf16[16,136,128]{2,1,0:T(8,128)(2,1)S(1)}, u32[]{:S(2)}, u32[]{:S(2)}) collective-permute-start(bf16[16,136,128]{2,1,0:T(8,128)(2,1)S(1)} %collective-permute-done.1.refs_0_.refs_2_), channel_id=1, source_target_pairs={{0,32},{32,0},{1,33},{33,1},{2,34},{34,2},{3,35},{35,3},{4,36},{36... | collective-permute-start | bytes 1671176 | tf_op jit(solution)/shard_map/ppermute | solution.py:669
  73.5 2.3 %collective-permute-start.6 = (bf16[16,136,128]{2,1,0:T(8,128)(2,1)S(1)}, bf16[16,136,128]{2,1,0:T(8,128)(2,1)S(1)}, u32[]{:S(2)}, u32[]{:S(2)}) collective-permute-start(bf16[16,136,128]{2,1,0:T(8,128)(2,1)S(1)} %collective-permute-done.3.refs_1_.refs_4_), channel_id=1, source_target_pairs={{0,32},{32,0},{1,33},{33,1},{2,34},{34,2},{3,35},{35,3},{4,36},{36... | collective-permute-start | bytes 1671176 | tf_op jit(solution)/shard_map/ppermute | solution.py:673
  73.7 2.5 %collective-permute-start.5 = (bf16[16,136,128]{2,1,0:T(8,128)(2,1)S(1)}, bf16[16,136,128]{2,1,0:T(8,128)(2,1)S(1)}, u32[]{:S(2)}, u32[]{:S(2)}) collective-permute-start(bf16[16,136,128]{2,1,0:T(8,128)(2,1)S(1)} %collective-permute-done.2.refs_0_.refs_3_), channel_id=1, source_target_pairs={{0,32},{32,0},{1,33},{33,1},{2,34},{34,2},{3,35},{35,3},{4,36},{36... | collective-permute-start | bytes 1671176 | tf_op jit(solution)/shard_map/ppermute | solution.py:673

commit v6 on v5

--- a/solution.py
+++ b/solution.py
@@ -16,7 +16,7 @@
 PAIRS = ATOMS * ATOMS
 OWN = H // MB
 GAP = 129
-ROWS = 136
+ROWS = 144
 SMALL = 8
 GROUP = 32
 CLASS = 8
@@ -381,7 +381,9 @@
             row = 241 + at * 3 + part
             small_scr[row : row + 1, :] = jnp.sum(rows_scr[own_rows, :], axis=0, keepdims=True)
     for at in range(GROUP):
-        send_ref[DP_AT[at], H:ROWS, :] = small_scr[at * SMALL : (at + 1) * SMALL, :].astype(BF)
+        high, low = halves(small_scr[at * SMALL : (at + 1) * SMALL, :])
+        both = jnp.concatenate([high.astype(F32), low.astype(F32)], axis=0)
+        send_ref[DP_AT[at], H:ROWS, :] = both.astype(BF)
 
     rows_scr[...] = back_zero + fine(nn, nn(adj_t, g_one), b_mat)
     base_ref[...] = rows_scr[own_rows, :]
@@ -394,7 +396,8 @@
         return total + got_ref[at].astype(F32)
 
     total = lax.fori_loop(1, GROUP, body, got_ref[0].astype(F32), unroll=True)
-    piece = jnp.concatenate([total[:H].T, total[H:]], axis=0).astype(BF)
+    high, low = halves(total[H : H + SMALL] + total[H + SMALL :])
+    piece = jnp.concatenate([total[:H].T, high.astype(F32), low.astype(F32)], axis=0).astype(BF)
 
     for at in range(2 * CLASS):
         out_ref[at] = piece
@@ -495,7 +498,8 @@
         for at in range(2 * CLASS):
             block = ((at // CLASS) * 2 + core) * GROUP + kind * CLASS + at % CLASS
             row = pl.multiple_of(block * SMALL, SMALL)
-            small[pl.ds(row, SMALL), :] = ref[at, H:ROWS, :].astype(F32)
+            both = ref[at, H:ROWS, :].astype(F32)
+            small[pl.ds(row, SMALL), :] = both[:SMALL] + both[SMALL:]
     misc = jnp.zeros((32, H), F32)
     for sect in range(MB):
         base = sect * GROUP * SMALL

time: 78.5 us -> 80 us (1.019)
  waiting for transfers between devices: 17.3 us -> 18.4 us
  transfers between devices with their start and end apart: 8 -> 8, of which waited for: 5 -> 6; matrix products, arithmetic and copies ran while one was open for 0% -> 0% of each run, Pallas kernels for 8% -> 8%
where the time goes in v6:
time: 80 us; the launch traced here: 79.5 us
  Pallas kernels  22.1 us (28%)
  blocking collectives  19 us (24%)
  waiting for transfers between devices  18.4 us (23%)
  starting transfers between devices  14.5 us (18%)
  local copies, waits for them, and re-layouts  4.61 us (6%)
  between operations  0.89 us (1%)
    all_to_all x1, blocking collectives, local(): lax.all_to_all(piece, ('zh', 'core', 'dp'), split_axis=0, concat_axis=0,...  19 us
    pallas_call x1, Pallas kernels, run_layers(): pl.pallas_call(local_kernel, out_shape=(shape((GROUP, ROWS, H), BF), shap...  14.2 us
    all_to_all x1, waiting for transfers between devices, local(): got = lax.all_to_all(send, 'dp', split_axis=0, concat_axis=0)  10.4 us
    all_to_all x1, starting transfers between devices, local(): got = lax.all_to_all(send, 'dp', split_axis=0, concat_axis=0)  9.23 us
    ppermute x3, waiting for transfers between devices, local(): lax.ppermute(near, ('zh', 'core', 'dp'), neighbours(axis))  7.27 us
    unnamed x8, local copies, waits for them, and re-layouts  4.61 us
    pallas_call x3, Pallas kernels, place_blocks(): pl.pallas_call(functools.partial(place_some, kinds, first), out_shape=who...  4.19 us
    ppermute x1, starting transfers between devices, local(): far = lax.ppermute(near, 'core', swap)  3.3 us
  transfers between devices with their start and end apart: 8, of which 6 were waited for; matrix products, arithmetic and copies ran while one was open for 0% of the time, Pallas kernels for 8%

profile of v6, /device:TPU:1, one launch (start us, length us, event | category | flops | bytes accessed | tf_op | source)
XLA Modules:
  0.0 79.5 jit_solution(15133379162794364636)
XLA Ops:
  0.6 14.2 %layers.1 = (bf16[32,144,128]{2,1,0:T(8,128)(2,1)}, f32[32,128]{1,0:T(8,128)}, f32[32,128]{1,0:T(8,128)}, bf16[128,128]{1,0:T(8,128)(2,1)}, bf16[1024,128]{1,0:T(8,128)(2,1)}) custom-call(s32[8,128]{1,0:T(8,128)} %bitcast.12, s32[8,128]{1,0:T(8,128)} %bitcast.13, s32[8,128]{1,0:T(8,128)} %bitcast.14, bf16[16,1024]{1,0:T(8,128)(2,1)} %refs_3_.1, ...), custom_call_target="tpu_custom_call" | custom-call | tf_op jit(solution)/shard_map/layers/pallas_call | solution.py:536
  14.9 9.2 %all-to-all-start = ((bf16[32,144,128]{2,1,0:T(8,128)(2,1)}), bf16[32,144,128]{2,1,0:T(8,128)(2,1)S(1)}, u32[]{:S(2)}, u32[]{:S(2)}) async-start(bf16[32,144,128]{2,1,0:T(8,128)(2,1)} %get-tuple-element.32), calls=%async_computation | async-start | bytes 2359296 | tf_op jit(solution)/shard_map/all_to_all | solution.py:626
  24.1 0.0 copy-start
  24.1 2.2 %copy-done = bf16[128,16384]{1,0:T(8,128)(2,1)S(1)} copy-done((bf16[128,16384]{1,0:T(8,128)(2,1)S(1)}, bf16[128,16384]{1,0:T(8,128)(2,1)}, u32[]{:S(2)}) %copy-start) | copy-done | bytes 4194328
  26.3 0.0 copy-start.1
  26.3 0.9 %copy-done.1 = bf16[1024,128]{1,0:T(8,128)(2,1)S(1)} copy-done((bf16[1024,128]{1,0:T(8,128)(2,1)S(1)}, bf16[1024,128]{1,0:T(8,128)(2,1)}, u32[]{:S(2)}) %copy-start.1) | copy-done | bytes 262168
  27.3 0.0 copy-start.2
  27.3 0.8 copy-done.2
  28.0 0.0 copy-start.3
  28.0 0.7 copy-done.3
  28.8 1.8 %states_back.1 = f32[32,128]{1,0:T(8,128)} custom-call(f32[32,128]{1,0:T(8,128)S(1)} %copy-done.3, bf16[128,128]{1,0:T(8,128)(2,1)S(1)} %copy-done.2, bf16[1024,128]{1,0:T(8,128)(2,1)S(1)} %copy-done.1, bf16[128,16384]{1,0:T(8,128)(2,1)S(1)} %copy-done), custom_call_target="tpu_custom_call" | custom-call | flops 134217728 | bytes 4194304 | tf_op jit(solution)/shard_map/states_back/pallas_call | solution.py:614
  30.6 10.4 %all-to-all-done.got_ref = bf16[32,144,128]{2,1,0:T(8,128)(2,1)S(1)} async-done(((bf16[32,144,128]{2,1,0:T(8,128)(2,1)}), bf16[32,144,128]{2,1,0:T(8,128)(2,1)S(1)}, u32[]{:S(2)}, u32[]{:S(2)}) %all-to-all-start) | async-done | bytes 1179680 | tf_op jit(solution)/shard_map/all_to_all | solution.py:626
  40.9 0.2 sum_parts.1
  41.2 19.0 %all_to_all.10.refs_0_ = bf16[16,144,128]{2,1,0:T(8,128)(2,1)S(1)} all-to-all(bf16[16,144,128]{2,1,0:T(8,128)(2,1)S(1)} %sum_parts.1), channel_id=1, replica_groups={{0,2,8,10,21,23,29,31,64,66,72,74,85,87,93,95},{4,6,12,14,17,19,25,27,6..., dimensions={0} | all-to-all | bytes 1179648 | tf_op jit(solution)/shard_map/all_to_all | solution.py:641
  60.2 3.3 %collective-permute-start = (bf16[16,144,128]{2,1,0:T(8,128)(2,1)S(1)}, bf16[16,144,128]{2,1,0:T(8,128)(2,1)S(1)}, u32[]{:S(2)}, u32[]{:S(2)}) collective-permute-start(bf16[16,144,128]{2,1,0:T(8,128)(2,1)S(1)} %all_to_all.10.refs_0_), channel_id=1, source_target_pairs={{0,32},{32,0},{1,33},{33,1},{2,34},{34,2},{3,35},{35,3},{4,36},{36... | collective-permute-start | bytes 1769480 | tf_op jit(solution)/shard_map/ppermute | solution.py:645
  63.5 0.4 collective-permute-start.1
  63.9 1.1 %collective-permute-start.2 = (bf16[16,144,128]{2,1,0:T(8,128)(2,1)S(1)}, bf16[16,144,128]{2,1,0:T(8,128)(2,1)S(1)}, u32[]{:S(2)}, u32[]{:S(2)}) collective-permute-start(bf16[16,144,128]{2,1,0:T(8,128)(2,1)S(1)} %all_to_all.10.refs_0_), channel_id=1, source_target_pairs={{4,0},{5,1},{6,2},{7,3},{8,4},{9,5},{10,6},{11,7},{12,8},{13,9},{1... | collective-permute-start | bytes 1769480 | tf_op jit(solution)/shard_map/ppermute | solution.py:646
  64.9 0.0 collective-permute-start.3
  64.9 0.2 collective-permute-done.refs_1_
  65.1 1.4 %place_own.1.refs_1_ = f32[128,16384]{1,0:T(8,128)} custom-call(bf16[16,144,128]{2,1,0:T(8,128)(2,1)S(1)} %all_to_all.10.refs_0_, bf16[16,144,128]{2,1,0:T(8,128)(2,1)S(1)} %collective-permute-done.refs_1_), custom_call_target="tpu_custom_call" | custom-call | bytes 6291456 | tf_op jit(solution)/shard_map/place_own/pallas_call | solution.py:659
  66.5 6.9 %collective-permute-done.1.refs_0_.refs_2_ = bf16[16,144,128]{2,1,0:T(8,128)(2,1)S(1)} collective-permute-done((bf16[16,144,128]{2,1,0:T(8,128)(2,1)S(1)}, bf16[16,144,128]{2,1,0:T(8,128)(2,1)S(1)}, u32[]{:S(2)}, u32[]{:S(2)}) %collective-permute-start.1) | collective-permute-done | bytes 589856 | tf_op jit(solution)/shard_map/ppermute | solution.py:646
  73.4 0.0 collective-permute-start.4
  73.4 1.0 %place_x.1.refs_3_ = f32[128,16384]{1,0:T(8,128)} custom-call(bf16[16,144,128]{2,1,0:T(8,128)(2,1)S(1)} %collective-permute-done.1.refs_0_.refs_2_, f32[128,16384]{1,0:T(8,128)} %place_own.1.refs_1_), custom_call_target="tpu_custom_call", output_to_operand_aliasing={{}: (1, {})} | custom-call | bytes 6291456 | tf_op jit(solution)/shard_map/place_x/pallas_call | solution.py:659
  74.5 0.0 collective-permute-done.2.refs_0_.refs_3_
  74.5 0.4 collective-permute-done.3.refs_1_.refs_4_
  74.9 0.2 collective-permute-start.6
  75.1 0.3 collective-permute-start.5
  75.4 0.1 collective-permute-done.4.refs_2_.refs_5_
  75.4 1.8 %place_y_z_far_x.1.refs_8_ = f32[128,16384]{1,0:T(8,128)} custom-call(bf16[16,144,128]{2,1,0:T(8,128)(2,1)S(1)} %collective-permute-done.2.refs_0_.refs_3_, bf16[16,144,128]{2,1,0:T(8,128)(2,1)S(1)} %collective-permute-done.3.refs_1_.refs_4_, bf16[16,144,128]{2,1,0:T(8,128)(2,1)S(1)} %collective-permute-done.4.refs_2_.refs_5_, ...), custom_call_target="tpu_custom_call", output_to_operand_aliasing={{}: (3, {})} | custom-call | bytes 6291456 | tf_op jit(solution)/shard_map/place_y_z_far_x/pallas_call | solution.py:659
  77.2 0.0 collective-permute-done.6.refs_7_
  77.2 0.5 collective-permute-done.5.refs_6_
  77.7 1.6 %place_last.1 = (f32[128,16384]{1,0:T(8,128)}, f32[128,128]{1,0:T(8,128)}, f32[128,384]{1,0:T(8,128)}, f32[128,384]{1,0:T(8,128)}, f32[16,128]{1,0:T(8,128)}, /*...) custom-call(bf16[16,144,128]{2,1,0:T(8,128)(2,1)S(1)} %all_to_all.10.refs_0_, ...), custom_call_target="tpu_custom_call", output_to_operand_aliasing={{0}: (8, {})} | custom-call | bytes 6291456 | tf_op jit(solution)/shard_map/place_last/pallas_call | solution.py:691
Async XLA Ops:
  14.9 26.1 %all-to-all-start = ((bf16[32,144,128]{2,1,0:T(8,128)(2,1)}), bf16[32,144,128]{2,1,0:T(8,128)(2,1)S(1)}, u32[]{:S(2)}, u32[]{:S(2)}) async-start(bf16[32,144,128]{2,1,0:T(8,128)(2,1)} %get-tuple-element.32), calls=%async_computation | async-start | bytes 2359296 | tf_op jit(solution)/shard_map/all_to_all | solution.py:626
  24.1 2.2 %copy-start = (bf16[128,16384]{1,0:T(8,128)(2,1)S(1)}, bf16[128,16384]{1,0:T(8,128)(2,1)}, u32[]{:S(2)}) copy-start(bf16[128,16384]{1,0:T(8,128)(2,1)} %w_ref.1) | copy-start | bytes 12582916
  26.3 0.9 %copy-start.1 = (bf16[1024,128]{1,0:T(8,128)(2,1)S(1)}, bf16[1024,128]{1,0:T(8,128)(2,1)}, u32[]{:S(2)}) copy-start(bf16[1024,128]{1,0:T(8,128)(2,1)} %get-tuple-element.35.pairs_ref) | copy-start | bytes 786436
  27.3 0.8 copy-start.2
  28.0 0.7 copy-start.3
  60.2 4.9 %collective-permute-start = (bf16[16,144,128]{2,1,0:T(8,128)(2,1)S(1)}, bf16[16,144,128]{2,1,0:T(8,128)(2,1)S(1)}, u32[]{:S(2)}, u32[]{:S(2)}) collective-permute-start(bf16[16,144,128]{2,1,0:T(8,128)(2,1)S(1)} %all_to_all.10.refs_0_), channel_id=1, source_target_pairs={{0,32},{32,0},{1,33},{33,1},{2,34},{34,2},{3,35},{35,3},{4,36},{36... | collective-permute-start | bytes 1769480 | tf_op jit(solution)/shard_map/ppermute | solution.py:645
  63.5 9.9 %collective-permute-start.1 = (bf16[16,144,128]{2,1,0:T(8,128)(2,1)S(1)}, bf16[16,144,128]{2,1,0:T(8,128)(2,1)S(1)}, u32[]{:S(2)}, u32[]{:S(2)}) collective-permute-start(bf16[16,144,128]{2,1,0:T(8,128)(2,1)S(1)} %all_to_all.10.refs_0_), channel_id=1, source_target_pairs={{1,0},{2,1},{3,2},{0,3},{5,4},{6,5},{7,6},{4,7},{9,8},{10,9},{11,1... | collective-permute-start | bytes 1769480 | tf_op jit(solution)/shard_map/ppermute | solution.py:646
  63.9 10.6 %collective-permute-start.2 = (bf16[16,144,128]{2,1,0:T(8,128)(2,1)S(1)}, bf16[16,144,128]{2,1,0:T(8,128)(2,1)S(1)}, u32[]{:S(2)}, u32[]{:S(2)}) collective-permute-start(bf16[16,144,128]{2,1,0:T(8,128)(2,1)S(1)} %all_to_all.10.refs_0_), channel_id=1, source_target_pairs={{4,0},{5,1},{6,2},{7,3},{8,4},{9,5},{10,6},{11,7},{12,8},{13,9},{1... | collective-permute-start | bytes 1769480 | tf_op jit(solution)/shard_map/ppermute | solution.py:646
  64.9 9.9 %collective-permute-start.3 = (bf16[16,144,128]{2,1,0:T(8,128)(2,1)S(1)}, bf16[16,144,128]{2,1,0:T(8,128)(2,1)S(1)}, u32[]{:S(2)}, u32[]{:S(2)}) collective-permute-start(bf16[16,144,128]{2,1,0:T(8,128)(2,1)S(1)} %all_to_all.10.refs_0_), channel_id=1, source_target_pairs={{16,0},{17,1},{18,2},{19,3},{20,4},{21,5},{22,6},{23,7},{24,8},{25... | collective-permute-start | bytes 1769480 | tf_op jit(solution)/shard_map/ppermute | solution.py:646
  73.4 2.0 %collective-permute-start.4 = (bf16[16,144,128]{2,1,0:T(8,128)(2,1)S(1)}, bf16[16,144,128]{2,1,0:T(8,128)(2,1)S(1)}, u32[]{:S(2)}, u32[]{:S(2)}) collective-permute-start(bf16[16,144,128]{2,1,0:T(8,128)(2,1)S(1)} %collective-permute-done.1.refs_0_.refs_2_), channel_id=1, source_target_pairs={{0,32},{32,0},{1,33},{33,1},{2,34},{34,2},{3,35},{35,3},{4,36},{36... | collective-permute-start | bytes 1769480 | tf_op jit(solution)/shard_map/ppermute | solution.py:673
  74.9 2.4 %collective-permute-start.6 = (bf16[16,144,128]{2,1,0:T(8,128)(2,1)S(1)}, bf16[16,144,128]{2,1,0:T(8,128)(2,1)S(1)}, u32[]{:S(2)}, u32[]{:S(2)}) collective-permute-start(bf16[16,144,128]{2,1,0:T(8,128)(2,1)S(1)} %collective-permute-done.3.refs_1_.refs_4_), channel_id=1, source_target_pairs={{0,32},{32,0},{1,33},{33,1},{2,34},{34,2},{3,35},{35,3},{4,36},{36... | collective-permute-start | bytes 1769480 | tf_op jit(solution)/shard_map/ppermute | solution.py:677
  75.1 2.6 %collective-permute-start.5 = (bf16[16,144,128]{2,1,0:T(8,128)(2,1)S(1)}, bf16[16,144,128]{2,1,0:T(8,128)(2,1)S(1)}, u32[]{:S(2)}, u32[]{:S(2)}) collective-permute-start(bf16[16,144,128]{2,1,0:T(8,128)(2,1)S(1)} %collective-permute-done.2.refs_0_.refs_3_), channel_id=1, source_target_pairs={{0,32},{32,0},{1,33},{33,1},{2,34},{34,2},{3,35},{35,3},{4,36},{36... | collective-permute-start | bytes 1769480 | tf_op jit(solution)/shard_map/ppermute | solution.py:677

commit v7 on v6

--- a/solution.py
+++ b/solution.py
@@ -218,8 +218,10 @@
                     ],
                     axis=1,
                 )
-                right = jnp.concatenate([u_rows(u_ref, first + q) for q in range(4)], axis=1)
-                return total + nt(left, right)
+                right = jnp.concatenate(
+                    [u_ref[pl.ds((first + q) * GAP, H), :] for q in range(4)], axis=1
+                )
+                return total + fine_right(nt, left, right)
 
             parts.append(lax.fori_loop(0, 8, body, jnp.zeros((ATOMS, H), F32), unroll=True))
         return (jnp.concatenate(parts, axis=0) + extra).astype(BF)

time: 80 us -> 82.3 us (1.029)
  Pallas kernels: 22.1 us -> 24.4 us
    pallas_call x1, Pallas kernels: 14.2 us -> 16.5 us  [run_layers(): pl.pallas_call(local_kernel, out_shape=(shape((GROUP, ROWS, H), BF), shap...]
  transfers between devices with their start and end apart: 8 -> 8, of which waited for: 6 -> 6; matrix products, arithmetic and copies ran while one was open for 0% -> 0% of each run, Pallas kernels for 8% -> 7%
where the time goes in v7:
time: 82.3 us; the launch traced here: 81.8 us
  Pallas kernels  24.4 us (30%)
  blocking collectives  18.9 us (23%)
  waiting for transfers between devices  18.4 us (22%)
  starting transfers between devices  14.5 us (18%)
  local copies, waits for them, and re-layouts  4.61 us (6%)
  between operations  0.89 us (1%)
    all_to_all x1, blocking collectives, local(): lax.all_to_all(piece, ('zh', 'core', 'dp'), split_axis=0, concat_axis=0,...  18.9 us
    pallas_call x1, Pallas kernels, run_layers(): pl.pallas_call(local_kernel, out_shape=(shape((GROUP, ROWS, H), BF), shap...  16.5 us
    all_to_all x1, waiting for transfers between devices, local(): got = lax.all_to_all(send, 'dp', split_axis=0, concat_axis=0)  10.4 us
    all_to_all x1, starting transfers between devices, local(): got = lax.all_to_all(send, 'dp', split_axis=0, concat_axis=0)  9.23 us
    ppermute x3, waiting for transfers between devices, local(): lax.ppermute(near, ('zh', 'core', 'dp'), neighbours(axis))  7.28 us
    unnamed x8, local copies, waits for them, and re-layouts  4.61 us
    pallas_call x3, Pallas kernels, place_blocks(): pl.pallas_call(functools.partial(place_some, kinds, first), out_shape=who...  4.19 us
    ppermute x1, starting transfers between devices, local(): far = lax.ppermute(near, 'core', swap)  3.34 us
  transfers between devices with their start and end apart: 8, of which 6 were waited for; matrix products, arithmetic and copies ran while one was open for 0% of the time, Pallas kernels for 7%

profile of v7, /device:TPU:1, one launch (start us, length us, event | category | flops | bytes accessed | tf_op | source)
XLA Modules:
  0.0 81.8 jit_solution(18185669132478688318)
XLA Ops:
  0.6 16.5 %layers.1 = (bf16[32,144,128]{2,1,0:T(8,128)(2,1)}, f32[32,128]{1,0:T(8,128)}, f32[32,128]{1,0:T(8,128)}, bf16[128,128]{1,0:T(8,128)(2,1)}, bf16[1024,128]{1,0:T(8,128)(2,1)}) custom-call(s32[8,128]{1,0:T(8,128)} %bitcast.12, s32[8,128]{1,0:T(8,128)} %bitcast.13, s32[8,128]{1,0:T(8,128)} %bitcast.14, bf16[16,1024]{1,0:T(8,128)(2,1)} %refs_3_.1, ...), custom_call_target="tpu_custom_call" | custom-call | tf_op jit(solution)/shard_map/layers/pallas_call | solution.py:538
  17.2 9.2 %all-to-all-start = ((bf16[32,144,128]{2,1,0:T(8,128)(2,1)}), bf16[32,144,128]{2,1,0:T(8,128)(2,1)S(1)}, u32[]{:S(2)}, u32[]{:S(2)}) async-start(bf16[32,144,128]{2,1,0:T(8,128)(2,1)} %get-tuple-element.32), calls=%async_computation | async-start | bytes 2359296 | tf_op jit(solution)/shard_map/all_to_all | solution.py:628
  26.4 0.0 copy-start
  26.5 2.2 %copy-done = bf16[128,16384]{1,0:T(8,128)(2,1)S(1)} copy-done((bf16[128,16384]{1,0:T(8,128)(2,1)S(1)}, bf16[128,16384]{1,0:T(8,128)(2,1)}, u32[]{:S(2)}) %copy-start) | copy-done | bytes 4194328
  28.6 0.0 copy-start.1
  28.6 0.9 %copy-done.1 = bf16[1024,128]{1,0:T(8,128)(2,1)S(1)} copy-done((bf16[1024,128]{1,0:T(8,128)(2,1)S(1)}, bf16[1024,128]{1,0:T(8,128)(2,1)}, u32[]{:S(2)}) %copy-start.1) | copy-done | bytes 262168
  29.6 0.0 copy-start.2
  29.6 0.8 copy-done.2
  30.3 0.0 copy-start.3
  30.3 0.7 copy-done.3
  31.1 1.8 %states_back.1 = f32[32,128]{1,0:T(8,128)} custom-call(f32[32,128]{1,0:T(8,128)S(1)} %copy-done.3, bf16[128,128]{1,0:T(8,128)(2,1)S(1)} %copy-done.2, bf16[1024,128]{1,0:T(8,128)(2,1)S(1)} %copy-done.1, bf16[128,16384]{1,0:T(8,128)(2,1)S(1)} %copy-done), custom_call_target="tpu_custom_call" | custom-call | flops 134217728 | bytes 4194304 | tf_op jit(solution)/shard_map/states_back/pallas_call | solution.py:616
  32.9 10.4 %all-to-all-done.got_ref = bf16[32,144,128]{2,1,0:T(8,128)(2,1)S(1)} async-done(((bf16[32,144,128]{2,1,0:T(8,128)(2,1)}), bf16[32,144,128]{2,1,0:T(8,128)(2,1)S(1)}, u32[]{:S(2)}, u32[]{:S(2)}) %all-to-all-start) | async-done | bytes 1179680 | tf_op jit(solution)/shard_map/all_to_all | solution.py:628
  43.3 0.2 sum_parts.1
  43.5 18.9 %all_to_all.10.refs_0_ = bf16[16,144,128]{2,1,0:T(8,128)(2,1)S(1)} all-to-all(bf16[16,144,128]{2,1,0:T(8,128)(2,1)S(1)} %sum_parts.1), channel_id=1, replica_groups={{0,2,8,10,21,23,29,31,64,66,72,74,85,87,93,95},{4,6,12,14,17,19,25,27,6..., dimensions={0} | all-to-all | bytes 1179648 | tf_op jit(solution)/shard_map/all_to_all | solution.py:643
  62.4 3.3 %collective-permute-start = (bf16[16,144,128]{2,1,0:T(8,128)(2,1)S(1)}, bf16[16,144,128]{2,1,0:T(8,128)(2,1)S(1)}, u32[]{:S(2)}, u32[]{:S(2)}) collective-permute-start(bf16[16,144,128]{2,1,0:T(8,128)(2,1)S(1)} %all_to_all.10.refs_0_), channel_id=1, source_target_pairs={{0,32},{32,0},{1,33},{33,1},{2,34},{34,2},{3,35},{35,3},{4,36},{36... | collective-permute-start | bytes 1769480 | tf_op jit(solution)/shard_map/ppermute | solution.py:647
  65.8 0.4 collective-permute-start.1
  66.2 1.0 %collective-permute-start.2 = (bf16[16,144,128]{2,1,0:T(8,128)(2,1)S(1)}, bf16[16,144,128]{2,1,0:T(8,128)(2,1)S(1)}, u32[]{:S(2)}, u32[]{:S(2)}) collective-permute-start(bf16[16,144,128]{2,1,0:T(8,128)(2,1)S(1)} %all_to_all.10.refs_0_), channel_id=1, source_target_pairs={{4,0},{5,1},{6,2},{7,3},{8,4},{9,5},{10,6},{11,7},{12,8},{13,9},{1... | collective-permute-start | bytes 1769480 | tf_op jit(solution)/shard_map/ppermute | solution.py:648
  67.2 0.0 collective-permute-start.3
  67.2 0.2 collective-permute-done.refs_1_
  67.4 1.4 %place_own.1.refs_1_ = f32[128,16384]{1,0:T(8,128)} custom-call(bf16[16,144,128]{2,1,0:T(8,128)(2,1)S(1)} %all_to_all.10.refs_0_, bf16[16,144,128]{2,1,0:T(8,128)(2,1)S(1)} %collective-permute-done.refs_1_), custom_call_target="tpu_custom_call" | custom-call | bytes 6291456 | tf_op jit(solution)/shard_map/place_own/pallas_call | solution.py:661
  68.8 6.9 %collective-permute-done.1.refs_0_.refs_2_ = bf16[16,144,128]{2,1,0:T(8,128)(2,1)S(1)} collective-permute-done((bf16[16,144,128]{2,1,0:T(8,128)(2,1)S(1)}, bf16[16,144,128]{2,1,0:T(8,128)(2,1)S(1)}, u32[]{:S(2)}, u32[]{:S(2)}) %collective-permute-start.1) | collective-permute-done | bytes 589856 | tf_op jit(solution)/shard_map/ppermute | solution.py:648
  75.7 0.0 collective-permute-start.4
  75.7 1.0 %place_x.1.refs_3_ = f32[128,16384]{1,0:T(8,128)} custom-call(bf16[16,144,128]{2,1,0:T(8,128)(2,1)S(1)} %collective-permute-done.1.refs_0_.refs_2_, f32[128,16384]{1,0:T(8,128)} %place_own.1.refs_1_), custom_call_target="tpu_custom_call", output_to_operand_aliasing={{}: (1, {})} | custom-call | bytes 6291456 | tf_op jit(solution)/shard_map/place_x/pallas_call | solution.py:661
  76.8 0.0 collective-permute-done.2.refs_0_.refs_3_
  76.8 0.4 collective-permute-done.3.refs_1_.refs_4_
  77.2 0.2 collective-permute-start.6
  77.4 0.3 collective-permute-start.5
  77.7 0.1 collective-permute-done.4.refs_2_.refs_5_
  77.7 1.8 %place_y_z_far_x.1.refs_8_ = f32[128,16384]{1,0:T(8,128)} custom-call(bf16[16,144,128]{2,1,0:T(8,128)(2,1)S(1)} %collective-permute-done.2.refs_0_.refs_3_, bf16[16,144,128]{2,1,0:T(8,128)(2,1)S(1)} %collective-permute-done.3.refs_1_.refs_4_, bf16[16,144,128]{2,1,0:T(8,128)(2,1)S(1)} %collective-permute-done.4.refs_2_.refs_5_, ...), custom_call_target="tpu_custom_call", output_to_operand_aliasing={{}: (3, {})} | custom-call | bytes 6291456 | tf_op jit(solution)/shard_map/place_y_z_far_x/pallas_call | solution.py:661
  79.5 0.0 collective-permute-done.6.refs_7_
  79.5 0.5 collective-permute-done.5.refs_6_
  80.0 1.6 %place_last.1 = (f32[128,16384]{1,0:T(8,128)}, f32[128,128]{1,0:T(8,128)}, f32[128,384]{1,0:T(8,128)}, f32[128,384]{1,0:T(8,128)}, f32[16,128]{1,0:T(8,128)}, /*...) custom-call(bf16[16,144,128]{2,1,0:T(8,128)(2,1)S(1)} %all_to_all.10.refs_0_, ...), custom_call_target="tpu_custom_call", output_to_operand_aliasing={{0}: (8, {})} | custom-call | bytes 6291456 | tf_op jit(solution)/shard_map/place_last/pallas_call | solution.py:693
Async XLA Ops:
  17.2 26.1 %all-to-all-start = ((bf16[32,144,128]{2,1,0:T(8,128)(2,1)}), bf16[32,144,128]{2,1,0:T(8,128)(2,1)S(1)}, u32[]{:S(2)}, u32[]{:S(2)}) async-start(bf16[32,144,128]{2,1,0:T(8,128)(2,1)} %get-tuple-element.32), calls=%async_computation | async-start | bytes 2359296 | tf_op jit(solution)/shard_map/all_to_all | solution.py:628
  26.4 2.2 %copy-start = (bf16[128,16384]{1,0:T(8,128)(2,1)S(1)}, bf16[128,16384]{1,0:T(8,128)(2,1)}, u32[]{:S(2)}) copy-start(bf16[128,16384]{1,0:T(8,128)(2,1)} %w_ref.1) | copy-start | bytes 12582916
  28.6 0.9 %copy-start.1 = (bf16[1024,128]{1,0:T(8,128)(2,1)S(1)}, bf16[1024,128]{1,0:T(8,128)(2,1)}, u32[]{:S(2)}) copy-start(bf16[1024,128]{1,0:T(8,128)(2,1)} %get-tuple-element.35.pairs_ref) | copy-start | bytes 786436
  29.6 0.8 copy-start.2
  30.3 0.7 copy-start.3
  62.4 5.0 %collective-permute-start = (bf16[16,144,128]{2,1,0:T(8,128)(2,1)S(1)}, bf16[16,144,128]{2,1,0:T(8,128)(2,1)S(1)}, u32[]{:S(2)}, u32[]{:S(2)}) collective-permute-start(bf16[16,144,128]{2,1,0:T(8,128)(2,1)S(1)} %all_to_all.10.refs_0_), channel_id=1, source_target_pairs={{0,32},{32,0},{1,33},{33,1},{2,34},{34,2},{3,35},{35,3},{4,36},{36... | collective-permute-start | bytes 1769480 | tf_op jit(solution)/shard_map/ppermute | solution.py:647
  65.8 9.9 %collective-permute-start.1 = (bf16[16,144,128]{2,1,0:T(8,128)(2,1)S(1)}, bf16[16,144,128]{2,1,0:T(8,128)(2,1)S(1)}, u32[]{:S(2)}, u32[]{:S(2)}) collective-permute-start(bf16[16,144,128]{2,1,0:T(8,128)(2,1)S(1)} %all_to_all.10.refs_0_), channel_id=1, source_target_pairs={{1,0},{2,1},{3,2},{0,3},{5,4},{6,5},{7,6},{4,7},{9,8},{10,9},{11,1... | collective-permute-start | bytes 1769480 | tf_op jit(solution)/shard_map/ppermute | solution.py:648
  66.2 10.6 %collective-permute-start.2 = (bf16[16,144,128]{2,1,0:T(8,128)(2,1)S(1)}, bf16[16,144,128]{2,1,0:T(8,128)(2,1)S(1)}, u32[]{:S(2)}, u32[]{:S(2)}) collective-permute-start(bf16[16,144,128]{2,1,0:T(8,128)(2,1)S(1)} %all_to_all.10.refs_0_), channel_id=1, source_target_pairs={{4,0},{5,1},{6,2},{7,3},{8,4},{9,5},{10,6},{11,7},{12,8},{13,9},{1... | collective-permute-start | bytes 1769480 | tf_op jit(solution)/shard_map/ppermute | solution.py:648
  67.2 9.9 %collective-permute-start.3 = (bf16[16,144,128]{2,1,0:T(8,128)(2,1)S(1)}, bf16[16,144,128]{2,1,0:T(8,128)(2,1)S(1)}, u32[]{:S(2)}, u32[]{:S(2)}) collective-permute-start(bf16[16,144,128]{2,1,0:T(8,128)(2,1)S(1)} %all_to_all.10.refs_0_), channel_id=1, source_target_pairs={{16,0},{17,1},{18,2},{19,3},{20,4},{21,5},{22,6},{23,7},{24,8},{25... | collective-permute-start | bytes 1769480 | tf_op jit(solution)/shard_map/ppermute | solution.py:648
  75.7 2.0 %collective-permute-start.4 = (bf16[16,144,128]{2,1,0:T(8,128)(2,1)S(1)}, bf16[16,144,128]{2,1,0:T(8,128)(2,1)S(1)}, u32[]{:S(2)}, u32[]{:S(2)}) collective-permute-start(bf16[16,144,128]{2,1,0:T(8,128)(2,1)S(1)} %collective-permute-done.1.refs_0_.refs_2_), channel_id=1, source_target_pairs={{0,32},{32,0},{1,33},{33,1},{2,34},{34,2},{3,35},{35,3},{4,36},{36... | collective-permute-start | bytes 1769480 | tf_op jit(solution)/shard_map/ppermute | solution.py:675
  77.2 2.4 %collective-permute-start.6 = (bf16[16,144,128]{2,1,0:T(8,128)(2,1)S(1)}, bf16[16,144,128]{2,1,0:T(8,128)(2,1)S(1)}, u32[]{:S(2)}, u32[]{:S(2)}) collective-permute-start(bf16[16,144,128]{2,1,0:T(8,128)(2,1)S(1)} %collective-permute-done.3.refs_1_.refs_4_), channel_id=1, source_target_pairs={{0,32},{32,0},{1,33},{33,1},{2,34},{34,2},{3,35},{35,3},{4,36},{36... | collective-permute-start | bytes 1769480 | tf_op jit(solution)/shard_map/ppermute | solution.py:679
  77.4 2.6 %collective-permute-start.5 = (bf16[16,144,128]{2,1,0:T(8,128)(2,1)S(1)}, bf16[16,144,128]{2,1,0:T(8,128)(2,1)S(1)}, u32[]{:S(2)}, u32[]{:S(2)}) collective-permute-start(bf16[16,144,128]{2,1,0:T(8,128)(2,1)S(1)} %collective-permute-done.2.refs_0_.refs_3_), channel_id=1, source_target_pairs={{0,32},{32,0},{1,33},{33,1},{2,34},{34,2},{3,35},{35,3},{4,36},{36... | collective-permute-start | bytes 1769480 | tf_op jit(solution)/shard_map/ppermute | solution.py:679

commit v8 on v5

--- a/solution.py
+++ b/solution.py
@@ -21,7 +21,6 @@
 GROUP = 32
 CLASS = 8
 AXES = 3
-W_PARTS = 1
 BF = jnp.bfloat16
 F32 = jnp.float32
 
@@ -76,12 +75,12 @@
 
 
 def gate_forward(message, states, w_input, w_hidden, b_input, b_hidden):
-    from_msg = nn(message, w_input) + b_input
-    from_state = nn(states, w_hidden) + b_hidden
-    reset = sigmoid(from_msg[:, :H] + from_state[:, :H])
-    update = sigmoid(from_msg[:, H : 2 * H] + from_state[:, H : 2 * H])
-    state_cand = from_state[:, 2 * H :]
-    candidate = jnp.tanh(from_msg[:, 2 * H :] + reset * state_cand)
+    both = jnp.concatenate([message, states], axis=1)
+    w_both = jnp.concatenate([w_input[:, : 2 * H], w_hidden[:, : 2 * H]], axis=0)
+    gates = sigmoid(nn(both, w_both) + (b_input + b_hidden)[:, : 2 * H])
+    reset, update = gates[:, :H], gates[:, H:]
+    state_cand = nn(states, w_hidden[:, 2 * H :]) + b_hidden[:, 2 * H :]
+    candidate = jnp.tanh(nn(message, w_input[:, 2 * H :]) + b_input[:, 2 * H :] + reset * state_cand)
     renewed = (1.0 - update) * candidate + update * states.astype(F32)
     return reset, update, candidate, state_cand, renewed
 
@@ -106,7 +105,7 @@
     ins, refs = refs[:14], refs[14:]
     (send_ref, final_ref, base_ref, grad_t_ref, pairs_out_ref), refs = refs[:5], refs[5:]
     held, refs = refs[:14], refs[14:]
-    u_one, u_two, d_all, d_own, pair_h, rows_scr, small_scr, q_scr, sems, w_sems = refs
+    u_one, u_two, d_all, d_own, pair_h, rows_scr, small_scr, q_scr, sems, w_sem = refs
     (
         source_ref,
         target_ref,
@@ -124,26 +123,22 @@
         w_ref,
     ) = held
     sect = section()
-    chunk = H * H // W_PARTS
     copies = [
         pltpu.make_async_copy(ins[at], held[at], sems.at[at]) for at in range(13)
     ]
 
-    def w_copy(at):
-        cols = pl.ds(at * chunk, chunk)
-        return pltpu.make_async_copy(ins[13].at[:, cols], w_ref.at[:, cols], w_sems.at[at])
-
-    for copy in copies:
+    for copy in copies[:7]:
         copy.start()
-    for at in range(W_PARTS):
-        w_copy(at).start()
-    for copy in copies:
+    w_copy = pltpu.make_async_copy(ins[13], w_ref, w_sem)
+    w_copy.start()
+    for copy in copies[7:]:
+        copy.start()
+    for copy in copies[:7]:
         copy.wait()
 
     states0 = states_ref[...]
     w_ein = w_ein_ref[...]
     b_ein = b_ein_ref[...]
-    b_mat = b_mat_ref[...]
     source = source_ref[...]
     target = target_ref[...]
     live = live_ref[...]
@@ -188,8 +183,7 @@
                 u_ref[pl.ds(at * 4 + q, NODES, stride=GAP), :] = out[:, q * H : (q + 1) * H]
 
         if wait:
-            for at in range(W_PARTS):
-                w_copy(at).wait()
+            w_copy.wait()
             for at in range(32):
                 step(at)
         else:
@@ -224,12 +218,15 @@
             parts.append(lax.fori_loop(0, 8, body, jnp.zeros((ATOMS, H), F32), unroll=True))
         return (jnp.concatenate(parts, axis=0) + extra).astype(BF)
 
+    spread(states0, u_one, True)
+    for copy in copies[7:]:
+        copy.wait()
+    b_mat = b_mat_ref[...]
     w_in = w_in_ref[...]
     w_hid = w_hid_ref[...]
     b_in = jnp.concatenate([b_in_ref[part : part + 1, :] for part in range(3)], axis=1)
     b_hid = jnp.concatenate([b_hid_ref[part : part + 1, :] for part in range(3)], axis=1)
 
-    spread(states0, u_one, True)
     msg_one = gather(states0, u_one)
     *parts_one, renewed = gate_forward(msg_one, states0, w_in, w_hid, b_in, b_hid)
     states1 = renewed.astype(BF)
@@ -551,7 +548,7 @@
             pltpu.VMEM((GROUP * SMALL, H), F32),
             pltpu.VMEM((PAIRS, H), BF),
             pltpu.SemaphoreType.DMA((13,)),
-            pltpu.SemaphoreType.DMA((W_PARTS,)),
+            pltpu.SemaphoreType.DMA,
         ],
         compiler_params=pltpu.CompilerParams(vmem_limit_bytes=BIG),
         name="layers",

time: 78.5 us -> 78.3 us (level)
  no operation moved by 1% of the time
where the time goes in v8:
time: 78.3 us; the launch traced here: 77.9 us
  Pallas kernels  21.9 us (28%)
  blocking collectives  18.6 us (24%)
  waiting for transfers between devices  17.3 us (22%)
  starting transfers between devices  14.5 us (19%)
  local copies, waits for them, and re-layouts  4.61 us (6%)
  between operations  0.89 us (1%)
    all_to_all x1, blocking collectives, local(): lax.all_to_all(piece, ('zh', 'core', 'dp'), split_axis=0, concat_axis=0,...  18.6 us
    pallas_call x1, Pallas kernels, run_layers(): pl.pallas_call(local_kernel, out_shape=(shape((GROUP, ROWS, H), BF), shap...  14 us
    all_to_all x1, waiting for transfers between devices, local(): got = lax.all_to_all(send, 'dp', split_axis=0, concat_axis=0)  9.73 us
    all_to_all x1, starting transfers between devices, local(): got = lax.all_to_all(send, 'dp', split_axis=0, concat_axis=0)  9.23 us
    ppermute x3, waiting for transfers between devices, local(): lax.ppermute(near, ('zh', 'core', 'dp'), neighbours(axis))  6.97 us
    unnamed x8, local copies, waits for them, and re-layouts  4.61 us
    pallas_call x3, Pallas kernels, place_blocks(): pl.pallas_call(functools.partial(place_some, kinds, first), out_shape=who...  4.2 us
    ppermute x1, starting transfers between devices, local(): far = lax.ppermute(near, 'core', swap)  3.36 us
  transfers between devices with their start and end apart: 8, of which 5 were waited for; matrix products, arithmetic and copies ran while one was open for 0% of the time, Pallas kernels for 8%

profile of v8, /device:TPU:1, one launch (start us, length us, event | category | flops | bytes accessed | tf_op | source)
XLA Modules:
  0.0 77.9 jit_solution(4397749163281798393)
XLA Ops:
  0.6 14.0 %layers.1 = (bf16[32,136,128]{2,1,0:T(8,128)(2,1)}, f32[32,128]{1,0:T(8,128)}, f32[32,128]{1,0:T(8,128)}, bf16[128,128]{1,0:T(8,128)(2,1)}, bf16[1024,128]{1,0:T(8,128)(2,1)}) custom-call(s32[8,128]{1,0:T(8,128)} %bitcast.12, s32[8,128]{1,0:T(8,128)} %bitcast.13, s32[8,128]{1,0:T(8,128)} %bitcast.14, bf16[16,1024]{1,0:T(8,128)(2,1)} %refs_3_.1, ...), custom_call_target="tpu_custom_call" | custom-call | tf_op jit(solution)/shard_map/layers/pallas_call | solution.py:529
  14.7 9.2 %all-to-all-start = ((bf16[32,136,128]{2,1,0:T(8,128)(2,1)}), bf16[32,136,128]{2,1,0:T(8,128)(2,1)S(1)}, u32[]{:S(2)}, u32[]{:S(2)}) async-start(bf16[32,136,128]{2,1,0:T(8,128)(2,1)} %get-tuple-element.32), calls=%async_computation | async-start | bytes 2228224 | tf_op jit(solution)/shard_map/all_to_all | solution.py:619
  23.9 0.0 copy-start
  24.0 2.2 %copy-done = bf16[128,16384]{1,0:T(8,128)(2,1)S(1)} copy-done((bf16[128,16384]{1,0:T(8,128)(2,1)S(1)}, bf16[128,16384]{1,0:T(8,128)(2,1)}, u32[]{:S(2)}) %copy-start) | copy-done | bytes 4194328
  26.1 0.0 copy-start.1
  26.1 0.9 %copy-done.1 = bf16[1024,128]{1,0:T(8,128)(2,1)S(1)} copy-done((bf16[1024,128]{1,0:T(8,128)(2,1)S(1)}, bf16[1024,128]{1,0:T(8,128)(2,1)}, u32[]{:S(2)}) %copy-start.1) | copy-done | bytes 262168
  27.1 0.0 copy-start.2
  27.1 0.8 copy-done.2
  27.8 0.0 copy-start.3
  27.8 0.7 copy-done.3
  28.6 1.8 %states_back.1 = f32[32,128]{1,0:T(8,128)} custom-call(f32[32,128]{1,0:T(8,128)S(1)} %copy-done.3, bf16[128,128]{1,0:T(8,128)(2,1)S(1)} %copy-done.2, bf16[1024,128]{1,0:T(8,128)(2,1)S(1)} %copy-done.1, bf16[128,16384]{1,0:T(8,128)(2,1)S(1)} %copy-done), custom_call_target="tpu_custom_call" | custom-call | flops 134217728 | bytes 4194304 | tf_op jit(solution)/shard_map/states_back/pallas_call | solution.py:607
  30.4 9.7 %all-to-all-done.got_ref = bf16[32,136,128]{2,1,0:T(8,128)(2,1)S(1)} async-done(((bf16[32,136,128]{2,1,0:T(8,128)(2,1)}), bf16[32,136,128]{2,1,0:T(8,128)(2,1)S(1)}, u32[]{:S(2)}, u32[]{:S(2)}) %all-to-all-start) | async-done | bytes 1114144 | tf_op jit(solution)/shard_map/all_to_all | solution.py:619
  40.1 0.2 sum_parts.1
  40.4 18.6 %all_to_all.10.refs_0_ = bf16[16,136,128]{2,1,0:T(8,128)(2,1)S(1)} all-to-all(bf16[16,136,128]{2,1,0:T(8,128)(2,1)S(1)} %sum_parts.1), channel_id=1, replica_groups={{0,2,8,10,21,23,29,31,64,66,72,74,85,87,93,95},{4,6,12,14,17,19,25,27,6..., dimensions={0} | all-to-all | bytes 1114112 | tf_op jit(solution)/shard_map/all_to_all | solution.py:634
  58.9 3.4 %collective-permute-start = (bf16[16,136,128]{2,1,0:T(8,128)(2,1)S(1)}, bf16[16,136,128]{2,1,0:T(8,128)(2,1)S(1)}, u32[]{:S(2)}, u32[]{:S(2)}) collective-permute-start(bf16[16,136,128]{2,1,0:T(8,128)(2,1)S(1)} %all_to_all.10.refs_0_), channel_id=1, source_target_pairs={{0,32},{32,0},{1,33},{33,1},{2,34},{34,2},{3,35},{35,3},{4,36},{36... | collective-permute-start | bytes 1671176 | tf_op jit(solution)/shard_map/ppermute | solution.py:638
  62.3 0.5 collective-permute-start.1
  62.8 0.9 %collective-permute-start.2 = (bf16[16,136,128]{2,1,0:T(8,128)(2,1)S(1)}, bf16[16,136,128]{2,1,0:T(8,128)(2,1)S(1)}, u32[]{:S(2)}, u32[]{:S(2)}) collective-permute-start(bf16[16,136,128]{2,1,0:T(8,128)(2,1)S(1)} %all_to_all.10.refs_0_), channel_id=1, source_target_pairs={{4,0},{5,1},{6,2},{7,3},{8,4},{9,5},{10,6},{11,7},{12,8},{13,9},{1... | collective-permute-start | bytes 1671176 | tf_op jit(solution)/shard_map/ppermute | solution.py:639
  63.7 0.0 collective-permute-start.3
  63.7 0.2 collective-permute-done.refs_1_
  63.9 1.4 %place_own.1.refs_1_ = f32[128,16384]{1,0:T(8,128)} custom-call(bf16[16,136,128]{2,1,0:T(8,128)(2,1)S(1)} %all_to_all.10.refs_0_, bf16[16,136,128]{2,1,0:T(8,128)(2,1)S(1)} %collective-permute-done.refs_1_), custom_call_target="tpu_custom_call" | custom-call | bytes 6291456 | tf_op jit(solution)/shard_map/place_own/pallas_call | solution.py:652
  65.3 6.6 %collective-permute-done.1.refs_0_.refs_2_ = bf16[16,136,128]{2,1,0:T(8,128)(2,1)S(1)} collective-permute-done((bf16[16,136,128]{2,1,0:T(8,128)(2,1)S(1)}, bf16[16,136,128]{2,1,0:T(8,128)(2,1)S(1)}, u32[]{:S(2)}, u32[]{:S(2)}) %collective-permute-start.1) | collective-permute-done | bytes 557088 | tf_op jit(solution)/shard_map/ppermute | solution.py:639
  71.9 0.0 collective-permute-start.4
  71.9 1.0 %place_x.1.refs_3_ = f32[128,16384]{1,0:T(8,128)} custom-call(bf16[16,136,128]{2,1,0:T(8,128)(2,1)S(1)} %collective-permute-done.1.refs_0_.refs_2_, f32[128,16384]{1,0:T(8,128)} %place_own.1.refs_1_), custom_call_target="tpu_custom_call", output_to_operand_aliasing={{}: (1, {})} | custom-call | bytes 6291456 | tf_op jit(solution)/shard_map/place_x/pallas_call | solution.py:652
  72.9 0.0 collective-permute-done.2.refs_0_.refs_3_
  72.9 0.4 collective-permute-done.3.refs_1_.refs_4_
  73.3 0.2 collective-permute-start.6
  73.5 0.3 collective-permute-start.5
  73.8 0.0 collective-permute-done.4.refs_2_.refs_5_
  73.8 1.8 %place_y_z_far_x.1.refs_8_ = f32[128,16384]{1,0:T(8,128)} custom-call(bf16[16,136,128]{2,1,0:T(8,128)(2,1)S(1)} %collective-permute-done.2.refs_0_.refs_3_, bf16[16,136,128]{2,1,0:T(8,128)(2,1)S(1)} %collective-permute-done.3.refs_1_.refs_4_, bf16[16,136,128]{2,1,0:T(8,128)(2,1)S(1)} %collective-permute-done.4.refs_2_.refs_5_, ...), custom_call_target="tpu_custom_call", output_to_operand_aliasing={{}: (3, {})} | custom-call | bytes 6291456 | tf_op jit(solution)/shard_map/place_y_z_far_x/pallas_call | solution.py:652
  75.6 0.0 collective-permute-done.6.refs_7_
  75.6 0.4 collective-permute-done.5.refs_6_
  76.1 1.6 %place_last.1 = (f32[128,16384]{1,0:T(8,128)}, f32[128,128]{1,0:T(8,128)}, f32[128,384]{1,0:T(8,128)}, f32[128,384]{1,0:T(8,128)}, f32[16,128]{1,0:T(8,128)}, /*...) custom-call(bf16[16,136,128]{2,1,0:T(8,128)(2,1)S(1)} %all_to_all.10.refs_0_, ...), custom_call_target="tpu_custom_call", output_to_operand_aliasing={{0}: (8, {})} | custom-call | bytes 6291456 | tf_op jit(solution)/shard_map/place_last/pallas_call | solution.py:684
Async XLA Ops:
  14.7 25.4 %all-to-all-start = ((bf16[32,136,128]{2,1,0:T(8,128)(2,1)}), bf16[32,136,128]{2,1,0:T(8,128)(2,1)S(1)}, u32[]{:S(2)}, u32[]{:S(2)}) async-start(bf16[32,136,128]{2,1,0:T(8,128)(2,1)} %get-tuple-element.32), calls=%async_computation | async-start | bytes 2228224 | tf_op jit(solution)/shard_map/all_to_all | solution.py:619
  23.9 2.2 %copy-start = (bf16[128,16384]{1,0:T(8,128)(2,1)S(1)}, bf16[128,16384]{1,0:T(8,128)(2,1)}, u32[]{:S(2)}) copy-start(bf16[128,16384]{1,0:T(8,128)(2,1)} %w_ref.1) | copy-start | bytes 12582916
  26.1 0.9 %copy-start.1 = (bf16[1024,128]{1,0:T(8,128)(2,1)S(1)}, bf16[1024,128]{1,0:T(8,128)(2,1)}, u32[]{:S(2)}) copy-start(bf16[1024,128]{1,0:T(8,128)(2,1)} %get-tuple-element.35.pairs_ref) | copy-start | bytes 786436
  27.1 0.8 copy-start.2
  27.8 0.7 copy-start.3
  58.9 4.9 %collective-permute-start = (bf16[16,136,128]{2,1,0:T(8,128)(2,1)S(1)}, bf16[16,136,128]{2,1,0:T(8,128)(2,1)S(1)}, u32[]{:S(2)}, u32[]{:S(2)}) collective-permute-start(bf16[16,136,128]{2,1,0:T(8,128)(2,1)S(1)} %all_to_all.10.refs_0_), channel_id=1, source_target_pairs={{0,32},{32,0},{1,33},{33,1},{2,34},{34,2},{3,35},{35,3},{4,36},{36... | collective-permute-start | bytes 1671176 | tf_op jit(solution)/shard_map/ppermute | solution.py:638
  62.3 9.6 %collective-permute-start.1 = (bf16[16,136,128]{2,1,0:T(8,128)(2,1)S(1)}, bf16[16,136,128]{2,1,0:T(8,128)(2,1)S(1)}, u32[]{:S(2)}, u32[]{:S(2)}) collective-permute-start(bf16[16,136,128]{2,1,0:T(8,128)(2,1)S(1)} %all_to_all.10.refs_0_), channel_id=1, source_target_pairs={{1,0},{2,1},{3,2},{0,3},{5,4},{6,5},{7,6},{4,7},{9,8},{10,9},{11,1... | collective-permute-start | bytes 1671176 | tf_op jit(solution)/shard_map/ppermute | solution.py:639
  62.8 10.1 %collective-permute-start.2 = (bf16[16,136,128]{2,1,0:T(8,128)(2,1)S(1)}, bf16[16,136,128]{2,1,0:T(8,128)(2,1)S(1)}, u32[]{:S(2)}, u32[]{:S(2)}) collective-permute-start(bf16[16,136,128]{2,1,0:T(8,128)(2,1)S(1)} %all_to_all.10.refs_0_), channel_id=1, source_target_pairs={{4,0},{5,1},{6,2},{7,3},{8,4},{9,5},{10,6},{11,7},{12,8},{13,9},{1... | collective-permute-start | bytes 1671176 | tf_op jit(solution)/shard_map/ppermute | solution.py:639
  63.7 9.6 %collective-permute-start.3 = (bf16[16,136,128]{2,1,0:T(8,128)(2,1)S(1)}, bf16[16,136,128]{2,1,0:T(8,128)(2,1)S(1)}, u32[]{:S(2)}, u32[]{:S(2)}) collective-permute-start(bf16[16,136,128]{2,1,0:T(8,128)(2,1)S(1)} %all_to_all.10.refs_0_), channel_id=1, source_target_pairs={{16,0},{17,1},{18,2},{19,3},{20,4},{21,5},{22,6},{23,7},{24,8},{25... | collective-permute-start | bytes 1671176 | tf_op jit(solution)/shard_map/ppermute | solution.py:639
  71.9 2.0 %collective-permute-start.4 = (bf16[16,136,128]{2,1,0:T(8,128)(2,1)S(1)}, bf16[16,136,128]{2,1,0:T(8,128)(2,1)S(1)}, u32[]{:S(2)}, u32[]{:S(2)}) collective-permute-start(bf16[16,136,128]{2,1,0:T(8,128)(2,1)S(1)} %collective-permute-done.1.refs_0_.refs_2_), channel_id=1, source_target_pairs={{0,32},{32,0},{1,33},{33,1},{2,34},{34,2},{3,35},{35,3},{4,36},{36... | collective-permute-start | bytes 1671176 | tf_op jit(solution)/shard_map/ppermute | solution.py:666
  73.3 2.3 %collective-permute-start.6 = (bf16[16,136,128]{2,1,0:T(8,128)(2,1)S(1)}, bf16[16,136,128]{2,1,0:T(8,128)(2,1)S(1)}, u32[]{:S(2)}, u32[]{:S(2)}) collective-permute-start(bf16[16,136,128]{2,1,0:T(8,128)(2,1)S(1)} %collective-permute-done.3.refs_1_.refs_4_), channel_id=1, source_target_pairs={{0,32},{32,0},{1,33},{33,1},{2,34},{34,2},{3,35},{35,3},{4,36},{36... | collective-permute-start | bytes 1671176 | tf_op jit(solution)/shard_map/ppermute | solution.py:670
  73.5 2.5 %collective-permute-start.5 = (bf16[16,136,128]{2,1,0:T(8,128)(2,1)S(1)}, bf16[16,136,128]{2,1,0:T(8,128)(2,1)S(1)}, u32[]{:S(2)}, u32[]{:S(2)}) collective-permute-start(bf16[16,136,128]{2,1,0:T(8,128)(2,1)S(1)} %collective-permute-done.2.refs_0_.refs_3_), channel_id=1, source_target_pairs={{0,32},{32,0},{1,33},{33,1},{2,34},{34,2},{3,35},{35,3},{4,36},{36... | collective-permute-start | bytes 1671176 | tf_op jit(solution)/shard_map/ppermute | solution.py:670
